TPU v7x, 32 devices: a whole 2x2x4 slice. The times are simulated.
32 devices in a mesh: dp: 4 (over x, core), fsdp: 8 (over z, y).
Axes of the slice: x: 2, y: 2, z: 4, core: 2. Of those that a mesh axis runs over, the one named last changes fastest.
Arguments:
- block_input: bfloat16 [16384, 1024], P(('dp', 'fsdp')), may hold values from -6 to 6
- in_weight: float32 [1024, 3072], P(('dp', 'fsdp')), may hold values from -0.1875 to 0.1875
- out_weight: float32 [1024, 1024], P(('dp', 'fsdp')), may hold values from -0.1875 to 0.1875
- gate_weight: float32 [1024, 4608], P(('dp', 'fsdp')), may hold values from -0.1875 to 0.1875
- up_weight: float32 [1024, 4608], P(('dp', 'fsdp')), may hold values from -0.1875 to 0.1875
- down_weight: float32 [4608, 1024], P(('dp', 'fsdp')), may hold values from -0.09375 to 0.09375
- norm_gain: float32 [1024], P(('dp', 'fsdp')), may hold values from 0.5 to 1.5
- ffn_gain: float32 [1024], P(('dp', 'fsdp')), may hold values from 0.5 to 1.5
- conv_weight: float32 [1024, 3], P(('dp', 'fsdp')), may hold values from -3 to 3
- seq_starts: int32 [4, 4], P('dp'), may hold values from 0 to 3072, as said below
- cotangent: bfloat16 [16384, 1024], P(('dp', 'fsdp')), may hold values from -6 to 6
Outputs:
- block_output: bfloat16 [16384, 1024], P(('dp', 'fsdp'))
- grad_input: bfloat16 [16384, 1024], P(('dp', 'fsdp'))
- grad_in_weight: float32 [1024, 3072], P(('dp', 'fsdp'))
- grad_out_weight: float32 [1024, 1024], P(('dp', 'fsdp'))
- grad_gate_weight: float32 [1024, 4608], P(('dp', 'fsdp'))
- grad_up_weight: float32 [1024, 4608], P(('dp', 'fsdp'))
- grad_down_weight: float32 [4608, 1024], P(('dp', 'fsdp'))
- grad_norm_gain: float32 [1024], P(('dp', 'fsdp'))
- grad_ffn_gain: float32 [1024], P(('dp', 'fsdp'))
- grad_conv_weight: float32 [1024, 3], P(('dp', 'fsdp'))
Inputs may be any that keep to these rules, and one draw needn't show every extreme that they name: `seq_starts`: row g holds the offsets within group g of the sequences packed there, in rising order, each sequence 1024, 2048 or 4096 tokens long, the first at 0; a row with fewer than 4 sequences repeats its last start. Some row holds four sequences.
All inputs are finite; a program needn't handle non-finite values.
Results may differ from a plain program's by a relative error of at most 0.012.
The roundings to bfloat16 on the way count: a program that leaves them out, or rounds other values in their place, can miss the bound.
Values may be sent and summed in bfloat16 or wider, within the bound.
No kernel may reach another device: no remote copies, remote signals or barrier semaphores. Data moves between devices by JAX's collectives and lax.ppermute only.
A program may use at most 320 MiB of HBM per device.

v0:
```python
import jax
import jax.numpy as jnp
from jax import lax
from jax.sharding import PartitionSpec as P

EPS = 1e-05


def passed_along(shard, axis, by):
    peers = lax.axis_size(axis)
    pairs = [(i, i + by) for i in range(peers) if 0 <= i + by < peers]
    return lax.ppermute(shard, axis, pairs)


def contract_rows(left, right):
    return lax.dot_general(
        left, right, (((0,), (0,)), ((), ())), preferred_element_type=jnp.float32
    )


def contract_cols(left, right):
    return lax.dot_general(
        left, right, (((1,), (1,)), ((), ())), preferred_element_type=jnp.float32
    )


def column_rows(left, right):
    return contract_rows(left, right)


def per_device(
    block_input,
    in_weight,
    out_weight,
    gate_weight,
    up_weight,
    down_weight,
    norm_gain,
    ffn_gain,
    conv_weight,
    seq_starts,
    cotangent,
):
    bfloat = jnp.bfloat16
    gathered = (
        lax.all_gather(in_weight.astype(bfloat), ("dp", "fsdp"), axis=0, tiled=True),
        lax.all_gather(out_weight.astype(bfloat), ("dp", "fsdp"), axis=0, tiled=True),
        lax.all_gather(gate_weight.astype(bfloat), ("dp", "fsdp"), axis=0, tiled=True),
        lax.all_gather(up_weight.astype(bfloat), ("dp", "fsdp"), axis=0, tiled=True),
        lax.all_gather(down_weight.astype(bfloat), ("dp", "fsdp"), axis=0, tiled=True),
        lax.all_gather(norm_gain.astype(bfloat), ("dp", "fsdp"), axis=0, tiled=True),
        lax.all_gather(ffn_gain.astype(bfloat), ("dp", "fsdp"), axis=0, tiled=True),
        lax.all_gather(conv_weight.astype(bfloat), ("dp", "fsdp"), axis=0, tiled=True),
    )
    mix_in, mix_out, ffn_gate, ffn_up, ffn_down, gain_mix, gain_ffn, conv_taps = gathered
    inputs = block_input.astype(jnp.float32)
    length = inputs.shape[0]
    width = inputs.shape[1]
    hidden_units = ffn_gate.shape[1]
    mix_gain = gain_mix.astype(jnp.float32)
    scale_mix = lax.rsqrt(jnp.mean(inputs * inputs, axis=1, keepdims=True) + EPS)
    normed_mix = (inputs * scale_mix * mix_gain[None, :]).astype(bfloat)
    projected = jnp.dot(normed_mix, mix_in, preferred_element_type=jnp.float32)
    b_branch = projected[:, :width]
    c_branch = projected[:, width : 2 * width]
    x_branch = projected[:, 2 * width :]
    product = b_branch * x_branch
    earlier = passed_along(product[length - 2 :], "fsdp", 1)
    padded = jnp.concatenate([earlier, product], 0)
    position = lax.axis_index("fsdp") * length + jnp.arange(length + 2, dtype=jnp.int32) - 2
    starts = seq_starts[0]
    begin = jnp.max(jnp.where(starts[None, :] <= position[:, None], starts[None, :], 0), axis=1)
    offset = position - begin
    own_offset = offset[2:]
    taps = conv_taps.astype(jnp.float32)
    mixed = jnp.zeros((length, width), jnp.float32)
    for lag in range(3):
        valid = (own_offset >= lag).astype(jnp.float32)[:, None]
        mixed = mixed + valid * taps[:, 2 - lag][None, :] * padded[2 - lag : 2 - lag + length]
    gated = (c_branch * mixed).astype(bfloat)
    hidden = inputs + jnp.dot(gated, mix_out, preferred_element_type=jnp.float32)
    ffn_scale = gain_ffn.astype(jnp.float32)
    scale_ffn = lax.rsqrt(jnp.mean(hidden * hidden, axis=1, keepdims=True) + EPS)
    normed_ffn = (hidden * scale_ffn * ffn_scale[None, :]).astype(bfloat)
    gate_pre = jnp.dot(normed_ffn, ffn_gate, preferred_element_type=jnp.float32)
    rise_pre = jnp.dot(normed_ffn, ffn_up, preferred_element_type=jnp.float32)
    swiglu = (jax.nn.silu(gate_pre) * rise_pre).astype(bfloat)
    result = hidden + jnp.dot(swiglu, ffn_down, preferred_element_type=jnp.float32)
    block_output = result.astype(bfloat)
    again = (
        lax.all_gather(in_weight.astype(bfloat), ("dp", "fsdp"), axis=0, tiled=True),
        lax.all_gather(out_weight.astype(bfloat), ("dp", "fsdp"), axis=0, tiled=True),
        lax.all_gather(gate_weight.astype(bfloat), ("dp", "fsdp"), axis=0, tiled=True),
        lax.all_gather(up_weight.astype(bfloat), ("dp", "fsdp"), axis=0, tiled=True),
        lax.all_gather(down_weight.astype(bfloat), ("dp", "fsdp"), axis=0, tiled=True),
        lax.all_gather(norm_gain.astype(bfloat), ("dp", "fsdp"), axis=0, tiled=True),
        lax.all_gather(ffn_gain.astype(bfloat), ("dp", "fsdp"), axis=0, tiled=True),
        lax.all_gather(conv_weight.astype(bfloat), ("dp", "fsdp"), axis=0, tiled=True),
    )
    mix_in, mix_out, ffn_gate, ffn_up, ffn_down, gain_mix, gain_ffn, conv_taps = again
    upstream = cotangent.astype(jnp.float32)
    part_down = lax.psum_scatter(
        column_rows(swiglu, cotangent), ("dp", "fsdp"), scatter_dimension=0, tiled=True
    )
    grad_swiglu = contract_cols(cotangent, ffn_down)
    sigma = jax.nn.sigmoid(gate_pre)
    grad_gate = (grad_swiglu * rise_pre * sigma * (1.0 + gate_pre * (1.0 - sigma))).astype(bfloat)
    grad_rise = (grad_swiglu * gate_pre * sigma).astype(bfloat)
    ffn_right = jnp.concatenate([grad_gate, grad_rise], 1)
    grad_normed = contract_cols(grad_gate, ffn_gate) + contract_cols(grad_rise, ffn_up)
    grad_gain_ffn = jnp.sum(grad_normed * hidden * scale_ffn, axis=0)
    weighted = grad_normed * ffn_scale[None, :]
    grad_hidden = (
        upstream
        + scale_ffn * weighted
        - hidden * scale_ffn**3 * jnp.mean(weighted * hidden, axis=1, keepdims=True)
    )
    hidden_low = grad_hidden.astype(bfloat)
    grad_gated = contract_cols(hidden_low, mix_out)
    grad_c = grad_gated * mixed
    grad_mixed = grad_gated * c_branch
    later = passed_along(grad_mixed[:2], "fsdp", -1)
    trailing = jnp.concatenate([grad_mixed, later], 0)
    next_position = lax.axis_index("fsdp") * length + jnp.arange(length + 2, dtype=jnp.int32)
    next_begin = jnp.max(
        jnp.where(starts[None, :] <= next_position[:, None], starts[None, :], 0), axis=1
    )
    next_offset = next_position - next_begin
    grad_product = jnp.zeros((length, width), jnp.float32)
    tap_grads = []
    for lag in range(3):
        ahead = (next_offset[lag : lag + length] >= lag).astype(jnp.float32)[:, None]
        grad_product = (
            grad_product + ahead * taps[:, 2 - lag][None, :] * trailing[lag : lag + length]
        )
    for column in range(3):
        lag = 2 - column
        valid = (own_offset >= lag).astype(jnp.float32)[:, None]
        tap_grads.append(jnp.sum(valid * grad_mixed * padded[column : column + length], axis=0))
    grad_taps = jnp.stack(tap_grads, axis=1)
    grad_projected = jnp.concatenate(
        [grad_product * x_branch, grad_c, grad_product * b_branch], 1
    ).astype(bfloat)
    grad_normed_mix = contract_cols(grad_projected, mix_in)
    mix_gain = gain_mix.astype(jnp.float32)
    grad_gain_mix = jnp.sum(grad_normed_mix * inputs * scale_mix, axis=0)
    weighted_mix = grad_normed_mix * mix_gain[None, :]
    grad_inputs = (
        grad_hidden
        + scale_mix * weighted_mix
        - inputs * scale_mix**3 * jnp.mean(weighted_mix * inputs, axis=1, keepdims=True)
    )
    wide_part = lax.psum_scatter(
        jnp.concatenate(
            [
                jnp.concatenate(
                    [column_rows(normed_mix, grad_projected), column_rows(gated, hidden_low)], 1
                ),
                column_rows(normed_ffn, ffn_right),
            ],
            1,
        ),
        ("dp", "fsdp"),
        scatter_dimension=0,
        tiled=True,
    )
    part_in = wide_part[:, : 3 * width]
    part_out = wide_part[:, 3 * width : 4 * width]
    part_gate = wide_part[:, 4 * width : 4 * width + hidden_units]
    part_rise = wide_part[:, 4 * width + hidden_units :]
    part_gain_mix, part_gain_ffn, part_taps = (
        lax.psum_scatter(grad_gain_mix, ("dp", "fsdp"), scatter_dimension=0, tiled=True),
        lax.psum_scatter(grad_gain_ffn, ("dp", "fsdp"), scatter_dimension=0, tiled=True),
        lax.psum_scatter(grad_taps, ("dp", "fsdp"), scatter_dimension=0, tiled=True),
    )
    return (
        block_output,
        grad_inputs.astype(bfloat),
        part_in,
        part_out,
        part_gate,
        part_rise,
        part_down,
        part_gain_mix,
        part_gain_ffn,
        part_taps,
    )


def solution(mesh):
    return jax.shard_map(
        per_device,
        mesh=mesh,
        in_specs=(
            P(("dp", "fsdp"), None),
            P(("dp", "fsdp"), None),
            P(("dp", "fsdp"), None),
            P(("dp", "fsdp"), None),
            P(("dp", "fsdp"), None),
            P(("dp", "fsdp"), None),
            P(("dp", "fsdp")),
            P(("dp", "fsdp")),
            P(("dp", "fsdp"), None),
            P("dp", None),
            P(("dp", "fsdp"), None),
        ),
        out_specs=(
            P(("dp", "fsdp"), None),
            P(("dp", "fsdp"), None),
            P(("dp", "fsdp"), None),
            P(("dp", "fsdp"), None),
            P(("dp", "fsdp"), None),
            P(("dp", "fsdp"), None),
            P(("dp", "fsdp"), None),
            P(("dp", "fsdp")),
            P(("dp", "fsdp")),
            P(("dp", "fsdp"), None),
        ),
        check_vma=False,
    )
```

profile of v0, /device:TPU:0, one launch (start us, length us, event | category | flops | bytes accessed | tf_op | source)
XLA Modules:
  0.0 1962.4 jit_solution(1930523280372209603)
XLA Ops:
  7.2 1.8 convert_element_type.99
  9.1 1.6 convert_element_type.106
  10.8 1.8 convert_element_type.111
  14.9 42.1 %all-reduce.5 = (bf16[1024]{0:T(1024)(128)(2,1)S(1)}, bf16[1024]{0:T(1024)(128)(2,1)S(1)}) all-reduce(bf16[1024]{0:T(1024)(128)(2,1)S(1)} %dynamic-update-slice, bf16[1024]{0:T(1024)(128)(2,1)S(1)} %dynamic-update-slice.1), channel_id=1, replica_groups=mesh['dp'=4,'fsdp'=8] {'dp','fsdp'}, use_global_device_ids=true, to_apply=%add | all-reduce | flops 2048 | bytes 8192
  57.0 66.5 %all-gather = bf16[32,32,3]{1,2,0:T(4,128)(2,1)S(1)} all-gather(bf16[1,32,3]{1,2,0:T(4,128)(2,1)S(1)} %convert_bitcast_fusion), channel_id=1, replica_groups=mesh['dp'=4,'fsdp'=8] {'dp','fsdp'}, dimensions={0}, use_global_device_ids=true | all-gather | bytes 6336 | tf_op jit(solution)/shard_map/all_gather | solution.py:53
  124.7 5.7 fusion.26
  131.0 1.6 collective-permute-start
  132.7 1.1 collective-permute-done
  133.8 2.4 multiply_convert_fusion.7
  136.2 6.6 all-gather.9.cloned.1.call-done
  142.8 3.3 multiply_reduce_fusion.5
  146.0 1.3 copy-done.5
  147.4 1.2 multiply_convert_fusion.6
  148.6 78.6 %all-gather.13.cloned.1.call-done = bf16[1024,4608]{1,0:T(8,128)(2,1)} async-done(((bf16[32,4608]{1,0:T(8,128)(2,1)}), bf16[1024,4608]{1,0:T(8,128)(2,1)}) %all-gather.13.cloned.1.call-update) | async-done | bytes 9437200 | tf_op jit(solution)/shard_map/all_gather | solution.py:49
  227.2 10.1 fusion.41
  237.3 73.9 %all-gather.11.cloned.1.call-done = bf16[1024,4608]{1,0:T(8,128)(2,1)} async-done(((bf16[32,4608]{1,0:T(8,128)(2,1)}), bf16[1024,4608]{1,0:T(8,128)(2,1)}) %all-gather.11.cloned.1.call-update) | async-done | bytes 9437200 | tf_op jit(solution)/shard_map/all_gather | solution.py:48
  311.2 10.1 fusion.40
  321.3 73.9 %all-gather.15.cloned.1.call-done = bf16[4608,1024]{1,0:T(8,128)(2,1)} async-done(((bf16[144,1024]{1,0:T(8,128)(2,1)}), bf16[4608,1024]{1,0:T(8,128)(2,1)}) %all-gather.15.cloned.1.call-update) | async-done | bytes 9437200 | tf_op jit(solution)/shard_map/all_gather | solution.py:50
  395.2 18.1 multiply_convert_fusion
  413.2 21.2 %fusion = f32[1024,9216]{1,0:T(8,128)} fusion(bf16[512,1024]{1,0:T(8,128)(2,1)} %multiply_convert_fusion.6, bf16[512,4608]{1,0:T(8,128)(2,1)} %get-tuple-element.28, bf16[512,4608]{1,0:T(8,128)(2,1)} %get-tuple-element.29), kind=kOutput, calls=%fused_computation.1 | convolution fusion | flops 9682550784 | bytes 48234496 | tf_op jit(solution)/shard_map/dot_general | solution.py:16
  434.5 9.2 fusion.42
  443.7 8.1 multiply_reduce_fusion.3
  453.1 3.2 fusion.21
  456.4 1.3 fusion.23
  458.0 3.3 multiply_reduce_fusion.2
  461.3 1.3 copy-done.4
  462.6 1.3 collective-permute-start.1
  463.9 1.0 copy.31
  465.0 3.1 collective-permute-done.1
  468.1 6.1 multiply_convert_fusion.5
  474.3 2.3 multiply_convert_fusion.3
  476.6 1.0 copy-done.13
  477.6 6.8 fusion.19
  484.4 36.2 %pad_maximum_fusion = f32[1024,13312]{1,0:T(8,128)} fusion(f32[1024,9216]{1,0:T(8,128)} %fusion, f32[1024,1024]{1,0:T(8,128)} %fusion.21, f32[1024,3072]{1,0:T(8,128)} %fusion.19), kind=kLoop, calls=%fused_computation | loop fusion | flops 27262976 | bytes 109051904 | tf_op jit(solution)/shard_map/concatenate | solution.py:154
  520.6 1.2 copy-done.18
  521.8 11.5 fusion.43
  533.3 1.6 copy-done.7
  534.9 10.0 add_convert_fusion
  544.8 8.0 fusion.17
  552.8 40.5 %all-reduce.4 = (f32[1024]{0:T(1024)S(1)}, f32[1024]{0:T(1024)S(1)}) all-reduce(f32[1024]{0:T(1024)S(1)} %get-tuple-element.15, f32[1024]{0:T(1024)S(1)} %get-tuple-element.13), channel_id=4, replica_groups=mesh['dp'=4,'fsdp'=8] {'dp','fsdp'}, use_global_device_ids=true, to_apply=%region_9.10.clone | all-reduce | flops 2048 | bytes 16384
  594.5 3.1 fusion.14
  597.6 2.3 reduce-scatter.10.cloned.1.call-done
  600.0 1.4 copy.32
  601.3 1139.0 %reduce-scatter.6.cloned.1.call-done = f32[32,13312]{1,0:T(8,128)} async-done(((f32[1024,13312]{1,0:T(8,128)}), f32[32,13312]{1,0:T(8,128)}) %reduce-scatter.6.cloned.1.call-update) | async-done | bytes 1703952 | tf_op jit(solution)/shard_map/reduce_scatter | solution.py:153
  1740.3 1.6 slice.98
  1741.8 1.8 slice.97
  1743.6 2.3 fusion.38
  1745.9 209.2 %reduce-scatter.8.cloned.1.call-done = f32[144,1024]{1,0:T(8,128)} async-done(((f32[4608,1024]{1,0:T(8,128)}), f32[144,1024]{1,0:T(8,128)}) %reduce-scatter.8.cloned.1.call-update) | async-done | bytes 589840 | tf_op jit(solution)/shard_map/reduce_scatter | solution.py:102
  (98 shorter events, 7.0 us)
Async XLA Ops:
  7.2 5.5 copy-start.19
  7.2 6.4 copy-start.20
  7.2 117.5 %all-gather.7.cloned.1.call-start = ((), (), s32[]{:S(2)}) async-start(), calls=%async_computation.3 | async-start | bytes 6488064 | tf_op jit(solution)/shard_map/all_gather | solution.py:46
  9.0 5.4 copy-start.25
  9.0 5.4 copy-start.26
  9.0 48.0 %copy-start.22 = (f32[32,3]{0,1:T(4,128)S(1)}, f32[32,3]{0,1:T(4,128)}, u32[]{:S(2)}) copy-start(f32[32,3]{0,1:T(4,128)} %param.19) | copy-start | bytes 1156
  9.0 114.6 %copy-start.23 = (s32[1,4]{1,0:T(1,128)S(1)}, s32[1,4]{1,0:T(1,128)}, u32[]{:S(2)}) copy-start(s32[1,4]{1,0:T(1,128)} %param.20) | copy-start | bytes 52
  9.0 114.7 %copy-start.3 = (bf16[512,1024]{1,0:T(8,128)(2,1)S(1)}, bf16[512,1024]{1,0:T(8,128)(2,1)}, u32[]{:S(2)}) copy-start(bf16[512,1024]{1,0:T(8,128)(2,1)} %param.11) | copy-start | bytes 3145732
  9.1 133.7 %all-gather.9.cloned.1.call-start = ((), (), s32[]{:S(2)}) async-start(), calls=%async_computation.4 | async-start | bytes 2162688 | tf_op jit(solution)/shard_map/all_gather | solution.py:47
  10.8 216.4 %all-gather.13.cloned.1.call-start = ((), (), s32[]{:S(2)}) async-start(), calls=%async_computation.6 | async-start | bytes 9732096 | tf_op jit(solution)/shard_map/all_gather | solution.py:49
  12.7 298.5 %all-gather.11.cloned.1.call-start = ((), (), s32[]{:S(2)}) async-start(), calls=%async_computation.5 | async-start | bytes 9732096 | tf_op jit(solution)/shard_map/all_gather | solution.py:48
  13.5 381.7 %all-gather.15.cloned.1.call-start = ((), (), s32[]{:S(2)}) async-start(), calls=%async_computation.7 | async-start | bytes 9732096 | tf_op jit(solution)/shard_map/all_gather | solution.py:50
  14.3 585.6 %reduce-scatter.10.cloned.1.call-start = ((), (), s32[]{:S(2)}) async-start(), calls=%async_computation.10 | async-start | bytes 540672
  130.4 3.3 copy-start
  131.0 2.8 collective-permute-start
  146.0 1.3 copy-start.5
  434.5 9.2 copy-start.6
  434.5 9.2 copy-start.10
  443.7 8.2 copy-start.17
  451.9 1.2 copy-start.9
  453.1 3.2 copy-start.1
  453.1 3.2 copy-start.24
  456.4 1.6 copy-start.8
  461.3 1.3 copy-start.4
  462.6 5.5 collective-permute-start.1
  465.0 1275.3 %reduce-scatter.6.cloned.1.call-start = ((), (), s32[]{:S(2)}) async-start(), calls=%async_computation.8 | async-start | bytes 56229888 | tf_op jit(solution)/shard_map/reduce_scatter | solution.py:153
  474.2 2.3 copy-start.11
  474.2 3.3 copy-start.15
  476.5 1.0 copy-start.13
  520.5 1.2 copy-start.18
  520.6 1434.6 %reduce-scatter.8.cloned.1.call-start = ((), (), s32[]{:S(2)}) async-start(), calls=%async_computation.9 | async-start | bytes 19464192 | tf_op jit(solution)/shard_map/reduce_scatter | solution.py:102
  533.3 1.6 copy-start.7
  534.8 10.0 copy-start.12
  534.8 10.0 copy-start.14
  534.8 10.0 copy-start.16
  544.8 49.7 %copy-start.2 = (f32[512,1024]{1,0:T(8,128)S(1)}, f32[512,1024]{1,0:T(8,128)}, u32[]{:S(2)}) copy-start(f32[512,1024]{1,0:T(8,128)} %copy-done.1) | copy-start | bytes 6291460
  544.8 49.7 %copy-start.21 = (f32[512]{0:T(512)S(1)}, f32[512]{0:T(512)}, u32[]{:S(2)}) copy-start(f32[512]{0:T(512)} %get-tuple-element.43) | copy-start | bytes 6148
Sparse Core Ops, SparseCore 0:
  11.5 72.5 all-gather.6
  87.6 55.0 all-gather.8
  146.2 80.8 all-gather.12
  230.5 80.6 all-gather.10
  314.5 80.6 all-gather.14
  465.1 134.8 reduce-scatter.9
  602.4 1137.8 reduce-scatter.5
  1748.4 206.7 reduce-scatter.7
where the time goes:
time: 1970 us; the launch traced here: 1960 us
  waiting for transfers between devices  1590 us (81%)
  blocking collectives  149 us (8%)
  matrix products  127 us (6%)
  other arithmetic  63.6 us (3%)
    reduce_scatter x1, waiting for transfers between devices, per_device(): lax.psum_scatter(jnp.concatenate([jnp.concatenate([column_rows(normed_mix...  1140 us
    reduce_scatter x1, waiting for transfers between devices, per_device(): lax.psum_scatter(column_rows(swiglu, cotangent), ('dp', 'fsdp'), scatter_...  209 us
    unnamed x2, blocking collectives  82.6 us
    all_gather x1, waiting for transfers between devices, per_device(): lax.all_gather(up_weight.astype(bfloat), ('dp', 'fsdp'), axis=0, tiled=True)  78.6 us
    all_gather x1, waiting for transfers between devices, per_device(): lax.all_gather(down_weight.astype(bfloat), ('dp', 'fsdp'), axis=0, tiled=...  73.9 us
    all_gather x1, waiting for transfers between devices, per_device(): lax.all_gather(gate_weight.astype(bfloat), ('dp', 'fsdp'), axis=0, tiled=...  73.9 us
    all_gather x1, blocking collectives, per_device(): lax.all_gather(conv_weight.astype(bfloat), ('dp', 'fsdp'), axis=0, tiled=...  66.5 us
    dot_general x5, matrix products, contract_cols(): lax.dot_general(left, right, (((1,), (1,)), ((), ())), preferred_element_...  44.7 us
  transfers between devices with their start and end apart: 10, of which 9 were waited for; matrix products, arithmetic and copies ran while one was open for 7% of the time, Pallas kernels for 0%

commit v1 on v0

v1 whole, which is shorter than its diff:
```python
import functools

import jax
import jax.numpy as jnp
from jax import lax
from jax.experimental import pallas as pl
from jax.experimental.pallas import tpu as pltpu
from jax.sharding import PartitionSpec as P

EPS = 1e-05
BF = jnp.bfloat16
F32 = jnp.float32


class Axis:
    def __init__(self, name, stride, size):
        self.name, self.stride, self.size = name, stride, size
        self.here = (lax.axis_index(name) // stride) % size

    def shift(self, value, by):
        total = lax.axis_size(self.name)
        pairs = []
        for i in range(total):
            at = (i // self.stride) % self.size
            pairs.append((i, i + ((at + by) % self.size - at) * self.stride))
        return lax.ppermute(value, self.name, pairs)


def passed_along(shard, axis, by):
    peers = lax.axis_size(axis)
    pairs = [(i, i + by) for i in range(peers) if 0 <= i + by < peers]
    return lax.ppermute(shard, axis, pairs)


def contract_rows(left, right):
    return lax.dot_general(
        left, right, (((0,), (0,)), ((), ())), preferred_element_type=F32
    )


def contract_cols(left, right):
    return lax.dot_general(
        left, right, (((1,), (1,)), ((), ())), preferred_element_type=F32
    )


def times(left, right):
    return jnp.dot(left, right, preferred_element_type=F32)


def spread(buffer, axis):
    return jnp.stack([buffer] + [axis.shift(buffer, by) for by in range(1, axis.size)])


def place_body(plan, nz, ny, nx, kept, here_ref, *refs):
    sources, (out_ref, sems) = refs[:-2], refs[-2:]
    x, y, z = here_ref[0], here_ref[1], here_ref[2]
    copies = []
    for source, (order, first_z, count_z) in zip(sources, plan, strict=True):
        for dx in range(nx):
            for dy in range(ny):
                for dz in range(count_z):
                    at_x = lax.rem(x + nx - dx, nx)
                    at_y = lax.rem(y + ny - dy, ny)
                    at_z = lax.rem(z + nz - (first_z + dz), nz)
                    lead = (dx, dy, dz) if order == "xy" else (dy, dx, dz)
                    if kept == 2:
                        target = out_ref.at[at_x, :, at_z, at_y]
                    else:
                        target = out_ref.at[at_x, 0, at_z, at_y]
                    copies.append((source.at[lead], target))
    started = []
    for i, (source, target) in enumerate(copies):
        copy = pltpu.make_async_copy(source, target, sems.at[i])
        copy.start()
        started.append(copy)
    for copy in started:
        copy.wait()


def place(here, sources, plan, sizes, kept, rows, columns):
    nx, ny, nz = sizes
    count = nx * ny * nz
    out = pl.pallas_call(
        functools.partial(place_body, plan, nz, ny, nx, kept),
        out_shape=jax.ShapeDtypeStruct((nx, kept, nz, ny, rows, columns), sources[0].dtype),
        in_specs=[pl.BlockSpec(memory_space=pltpu.SMEM)]
        + [pl.BlockSpec(memory_space=pl.ANY)] * len(sources),
        out_specs=pl.BlockSpec(memory_space=pl.ANY),
        scratch_shapes=[pltpu.SemaphoreType.DMA((count,))],
        cost_estimate=pl.CostEstimate(
            flops=0, bytes_accessed=4 * count * kept * rows * columns, transcendentals=0
        ),
    )(here, *sources)
    return out.reshape(nx * kept * nz * ny * rows, columns)


def gather(block, here, ax, ay, az):
    kept, rows, columns = block.shape
    lower = az.size // 2
    parts = [block] + [az.shift(block, by) for by in range(1, az.size)]
    first, second = jnp.stack(parts[:lower]), jnp.stack(parts[lower:])
    first = spread(spread(first, ax), ay)
    second = spread(spread(second, ay), ax)
    shape = (rows, columns) if kept == 1 else (kept, rows, columns)
    first = first.reshape(first.shape[:3] + shape)
    second = second.reshape(second.shape[:3] + shape)
    plan = (("yx", 0, lower), ("xy", lower, az.size - lower))
    return place(here, (first, second), plan, (ax.size, ay.size, az.size), kept, rows, columns)


def folded(value, axis, dim):
    own = lax.dynamic_index_in_dim(value, axis.here, dim, keepdims=False).astype(F32)
    for by in range(1, axis.size):
        there = lax.rem(axis.here + by, axis.size)
        own = own + axis.shift(
            lax.dynamic_index_in_dim(value, there, dim, keepdims=False), by
        ).astype(F32)
    return own


def scatter(whole, kept, ax, ay, az):
    columns = whole.shape[1]
    rows = whole.shape[0] // (ax.size * kept * az.size * ay.size)
    whole = whole.reshape(ax.size, kept, az.size, ay.size, rows, columns)
    lower = az.size // 2
    first, second = whole[:, :, :lower], whole[:, :, lower:]
    first = folded(folded(first, ay, 3).astype(BF), ax, 0).astype(BF)
    second = folded(folded(second, ax, 0).astype(BF), ay, 2).astype(BF)
    return folded(jnp.concatenate([first, second], 1), az, 1)


def core_columns(matrix, groups, which):
    rows, columns = matrix.shape
    blocks = matrix.reshape(rows, groups, 2, columns // (2 * groups))
    return lax.dynamic_index_in_dim(blocks, which, 2, keepdims=False).reshape(rows, columns // 2)


def both_columns(mine, other, groups, core):
    rows, half = mine.shape
    mine = mine.reshape(rows, groups, half // groups)
    other = other.reshape(rows, groups, half // groups)
    low = jnp.where(core == 0, mine, other)
    high = jnp.where(core == 0, other, mine)
    return jnp.stack([low, high], 2).reshape(rows, 2 * half)


def per_device(
    block_input,
    in_weight,
    out_weight,
    gate_weight,
    up_weight,
    down_weight,
    norm_gain,
    ffn_gain,
    conv_weight,
    seq_starts,
    cotangent,
):
    nd, nf = lax.axis_size("dp"), lax.axis_size("fsdp")
    ny = 1
    while (2 * ny) ** 2 <= nf:
        ny *= 2
    nx, nz = nd // 2, nf // ny
    ac, ax = Axis("dp", 1, 2), Axis("dp", 2, nx)
    ay, az = Axis("fsdp", 1, ny), Axis("fsdp", ny, nz)
    core = ac.here
    here = jnp.stack([ax.here, ay.here, az.here]).astype(jnp.int32)

    def swap(value):
        return ac.shift(value, 1)

    tokens, width = block_input.shape
    rows = in_weight.shape[0]
    hidden = gate_weight.shape[1] // 2
    feats = width // 2

    small = jnp.concatenate(
        [norm_gain[:, None], ffn_gain[:, None], conv_weight, jnp.zeros((rows, 123), F32)], 1
    ).astype(BF)
    in_low, gate_low, up_low = (w.astype(BF) for w in (in_weight, gate_weight, up_weight))

    def halves(which):
        return jnp.concatenate(
            [
                core_columns(in_low, 3 * nx, which),
                small,
                core_columns(gate_low, nx, which),
                core_columns(up_low, nx, which),
            ],
            1,
        )

    mine, theirs = halves(core), swap(halves(1 - core))
    pair = jnp.stack([jnp.where(core == 0, mine, theirs), jnp.where(core == 0, theirs, mine)])
    cut = 3 * feats + 128
    x_all = jnp.concatenate([block_input, swap(block_input)], 0)
    dy_all = jnp.concatenate([cotangent, swap(cotangent)], 0)
    starts = jnp.concatenate([seq_starts, swap(seq_starts)], 0)

    in_full = gather(pair[:, :, :cut], here, ax, ay, az)
    mix_out = gather(out_weight.astype(BF)[None], here, ax, ay, az)
    ffn_gate = gather(pair[:, :, cut : cut + hidden], here, ax, ay, az)
    ffn_up = gather(pair[:, :, cut + hidden :], here, ax, ay, az)
    ffn_down = gather(down_weight.astype(BF)[None], here, ax, ay, az)
    mix_in = in_full[:, : 3 * feats]
    tiny = in_full[:, 3 * feats : 3 * feats + 8].astype(F32)
    gain_mix, gain_ffn = tiny[:, 0], tiny[:, 1]
    taps = lax.dynamic_index_in_dim(
        tiny[:, 2:5].reshape(nx, 2, feats // nx, 3), core, 1, keepdims=False
    ).reshape(feats, 3)

    inputs = x_all.astype(F32)
    scale_mix = lax.rsqrt(jnp.mean(inputs * inputs, axis=1, keepdims=True) + EPS)
    normed_mix = (inputs * scale_mix * gain_mix[None, :]).astype(BF)
    projected = times(normed_mix, mix_in)
    b_branch = projected[:, :feats]
    c_branch = projected[:, feats : 2 * feats]
    x_branch = projected[:, 2 * feats :]
    product = (b_branch * x_branch).reshape(2, tokens, feats)
    earlier = passed_along(product[:, tokens - 2 :], "fsdp", 1)
    padded = jnp.concatenate([earlier, product], 1)
    position = lax.axis_index("fsdp") * tokens + jnp.arange(tokens + 2, dtype=jnp.int32)

    def offsets(at):
        reached = starts[:, None, :] <= at[None, :, None]
        return at[None, :] - jnp.max(jnp.where(reached, starts[:, None, :], 0), axis=2)

    own_offset = offsets(position[:tokens])
    mixed = jnp.zeros((2, tokens, feats), F32)
    for lag in range(3):
        valid = (own_offset >= lag).astype(F32)[:, :, None]
        mixed = mixed + valid * taps[:, 2 - lag] * padded[:, 2 - lag : 2 - lag + tokens]
    mixed = mixed.reshape(2 * tokens, feats)
    gated = (c_branch * mixed).astype(BF)
    mixer = times(gated, mix_out)
    own_inputs = inputs[:tokens]
    h = own_inputs + (mixer[:tokens] + swap(mixer[tokens:]))

    scale_ffn = lax.rsqrt(jnp.mean(h * h, axis=1, keepdims=True) + EPS)
    normed_own = (h * scale_ffn * gain_ffn[None, :]).astype(BF)
    normed_ffn = jnp.concatenate([normed_own, swap(normed_own)], 0)
    gate_pre = times(normed_ffn, ffn_gate)
    rise_pre = times(normed_ffn, ffn_up)
    sigma = jax.nn.sigmoid(gate_pre)
    swiglu = (gate_pre * sigma * rise_pre).astype(BF)
    grad_down = contract_rows(swiglu, dy_all).astype(BF)
    fed = times(swiglu, ffn_down)
    block_output = (h + (fed[:tokens] + swap(fed[tokens:]))).astype(BF)
    part_down = scatter(grad_down, 1, ax, ay, az)[0]

    grad_swiglu = contract_cols(dy_all, ffn_down)
    grad_gate = (grad_swiglu * rise_pre * sigma * (1.0 + gate_pre * (1.0 - sigma))).astype(BF)
    grad_rise = (grad_swiglu * gate_pre * sigma).astype(BF)
    part_gate = scatter(contract_rows(normed_ffn, grad_gate).astype(BF), 2, ax, ay, az)
    part_rise = scatter(contract_rows(normed_ffn, grad_rise).astype(BF), 2, ax, ay, az)
    grad_normed = contract_cols(grad_gate, ffn_gate) + contract_cols(grad_rise, ffn_up)
    grad_normed = grad_normed[:tokens] + swap(grad_normed[tokens:])
    grad_gain_ffn = jnp.sum(grad_normed * h * scale_ffn, axis=0)
    weighted = grad_normed * gain_ffn[None, :]
    grad_hidden = (
        cotangent.astype(F32)
        + scale_ffn * weighted
        - h * scale_ffn**3 * jnp.mean(weighted * h, axis=1, keepdims=True)
    )

    hidden_low = grad_hidden.astype(BF)
    hidden_low = jnp.concatenate([hidden_low, swap(hidden_low)], 0)
    part_out = scatter(contract_rows(gated, hidden_low).astype(BF), 1, ax, ay, az)[0]
    grad_gated = contract_cols(hidden_low, mix_out)
    grad_c = grad_gated * mixed
    grad_mixed = (grad_gated * c_branch).reshape(2, tokens, feats)
    later = passed_along(grad_mixed[:, :2], "fsdp", -1)
    trailing = jnp.concatenate([grad_mixed, later], 1)
    next_offset = offsets(position)
    grad_product = jnp.zeros((2, tokens, feats), F32)
    tap_grads = []
    for lag in range(3):
        ahead = (next_offset[:, lag : lag + tokens] >= lag).astype(F32)[:, :, None]
        grad_product = grad_product + ahead * taps[:, 2 - lag] * trailing[:, lag : lag + tokens]
    for column in range(3):
        valid = (own_offset >= 2 - column).astype(F32)[:, :, None]
        tap_grads.append(
            jnp.sum(valid * grad_mixed * padded[:, column : column + tokens], axis=(0, 1))
        )
    grad_product = grad_product.reshape(2 * tokens, feats)
    grad_projected = jnp.concatenate(
        [grad_product * x_branch, grad_c, grad_product * b_branch], 1
    ).astype(BF)
    part_in = scatter(contract_rows(normed_mix, grad_projected).astype(BF), 2, ax, ay, az)
    grad_normed_mix = contract_cols(grad_projected, mix_in)
    grad_normed_mix = grad_normed_mix[:tokens] + swap(grad_normed_mix[tokens:])
    own_scale = scale_mix[:tokens]
    grad_gain_mix = jnp.sum(grad_normed_mix * own_inputs * own_scale, axis=0)
    weighted_mix = grad_normed_mix * gain_mix[None, :]
    grad_inputs = (
        grad_hidden
        + own_scale * weighted_mix
        - own_inputs * own_scale**3 * jnp.mean(weighted_mix * own_inputs, axis=1, keepdims=True)
    )

    tap_rows = jnp.stack(tap_grads).reshape(3, nx, 1, feats // nx)
    on_core = (jnp.arange(2) == core).astype(F32)[None, None, :, None]
    tap_rows = (tap_rows * on_core).reshape(3, width)
    terms = jnp.concatenate([grad_gain_mix[None], grad_gain_ffn[None], tap_rows], 0)
    for axis in (ac, ax, ay, az):
        gone = terms
        for by in range(1, axis.size):
            terms = terms + axis.shift(gone, by)
    at = (lax.axis_index("dp") * nf + lax.axis_index("fsdp")) * rows
    own_terms = lax.dynamic_slice_in_dim(terms, at, rows, 1)

    wide = jnp.concatenate([part_in, part_gate, part_rise], 2)
    own_wide = lax.dynamic_index_in_dim(wide, core, 0, keepdims=False)
    got = swap(lax.dynamic_index_in_dim(wide, 1 - core, 0, keepdims=False))
    ends = (0, 3 * feats, 3 * feats + hidden, 3 * feats + 2 * hidden)
    full = [
        both_columns(own_wide[:, a:b], got[:, a:b], groups, core)
        for a, b, groups in zip(ends[:-1], ends[1:], (3 * nx, nx, nx), strict=True)
    ]
    return (
        block_output,
        grad_inputs.astype(BF),
        full[0],
        part_out,
        full[1],
        full[2],
        part_down,
        own_terms[0],
        own_terms[1],
        own_terms[2:].T,
    )


def solution(mesh):
    rows = P(("dp", "fsdp"), None)
    line = P(("dp", "fsdp"))
    return jax.shard_map(
        per_device,
        mesh=mesh,
        in_specs=(rows,) * 6 + (line, line, rows, P("dp", None), rows),
        out_specs=(rows,) * 7 + (line, line, rows),
        check_vma=False,
    )
```

time: 1970 us -> 1200 us (0.61)
  waiting for transfers between devices: 1590 us -> 248 us
  Pallas kernels: 0 us -> 574 us
  blocking collectives: 149 us -> 0 us
  starting transfers between devices: 3.19 us -> 141 us
  matrix products: 127 us -> 106 us
  other arithmetic: 63.6 us -> 83.5 us
    reduce_scatter x2 -> x0, waiting for transfers between devices: 1350 us -> none  [the longest x1 1140 us: per_device(): lax.psum_scatter(jnp.concatenate([jnp.concatenate([column_rows(normed_mix...]
    pallas_call x0 -> x5, Pallas kernels: none -> 574 us  [place(): pl.pallas_call(functools.partial(place_body, plan, nz, ny, nx, kept), out...]
    ppermute x0 -> x87, waiting for transfers between devices: none -> 247 us  [shift(): return lax.ppermute(value, self.name, pairs)]
    all_gather x5 -> x0, waiting for transfers between devices: 233 us -> none  [the longest x1 78.6 us: per_device(): lax.all_gather(up_weight.astype(bfloat), ('dp', 'fsdp'), axis=0, tiled=True)]
    ppermute x0 -> x87, starting transfers between devices: none -> 136 us  [shift(): return lax.ppermute(value, self.name, pairs)]
    unnamed x2 -> x0, blocking collectives: 82.6 us -> none
    all_gather x1 -> x0, blocking collectives: 66.5 us -> none  [per_device(): lax.all_gather(conv_weight.astype(bfloat), ('dp', 'fsdp'), axis=0, tiled=...]
    concatenate x1 -> x3, other arithmetic: 36.2 us -> 0.13 us  [the longest x1 0.1 us: per_device(): wide = jnp.concatenate([part_in, part_gate, part_rise], 2)]
  transfers between devices with their start and end apart: 10 -> 89, of which waited for: 9 -> 32; matrix products, arithmetic and copies ran while one was open for 7% -> 14% of each run, Pallas kernels for 0% -> 48%
where the time goes in v1:
time: 1200 us; the launch traced here: 1190 us
  Pallas kernels  574 us (48%)
  waiting for transfers between devices  248 us (21%)
  starting transfers between devices  141 us (12%)
  matrix products  106 us (9%)
  other arithmetic  83.5 us (7%)
  local copies, waits for them, and re-layouts  33.9 us (3%)
    pallas_call x5, Pallas kernels, place(): pl.pallas_call(functools.partial(place_body, plan, nz, ny, nx, kept), out...  574 us
    ppermute x87, waiting for transfers between devices, shift(): return lax.ppermute(value, self.name, pairs)  247 us
    ppermute x87, starting transfers between devices, shift(): return lax.ppermute(value, self.name, pairs)  136 us
    dot_general x5, matrix products, times(): return jnp.dot(left, right, preferred_element_type=F32)  42.7 us
    dot_general x5, matrix products, contract_cols(): lax.dot_general(left, right, (((1,), (1,)), ((), ())), preferred_element_...  34.2 us
    another operation x26, other arithmetic, spread(): jnp.stack([buffer] + [axis.shift(buffer, by) for by in range(1, axis.size)])  31.3 us
    dot_general x5, matrix products, contract_rows(): lax.dot_general(left, right, (((0,), (0,)), ((), ())), preferred_element_...  28.7 us
  transfers between devices with their start and end apart: 89, of which 32 were waited for; matrix products, arithmetic and copies ran while one was open for 14% of the time, Pallas kernels for 48%

profile of v1, /device:TPU:0, one launch (start us, length us, event | category | flops | bytes accessed | tf_op | source)
XLA Modules:
  0.0 1188.2 jit_solution(3952614941547133314)
XLA Ops:
  1.6 4.1 collective-permute-start.14
  12.0 4.0 dynamic-slice_reduce_fusion.2
  42.9 3.7 collective-permute-start.5
  46.6 3.3 collective-permute-start.6
  51.6 33.7 %shard_map.187 = bf16[2,1,4,2,32,1024]{5,4,3,2,1,0:T(8,128)(2,1)} custom-call(s32[3]{0:T(128)} %pad_add_fusion.1.here_ref, bf16[2,2,2,32,1024]{4,3,2,1,0:T(8,128)(2,1)} %maximum_bitcast_fusion.2.refs_0_, bf16[2,2,2,32,1024]{4,3,2,1,0:T(8,128)(2,1)} %maximum_bitcast_fusion.3.refs_1_), custom_call_target="tpu_custom_call" | custom-call | bytes 2097152 | tf_op jit(solution)/shard_map/pallas_call | solution.py:84
  88.5 8.5 collective-permute-done.2
  102.9 7.5 collective-permute-done.20
  110.5 9.8 collective-permute-done.30
  121.9 4.2 collective-permute-done.31
  129.0 7.9 collective-permute-done.27
  143.2 6.4 collective-permute-done.7
  167.9 6.9 collective-permute-done.32
  176.9 42.0 %collective-permute-done.8 = bf16[2,2,2,32,1664]{4,3,2,1,0:T(8,128)(2,1)S(1)} collective-permute-done((bf16[2,2,2,32,1664]{4,3,2,1,0:T(8,128)(2,1)S(1)}, bf16[2,2,2,32,1664]{4,3,2,1,0:T(8,128)(2,1)S(1)}, u32[]{:S(2)}, u32[]{:S(2)}) %collective-permute-start.8) | collective-permute-done | bytes 852000 | tf_op jit(solution)/shard_map/ppermute | solution.py:26
  222.2 105.2 %shard_map.186 = bf16[2,2,4,2,32,1664]{5,4,3,2,1,0:T(8,128)(2,1)} custom-call(s32[3]{0:T(128)} %pad_add_fusion.1.here_ref, bf16[2,2,2,2,32,1664]{5,4,3,2,1,0:T(8,128)(2,1)} %pad_maximum_fusion.9.refs_0_, bf16[2,2,2,2,32,1664]{5,4,3,2,1,0:T(8,128)(2,1)} %pad_maximum_fusion.10.refs_1_), custom_call_target="tpu_custom_call" | custom-call | bytes 6815744 | tf_op jit(solution)/shard_map/pallas_call | solution.py:84
  329.1 5.4 fusion.2
  360.8 144.9 %shard_map.190 = bf16[2,1,4,2,144,1024]{5,4,3,2,1,0:T(8,128)(2,1)} custom-call(s32[3]{0:T(128)} %pad_add_fusion.1.here_ref, bf16[2,2,2,144,1024]{4,3,2,1,0:T(8,128)(2,1)} %maximum_bitcast_fusion.refs_0_, bf16[2,2,2,144,1024]{4,3,2,1,0:T(8,128)(2,1)} %maximum_bitcast_fusion.1.refs_1_), custom_call_target="tpu_custom_call" | custom-call | bytes 9437184 | tf_op jit(solution)/shard_map/pallas_call | solution.py:84
  505.6 10.3 fusion.133
  525.5 145.0 %shard_map.188 = bf16[2,2,4,2,32,2304]{5,4,3,2,1,0:T(8,128)(2,1)} custom-call(s32[3]{0:T(128)} %pad_add_fusion.1.here_ref, bf16[2,2,2,2,32,2304]{5,4,3,2,1,0:T(8,128)(2,1)} %pad_maximum_fusion.1.refs_0_, bf16[2,2,2,2,32,2304]{5,4,3,2,1,0:T(8,128)(2,1)} %pad_maximum_fusion.2.refs_1_), custom_call_target="tpu_custom_call" | custom-call | bytes 9437184 | tf_op jit(solution)/shard_map/pallas_call | solution.py:84
  676.4 144.9 %shard_map.189 = bf16[2,2,4,2,32,2304]{5,4,3,2,1,0:T(8,128)(2,1)} custom-call(s32[3]{0:T(128)} %pad_add_fusion.1.here_ref, bf16[2,2,2,2,32,2304]{5,4,3,2,1,0:T(8,128)(2,1)} %pad_maximum_fusion.3.refs_0_, bf16[2,2,2,2,32,2304]{5,4,3,2,1,0:T(8,128)(2,1)} %pad_maximum_fusion.4.refs_1_), custom_call_target="tpu_custom_call" | custom-call | bytes 9437184 | tf_op jit(solution)/shard_map/pallas_call | solution.py:84
  821.3 11.7 fusion.104
  833.0 17.0 %multiply_convert_fusion.1 = (bf16[1024,2304]{1,0:T(8,128)(2,1)}, bf16[1024,2304]{1,0:T(8,128)(2,1)}, bf16[1024,2304]{1,0:T(8,128)(2,1)}) fusion(f32[1024,2304]{1,0:T(8,128)} %fusion.133, f32[1024,2304]{1,0:T(8,128)} %fusion.104, bf16[1024,2304]{1,0:T(8,128)(2,1)} %bitcast.409, bf16[512,1024]{1,0:T(8,128)(2,1)} %collective-permute-done.19, ...), kind=kOutput, calls=%fused_computation.1 | convolution fusion | flops 4873781248 | bytes 39845888 | tf_op jit(solution)/shard_map/dot_general | solution.py:48
  850.1 7.4 fusion.132
  857.5 8.5 convolution_convert_fusion
  866.6 9.3 fusion.134
  876.0 7.3 convolution_add_fusion
  889.5 7.2 convolution_convert_fusion.2
  898.8 8.0 convolution_convert_fusion.1
  907.9 8.1 collective-permute-done.76
  921.6 18.6 %collective-permute-done.56 = bf16[2,2,2,32,2304]{4,3,2,1,0:T(8,128)(2,1)} collective-permute-done((bf16[2,2,2,32,2304]{4,3,2,1,0:T(8,128)(2,1)S(1)}, bf16[2,2,2,32,2304]{4,3,2,1,0:T(8,128)(2,1)}, u32[]{:S(2)}, u32[]{:S(2)}) %collective-permute-start.56) | collective-permute-done | bytes 1179680 | tf_op jit(solution)/shard_map/ppermute | solution.py:26
  946.2 18.7 %collective-permute-done.63 = bf16[2,2,2,32,2304]{4,3,0,1,2:T(8,128)(2,1)S(1)} collective-permute-done((bf16[2,2,2,32,2304]{4,3,0,1,2:T(8,128)(2,1)S(1)}, bf16[2,2,2,32,2304]{4,3,0,1,2:T(8,128)(2,1)S(1)}, u32[]{:S(2)}, u32[]{:S(2)}) %collective-permute-start.63) | collective-permute-done | bytes 1179680 | tf_op jit(solution)/shard_map/ppermute | solution.py:26
  965.6 4.2 collective-permute-done.61
  971.5 11.0 collective-permute-done.79
  986.9 8.2 collective-permute-done.57
  998.5 8.0 collective-permute-done.64
  1016.7 3.9 fusion.122
  1022.6 13.8 %collective-permute-done.81 = bf16[1,144,1024]{2,1,0:T(8,128)(2,1)S(1)} collective-permute-done((bf16[1,144,1024]{2,1,0:T(8,128)(2,1)S(1)}, bf16[1,144,1024]{2,1,0:T(8,128)(2,1)S(1)}, u32[]{:S(2)}, u32[]{:S(2)}) %collective-permute-start.81) | collective-permute-done | bytes 294944 | tf_op jit(solution)/shard_map/ppermute | solution.py:26
  1036.5 13.1 %collective-permute-start.66 = (bf16[2,32,2304]{2,1,0:T(8,128)(2,1)S(1)}, bf16[2,32,2304]{2,1,0:T(8,128)(2,1)S(1)}, u32[]{:S(2)}, u32[]{:S(2)}) collective-permute-start(bf16[2,32,2304]{2,1,0:T(8,128)(2,1)S(1)} %get-tuple-element.62), channel_id=1, source_target_pairs={{0,4},{1,5},{2,6},{3,7},{4,0},{5,1},{6,2},{7,3},{8,12},{9,13},{10,... | collective-permute-start | bytes 884744 | tf_op jit(solution)/shard_map/ppermute | solution.py:26
  1049.5 13.5 %collective-permute-start.67 = (bf16[2,32,2304]{2,1,0:T(8,128)(2,1)S(1)}, bf16[2,32,2304]{2,1,0:T(8,128)(2,1)S(1)}, u32[]{:S(2)}, u32[]{:S(2)}) collective-permute-start(bf16[2,32,2304]{2,1,0:T(8,128)(2,1)S(1)} %get-tuple-element.63), channel_id=1, source_target_pairs={{0,6},{1,7},{2,0},{3,1},{4,2},{5,3},{6,4},{7,5},{8,14},{9,15},{10,... | collective-permute-start | bytes 884744 | tf_op jit(solution)/shard_map/ppermute | solution.py:26
  1065.2 9.1 collective-permute-done.66
  1075.5 3.9 multiply_reduce_fusion.3
  1092.9 3.4 fusion
  1097.9 3.7 convolution_convert_fusion.3
  1107.0 18.4 %collective-permute-done.72 = bf16[1,2,32,1024]{3,2,1,0:T(8,128)(2,1)S(1)} collective-permute-done((bf16[1,2,32,1024]{3,2,1,0:T(8,128)(2,1)S(1)}, bf16[1,2,32,1024]{3,2,1,0:T(8,128)(2,1)S(1)}, u32[]{:S(2)}, u32[]{:S(2)}) %collective-permute-start.72) | collective-permute-done | bytes 131104 | tf_op jit(solution)/shard_map/ppermute | solution.py:26
  1125.7 3.4 collective-permute-start.73
  1135.1 6.6 collective-permute-done.50
  1142.7 6.8 collective-permute-done.48
  1154.9 3.6 collective-permute-done.51
  1158.5 5.6 collective-permute-done.52
  (511 shorter events, 225.8 us)
Async XLA Ops:
  1.6 25.1 %collective-permute-start.14 = (bf16[1,32,1024]{2,1,0:T(8,128)(2,1)S(1)}, bf16[1,32,1024]{2,1,0:T(8,128)(2,1)S(1)}, u32[]{:S(2)}, u32[]{:S(2)}) collective-permute-start(bf16[1,32,1024]{2,1,0:T(8,128)(2,1)S(1)} %get-tuple-element.121), channel_id=1, source_target_pairs={{0,4},{1,5},{2,6},{3,7},{4,0},{5,1},{6,2},{7,3},{8,12},{9,13},{10,... | collective-permute-start | bytes 196616 | tf_op jit(solution)/shard_map/ppermute | solution.py:26
  7.1 21.3 %collective-permute-start.11 = (bf16[1,32,1024]{2,1,0:T(8,128)(2,1)S(1)}, bf16[1,32,1024]{2,1,0:T(8,128)(2,1)S(1)}, u32[]{:S(2)}, u32[]{:S(2)}) collective-permute-start(bf16[1,32,1024]{2,1,0:T(8,128)(2,1)S(1)} %get-tuple-element.121), channel_id=1, source_target_pairs={{0,2},{1,3},{2,4},{3,5},{4,6},{5,7},{6,0},{7,1},{8,10},{9,11},{10,... | collective-permute-start | bytes 196616 | tf_op jit(solution)/shard_map/ppermute | solution.py:26
  9.6 24.0 %collective-permute-start.37 = (bf16[1,144,1024]{2,1,0:T(8,128)(2,1)}, bf16[1,144,1024]{2,1,0:T(8,128)(2,1)S(1)}, u32[]{:S(2)}, u32[]{:S(2)}) collective-permute-start(bf16[1,144,1024]{2,1,0:T(8,128)(2,1)} %get-tuple-element.94), channel_id=1, source_target_pairs={{0,4},{1,5},{2,6},{3,7},{4,0},{5,1},{6,2},{7,3},{8,12},{9,13},{10,... | collective-permute-start | bytes 884744 | tf_op jit(solution)/shard_map/ppermute | solution.py:26
  33.6 120.2 %collective-permute-start.42 = (bf16[512,1024]{1,0:T(8,128)(2,1)}, bf16[512,1024]{1,0:T(8,128)(2,1)}, u32[]{:S(2)}, u32[]{:S(2)}) collective-permute-start(bf16[512,1024]{1,0:T(8,128)(2,1)} %param.21), channel_id=1, source_target_pairs={{0,8},{8,0},{16,24},{24,16},{1,9},{9,1},{17,25},{25,17},{2,10},{10... | collective-permute-start | bytes 3145736 | tf_op jit(solution)/shard_map/ppermute | solution.py:26
  33.6 118.8 %collective-permute-start = (bf16[512,1024]{1,0:T(8,128)(2,1)S(1)}, bf16[512,1024]{1,0:T(8,128)(2,1)S(1)}, u32[]{:S(2)}, u32[]{:S(2)}) collective-permute-start(bf16[512,1024]{1,0:T(8,128)(2,1)S(1)} %copy-done.14), channel_id=1, source_target_pairs={{0,8},{8,0},{16,24},{24,16},{1,9},{9,1},{17,25},{25,17},{2,10},{10... | collective-permute-start | bytes 3145736 | tf_op jit(solution)/shard_map/ppermute | solution.py:26
  42.9 42.4 %collective-permute-start.5 = (bf16[2,32,1664]{2,1,0:T(8,128)(2,1)}, bf16[2,32,1664]{2,1,0:T(8,128)(2,1)}, u32[]{:S(2)}, u32[]{:S(2)}) collective-permute-start(bf16[2,32,1664]{2,1,0:T(8,128)(2,1)} %pad_maximum_fusion.39), channel_id=1, source_target_pairs={{0,4},{1,5},{2,6},{3,7},{4,0},{5,1},{6,2},{7,3},{8,12},{9,13},{10,... | collective-permute-start | bytes 638984 | tf_op jit(solution)/shard_map/ppermute | solution.py:26
  46.6 40.8 %collective-permute-start.6 = (bf16[2,32,1664]{2,1,0:T(8,128)(2,1)}, bf16[2,32,1664]{2,1,0:T(8,128)(2,1)}, u32[]{:S(2)}, u32[]{:S(2)}) collective-permute-start(bf16[2,32,1664]{2,1,0:T(8,128)(2,1)} %pad_maximum_fusion.39), channel_id=1, source_target_pairs={{0,6},{1,7},{2,0},{3,1},{4,2},{5,3},{6,4},{7,5},{8,14},{9,15},{10,... | collective-permute-start | bytes 638984 | tf_op jit(solution)/shard_map/ppermute | solution.py:26
  50.8 47.8 %collective-permute-start.23 = (bf16[2,32,2304]{2,1,0:T(8,128)(2,1)S(1)}, bf16[2,32,2304]{2,1,0:T(8,128)(2,1)}, u32[]{:S(2)}, u32[]{:S(2)}) collective-permute-start(bf16[2,32,2304]{2,1,0:T(8,128)(2,1)S(1)} %get-tuple-element.82), channel_id=1, source_target_pairs={{0,4},{1,5},{2,6},{3,7},{4,0},{5,1},{6,2},{7,3},{8,12},{9,13},{10,... | collective-permute-start | bytes 884744 | tf_op jit(solution)/shard_map/ppermute | solution.py:26
  97.0 41.4 %collective-permute-start.39 = (bf16[2,1,144,1024]{3,2,0,1:T(8,128)(2,1)S(1)}, bf16[2,1,144,1024]{3,2,0,1:T(8,128)(2,1)S(1)}, u32[]{:S(2)}, u32[]{:S(2)}) collective-permute-start(bf16[2,1,144,1024]{3,2,0,1:T(8,128)(2,1)S(1)} %get-tuple-element.90), channel_id=1, source_target_pairs={{0,1},{1,0},{2,3},{3,2},{4,5},{5,4},{6,7},{7,6},{8,9},{9,8},{10,11... | collective-permute-start | bytes 1769480 | tf_op jit(solution)/shard_map/ppermute | solution.py:26
  140.1 22.1 %collective-permute-start.25 = (bf16[2,2,32,2304]{3,2,1,0:T(8,128)(2,1)S(1)}, bf16[2,2,32,2304]{3,2,1,0:T(8,128)(2,1)S(1)}, u32[]{:S(2)}, u32[]{:S(2)}) collective-permute-start(bf16[2,2,32,2304]{3,2,1,0:T(8,128)(2,1)S(1)} %get-tuple-element.96), channel_id=1, source_target_pairs={{0,1},{1,0},{2,3},{3,2},{4,5},{5,4},{6,7},{7,6},{8,9},{9,8},{10,11... | collective-permute-start | bytes 1769480 | tf_op jit(solution)/shard_map/ppermute | solution.py:26
  150.2 24.6 %collective-permute-start.32 = (bf16[2,2,32,2304]{3,2,1,0:T(8,128)(2,1)S(1)}, bf16[2,2,32,2304]{3,2,1,0:T(8,128)(2,1)S(1)}, u32[]{:S(2)}, u32[]{:S(2)}) collective-permute-start(bf16[2,2,32,2304]{3,2,1,0:T(8,128)(2,1)S(1)} %get-tuple-element.100), channel_id=1, source_target_pairs={{0,1},{1,0},{2,3},{3,2},{4,5},{5,4},{6,7},{7,6},{8,9},{9,8},{10,11... | collective-permute-start | bytes 1769480 | tf_op jit(solution)/shard_map/ppermute | solution.py:26
  152.5 198.3 %collective-permute-start.28 = (bf16[2,2,32,2304]{3,2,1,0:T(8,128)(2,1)}, bf16[2,2,32,2304]{3,2,1,0:T(8,128)(2,1)}, u32[]{:S(2)}, u32[]{:S(2)}) collective-permute-start(bf16[2,2,32,2304]{3,2,1,0:T(8,128)(2,1)} %get-tuple-element.102), channel_id=1, source_target_pairs={{0,16},{8,24},{16,0},{24,8},{1,17},{9,25},{17,1},{25,9},{2,18},{10... | collective-permute-start | bytes 1769480 | tf_op jit(solution)/shard_map/ppermute | solution.py:26
  153.8 199.5 %collective-permute-start.40 = (bf16[2,2,1,144,1024]{4,3,1,0,2:T(8,128)(2,1)}, bf16[2,2,1,144,1024]{4,3,1,0,2:T(8,128)(2,1)}, u32[]{:S(2)}, u32[]{:S(2)}) collective-permute-start(bf16[2,2,1,144,1024]{4,3,1,0,2:T(8,128)(2,1)} %get-tuple-element.65), channel_id=1, source_target_pairs={{0,16},{8,24},{16,0},{24,8},{1,17},{9,25},{17,1},{25,9},{2,18},{10... | collective-permute-start | bytes 3538952 | tf_op jit(solution)/shard_map/ppermute | solution.py:26
  162.2 56.7 %collective-permute-start.8 = (bf16[2,2,2,32,1664]{4,3,2,1,0:T(8,128)(2,1)S(1)}, bf16[2,2,2,32,1664]{4,3,2,1,0:T(8,128)(2,1)S(1)}, u32[]{:S(2)}, u32[]{:S(2)}) collective-permute-start(bf16[2,2,2,32,1664]{4,3,2,1,0:T(8,128)(2,1)S(1)} %get-tuple-element.79), channel_id=1, source_target_pairs={{0,16},{8,24},{16,0},{24,8},{1,17},{9,25},{17,1},{25,9},{2,18},{10... | collective-permute-start | bytes 2555912 | tf_op jit(solution)/shard_map/ppermute | solution.py:26
  165.8 55.0 %collective-permute-start.4 = (bf16[2,2,2,32,1664]{4,3,2,1,0:T(8,128)(2,1)S(1)}, bf16[2,2,2,32,1664]{4,3,2,1,0:T(8,128)(2,1)S(1)}, u32[]{:S(2)}, u32[]{:S(2)}) collective-permute-start(bf16[2,2,2,32,1664]{4,3,2,1,0:T(8,128)(2,1)S(1)} %get-tuple-element.81), channel_id=1, source_target_pairs={{0,1},{1,0},{2,3},{3,2},{4,5},{5,4},{6,7},{7,6},{8,9},{9,8},{10,11... | collective-permute-start | bytes 2555912 | tf_op jit(solution)/shard_map/ppermute | solution.py:26
  174.8 183.0 %collective-permute-start.36 = (bf16[2,2,1,144,1024]{4,3,1,2,0:T(8,128)(2,1)}, bf16[2,2,1,144,1024]{4,3,1,2,0:T(8,128)(2,1)}, u32[]{:S(2)}, u32[]{:S(2)}) collective-permute-start(bf16[2,2,1,144,1024]{4,3,1,2,0:T(8,128)(2,1)} %get-tuple-element.67), channel_id=1, source_target_pairs={{0,1},{1,0},{2,3},{3,2},{4,5},{5,4},{6,7},{7,6},{8,9},{9,8},{10,11... | collective-permute-start | bytes 3538952 | tf_op jit(solution)/shard_map/ppermute | solution.py:26
  218.9 297.0 %collective-permute-start.26 = (bf16[2,2,2,32,2304]{4,3,2,1,0:T(8,128)(2,1)}, bf16[2,2,2,32,2304]{4,3,2,1,0:T(8,128)(2,1)}, u32[]{:S(2)}, u32[]{:S(2)}) collective-permute-start(bf16[2,2,2,32,2304]{4,3,2,1,0:T(8,128)(2,1)} %get-tuple-element.69), channel_id=1, source_target_pairs={{0,16},{8,24},{16,0},{24,8},{1,17},{9,25},{17,1},{25,9},{2,18},{10... | collective-permute-start | bytes 3538952 | tf_op jit(solution)/shard_map/ppermute | solution.py:26
  340.9 181.7 %collective-permute-start.22 = (bf16[2,2,2,32,2304]{4,3,2,1,0:T(8,128)(2,1)}, bf16[2,2,2,32,2304]{4,3,2,1,0:T(8,128)(2,1)}, u32[]{:S(2)}, u32[]{:S(2)}) collective-permute-start(bf16[2,2,2,32,2304]{4,3,2,1,0:T(8,128)(2,1)} %get-tuple-element.71), channel_id=1, source_target_pairs={{0,1},{1,0},{2,3},{3,2},{4,5},{5,4},{6,7},{7,6},{8,9},{9,8},{10,11... | collective-permute-start | bytes 3538952 | tf_op jit(solution)/shard_map/ppermute | solution.py:26
  350.7 168.3 %collective-permute-start.18 = (f32[512,1024]{1,0:T(8,128)S(1)}, f32[512,1024]{1,0:T(8,128)}, u32[]{:S(2)}, u32[]{:S(2)}) collective-permute-start(f32[512,1024]{1,0:T(8,128)S(1)} %slice.236), channel_id=1, source_target_pairs={{0,8},{8,0},{16,24},{24,16},{1,9},{9,1},{17,25},{25,17},{2,10},{10... | collective-permute-start | bytes 6291464 | tf_op jit(solution)/shard_map/ppermute | solution.py:26
  353.3 317.2 %collective-permute-start.33 = (bf16[2,2,2,32,2304]{4,3,2,1,0:T(8,128)(2,1)}, bf16[2,2,2,32,2304]{4,3,2,1,0:T(8,128)(2,1)}, u32[]{:S(2)}, u32[]{:S(2)}) collective-permute-start(bf16[2,2,2,32,2304]{4,3,2,1,0:T(8,128)(2,1)} %get-tuple-element.73), channel_id=1, source_target_pairs={{0,16},{8,24},{16,0},{24,8},{1,17},{9,25},{17,1},{25,9},{2,18},{10... | collective-permute-start | bytes 3538952 | tf_op jit(solution)/shard_map/ppermute | solution.py:26
  357.9 315.7 %collective-permute-start.29 = (bf16[2,2,2,32,2304]{4,3,2,1,0:T(8,128)(2,1)}, bf16[2,2,2,32,2304]{4,3,2,1,0:T(8,128)(2,1)}, u32[]{:S(2)}, u32[]{:S(2)}) collective-permute-start(bf16[2,2,2,32,2304]{4,3,2,1,0:T(8,128)(2,1)} %get-tuple-element.75), channel_id=1, source_target_pairs={{0,1},{1,0},{2,3},{3,2},{4,5},{5,4},{6,7},{7,6},{8,9},{9,8},{10,11... | collective-permute-start | bytes 3538952 | tf_op jit(solution)/shard_map/ppermute | solution.py:26
  522.4 298.9 %collective-permute-start.19 = (bf16[512,1024]{1,0:T(8,128)(2,1)}, bf16[512,1024]{1,0:T(8,128)(2,1)}, u32[]{:S(2)}, u32[]{:S(2)}) collective-permute-start(bf16[512,1024]{1,0:T(8,128)(2,1)} %multiply_convert_fusion.4), channel_id=1, source_target_pairs={{0,8},{8,0},{16,24},{24,16},{1,9},{9,1},{17,25},{25,17},{2,10},{10... | collective-permute-start | bytes 3145736 | tf_op jit(solution)/shard_map/ppermute | solution.py:26
  866.3 148.3 %collective-permute-start.41 = (f32[512,1024]{1,0:T(8,128)S(1)}, f32[512,1024]{1,0:T(8,128)}, u32[]{:S(2)}, u32[]{:S(2)}) collective-permute-start(f32[512,1024]{1,0:T(8,128)S(1)} %slice.239), channel_id=1, source_target_pairs={{0,8},{8,0},{16,24},{24,16},{1,9},{9,1},{17,25},{25,17},{2,10},{10... | collective-permute-start | bytes 6291464 | tf_op jit(solution)/shard_map/ppermute | solution.py:26
  883.5 129.8 %collective-permute-start.43 = (f32[512,1024]{1,0:T(8,128)S(1)}, f32[512,1024]{1,0:T(8,128)S(1)}, u32[]{:S(2)}, u32[]{:S(2)}) collective-permute-start(f32[512,1024]{1,0:T(8,128)S(1)} %slice.241), channel_id=1, source_target_pairs={{0,8},{8,0},{16,24},{24,16},{1,9},{9,1},{17,25},{25,17},{2,10},{10... | collective-permute-start | bytes 6291464 | tf_op jit(solution)/shard_map/ppermute | solution.py:26
  885.8 33.6 %collective-permute-start.78 = (bf16[1,2,2,144,1024]{4,3,1,2,0:T(8,128)(2,1)}, bf16[1,2,2,144,1024]{4,3,1,2,0:T(8,128)(2,1)S(1)}, u32[]{:S(2)}, u32[]{:S(2)}) collective-permute-start(bf16[1,2,2,144,1024]{4,3,1,2,0:T(8,128)(2,1)} %bitcast.392), channel_id=1, source_target_pairs={{0,16},{8,24},{16,0},{24,8},{1,17},{9,25},{17,1},{25,9},{2,18},{10... | collective-permute-start | bytes 3538952 | tf_op jit(solution)/shard_map/ppermute | solution.py:26
  887.5 28.5 %collective-permute-start.76 = (bf16[2,1,2,144,1024]{4,3,2,1,0:T(8,128)(2,1)}, bf16[2,1,2,144,1024]{4,3,2,1,0:T(8,128)(2,1)}, u32[]{:S(2)}, u32[]{:S(2)}) collective-permute-start(bf16[2,1,2,144,1024]{4,3,2,1,0:T(8,128)(2,1)} %dynamic-slice_bitcast_fusion), channel_id=1, source_target_pairs={{0,1},{1,0},{2,3},{3,2},{4,5},{5,4},{6,7},{7,6},{8,9},{9,8},{10,11... | collective-permute-start | bytes 3538952 | tf_op jit(solution)/shard_map/ppermute | solution.py:26
  897.3 43.0 %collective-permute-start.56 = (bf16[2,2,2,32,2304]{4,3,2,1,0:T(8,128)(2,1)S(1)}, bf16[2,2,2,32,2304]{4,3,2,1,0:T(8,128)(2,1)}, u32[]{:S(2)}, u32[]{:S(2)}) collective-permute-start(bf16[2,2,2,32,2304]{4,3,2,1,0:T(8,128)(2,1)S(1)} %dynamic-slice_bitcast_fusion.1), channel_id=1, source_target_pairs={{0,16},{8,24},{16,0},{24,8},{1,17},{9,25},{17,1},{25,9},{2,18},{10... | collective-permute-start | bytes 3538952 | tf_op jit(solution)/shard_map/ppermute | solution.py:26
  916.0 28.6 %collective-permute-start.54 = (bf16[2,2,2,32,2304]{4,3,2,1,0:T(8,128)(2,1)S(1)}, bf16[2,2,2,32,2304]{4,3,2,1,0:T(8,128)(2,1)S(1)}, u32[]{:S(2)}, u32[]{:S(2)}) collective-permute-start(bf16[2,2,2,32,2304]{4,3,2,1,0:T(8,128)(2,1)S(1)} %dynamic-slice_bitcast_fusion.2), channel_id=1, source_target_pairs={{0,1},{1,0},{2,3},{3,2},{4,5},{5,4},{6,7},{7,6},{8,9},{9,8},{10,11... | collective-permute-start | bytes 3538952 | tf_op jit(solution)/shard_map/ppermute | solution.py:26
  919.5 45.3 %collective-permute-start.63 = (bf16[2,2,2,32,2304]{4,3,0,1,2:T(8,128)(2,1)S(1)}, bf16[2,2,2,32,2304]{4,3,0,1,2:T(8,128)(2,1)S(1)}, u32[]{:S(2)}, u32[]{:S(2)}) collective-permute-start(bf16[2,2,2,32,2304]{4,3,0,1,2:T(8,128)(2,1)S(1)} %bitcast.427), channel_id=1, source_target_pairs={{0,16},{8,24},{16,0},{24,8},{1,17},{9,25},{17,1},{25,9},{2,18},{10... | collective-permute-start | bytes 3538952 | tf_op jit(solution)/shard_map/ppermute | solution.py:26
  940.2 29.6 %collective-permute-start.61 = (bf16[2,2,2,32,2304]{4,3,1,2,0:T(8,128)(2,1)S(1)}, bf16[2,2,2,32,2304]{4,3,1,2,0:T(8,128)(2,1)S(1)}, u32[]{:S(2)}, u32[]{:S(2)}) collective-permute-start(bf16[2,2,2,32,2304]{4,3,1,2,0:T(8,128)(2,1)S(1)} %bitcast.426), channel_id=1, source_target_pairs={{0,1},{1,0},{2,3},{3,2},{4,5},{5,4},{6,7},{7,6},{8,9},{9,8},{10,11... | collective-permute-start | bytes 3538952 | tf_op jit(solution)/shard_map/ppermute | solution.py:26
  944.6 37.9 %collective-permute-start.79 = (bf16[1,2,144,1024]{3,2,1,0:T(8,128)(2,1)S(1)}, bf16[1,2,144,1024]{3,2,1,0:T(8,128)(2,1)S(1)}, u32[]{:S(2)}, u32[]{:S(2)}) collective-permute-start(bf16[1,2,144,1024]{3,2,1,0:T(8,128)(2,1)S(1)} %dynamic-slice_bitcast_fusion.7), channel_id=1, source_target_pairs={{0,1},{1,0},{2,3},{3,2},{4,5},{5,4},{6,7},{7,6},{8,9},{9,8},{10,11... | collective-permute-start | bytes 1769480 | tf_op jit(solution)/shard_map/ppermute | solution.py:26
  969.9 25.3 %collective-permute-start.57 = (bf16[2,2,32,2304]{3,2,1,0:T(8,128)(2,1)S(1)}, bf16[2,2,32,2304]{3,2,1,0:T(8,128)(2,1)S(1)}, u32[]{:S(2)}, u32[]{:S(2)}) collective-permute-start(bf16[2,2,32,2304]{3,2,1,0:T(8,128)(2,1)S(1)} %dynamic-slice_bitcast_fusion.11), channel_id=1, source_target_pairs={{0,1},{1,0},{2,3},{3,2},{4,5},{5,4},{6,7},{7,6},{8,9},{9,8},{10,11... | collective-permute-start | bytes 1769480 | tf_op jit(solution)/shard_map/ppermute | solution.py:26
  984.6 22.0 %collective-permute-start.64 = (bf16[2,2,32,2304]{3,2,0,1:T(8,128)(2,1)S(1)}, bf16[2,2,32,2304]{3,2,0,1:T(8,128)(2,1)S(1)}, u32[]{:S(2)}, u32[]{:S(2)}) collective-permute-start(bf16[2,2,32,2304]{3,2,0,1:T(8,128)(2,1)S(1)} %dynamic-slice_bitcast_fusion.9), channel_id=1, source_target_pairs={{0,1},{1,0},{2,3},{3,2},{4,5},{5,4},{6,7},{7,6},{8,9},{9,8},{10,11... | collective-permute-start | bytes 1769480 | tf_op jit(solution)/shard_map/ppermute | solution.py:26
  997.1 23.5 %collective-permute-start.80 = (bf16[1,144,1024]{2,1,0:T(8,128)(2,1)S(1)}, bf16[1,144,1024]{2,1,0:T(8,128)(2,1)S(1)}, u32[]{:S(2)}, u32[]{:S(2)}) collective-permute-start(bf16[1,144,1024]{2,1,0:T(8,128)(2,1)S(1)} %get-tuple-element.55), channel_id=1, source_target_pairs={{0,2},{1,3},{2,4},{3,5},{4,6},{5,7},{6,0},{7,1},{8,10},{9,11},{10,... | collective-permute-start | bytes 884744 | tf_op jit(solution)/shard_map/ppermute | solution.py:26
  1006.5 29.9 %collective-permute-start.81 = (bf16[1,144,1024]{2,1,0:T(8,128)(2,1)S(1)}, bf16[1,144,1024]{2,1,0:T(8,128)(2,1)S(1)}, u32[]{:S(2)}, u32[]{:S(2)}) collective-permute-start(bf16[1,144,1024]{2,1,0:T(8,128)(2,1)S(1)} %get-tuple-element.56), channel_id=1, source_target_pairs={{0,4},{1,5},{2,6},{3,7},{4,0},{5,1},{6,2},{7,3},{8,12},{9,13},{10,... | collective-permute-start | bytes 884744 | tf_op jit(solution)/shard_map/ppermute | solution.py:26
  1010.1 26.4 %collective-permute-start.58 = (bf16[2,32,2304]{2,1,0:T(8,128)(2,1)S(1)}, bf16[2,32,2304]{2,1,0:T(8,128)(2,1)S(1)}, u32[]{:S(2)}, u32[]{:S(2)}) collective-permute-start(bf16[2,32,2304]{2,1,0:T(8,128)(2,1)S(1)} %get-tuple-element.58), channel_id=1, source_target_pairs={{0,2},{1,3},{2,4},{3,5},{4,6},{5,7},{6,0},{7,1},{8,10},{9,11},{10,... | collective-permute-start | bytes 884744 | tf_op jit(solution)/shard_map/ppermute | solution.py:26
  1013.4 36.1 %collective-permute-start.59 = (bf16[2,32,2304]{2,1,0:T(8,128)(2,1)S(1)}, bf16[2,32,2304]{2,1,0:T(8,128)(2,1)S(1)}, u32[]{:S(2)}, u32[]{:S(2)}) collective-permute-start(bf16[2,32,2304]{2,1,0:T(8,128)(2,1)S(1)} %get-tuple-element.59), channel_id=1, source_target_pairs={{0,4},{1,5},{2,6},{3,7},{4,0},{5,1},{6,2},{7,3},{8,12},{9,13},{10,... | collective-permute-start | bytes 884744 | tf_op jit(solution)/shard_map/ppermute | solution.py:26
  1014.6 48.5 %collective-permute-start.60 = (bf16[2,32,2304]{2,1,0:T(8,128)(2,1)S(1)}, bf16[2,32,2304]{2,1,0:T(8,128)(2,1)S(1)}, u32[]{:S(2)}, u32[]{:S(2)}) collective-permute-start(bf16[2,32,2304]{2,1,0:T(8,128)(2,1)S(1)} %get-tuple-element.60), channel_id=1, source_target_pairs={{0,6},{1,7},{2,0},{3,1},{4,2},{5,3},{6,4},{7,5},{8,14},{9,15},{10,... | collective-permute-start | bytes 884744 | tf_op jit(solution)/shard_map/ppermute | solution.py:26
  1020.6 43.6 %collective-permute-start.82 = (bf16[1,144,1024]{2,1,0:T(8,128)(2,1)S(1)}, bf16[1,144,1024]{2,1,0:T(8,128)(2,1)S(1)}, u32[]{:S(2)}, u32[]{:S(2)}) collective-permute-start(bf16[1,144,1024]{2,1,0:T(8,128)(2,1)S(1)} %get-tuple-element.57), channel_id=1, source_target_pairs={{0,6},{1,7},{2,0},{3,1},{4,2},{5,3},{6,4},{7,5},{8,14},{9,15},{10,... | collective-permute-start | bytes 884744 | tf_op jit(solution)/shard_map/ppermute | solution.py:26
  1036.5 28.8 %collective-permute-start.65 = (bf16[2,32,2304]{2,1,0:T(8,128)(2,1)S(1)}, bf16[2,32,2304]{2,1,0:T(8,128)(2,1)S(1)}, u32[]{:S(2)}, u32[]{:S(2)}) collective-permute-start(bf16[2,32,2304]{2,1,0:T(8,128)(2,1)S(1)} %get-tuple-element.61), channel_id=1, source_target_pairs={{0,2},{1,3},{2,4},{3,5},{4,6},{5,7},{6,0},{7,1},{8,10},{9,11},{10,... | collective-permute-start | bytes 884744 | tf_op jit(solution)/shard_map/ppermute | solution.py:26
  1036.5 37.9 %collective-permute-start.66 = (bf16[2,32,2304]{2,1,0:T(8,128)(2,1)S(1)}, bf16[2,32,2304]{2,1,0:T(8,128)(2,1)S(1)}, u32[]{:S(2)}, u32[]{:S(2)}) collective-permute-start(bf16[2,32,2304]{2,1,0:T(8,128)(2,1)S(1)} %get-tuple-element.62), channel_id=1, source_target_pairs={{0,4},{1,5},{2,6},{3,7},{4,0},{5,1},{6,2},{7,3},{8,12},{9,13},{10,... | collective-permute-start | bytes 884744 | tf_op jit(solution)/shard_map/ppermute | solution.py:26
  1049.5 24.8 %collective-permute-start.67 = (bf16[2,32,2304]{2,1,0:T(8,128)(2,1)S(1)}, bf16[2,32,2304]{2,1,0:T(8,128)(2,1)S(1)}, u32[]{:S(2)}, u32[]{:S(2)}) collective-permute-start(bf16[2,32,2304]{2,1,0:T(8,128)(2,1)S(1)} %get-tuple-element.63), channel_id=1, source_target_pairs={{0,6},{1,7},{2,0},{3,1},{4,2},{5,3},{6,4},{7,5},{8,14},{9,15},{10,... | collective-permute-start | bytes 884744 | tf_op jit(solution)/shard_map/ppermute | solution.py:26
  1096.6 67.7 %collective-permute-start.46 = (f32[512,1024]{1,0:T(8,128)S(1)}, f32[512,1024]{1,0:T(8,128)S(1)}, u32[]{:S(2)}, u32[]{:S(2)}) collective-permute-start(f32[512,1024]{1,0:T(8,128)S(1)} %slice.249), channel_id=1, source_target_pairs={{0,8},{8,0},{16,24},{24,16},{1,9},{9,1},{17,25},{25,17},{2,10},{10... | collective-permute-start | bytes 6291464 | tf_op jit(solution)/shard_map/ppermute | solution.py:26
  1101.9 30.4 %collective-permute-start.49 = (bf16[2,2,2,32,1536]{4,3,2,1,0:T(8,128)(2,1)S(1)}, bf16[2,2,2,32,1536]{4,3,2,1,0:T(8,128)(2,1)S(1)}, u32[]{:S(2)}, u32[]{:S(2)}) collective-permute-start(bf16[2,2,2,32,1536]{4,3,2,1,0:T(8,128)(2,1)S(1)} %dynamic-slice_bitcast_fusion.5), channel_id=1, source_target_pairs={{0,16},{8,24},{16,0},{24,8},{1,17},{9,25},{17,1},{25,9},{2,18},{10... | collective-permute-start | bytes 2359304 | tf_op jit(solution)/shard_map/ppermute | solution.py:26
  1102.8 30.3 %collective-permute-start.47 = (bf16[2,2,2,32,1536]{4,3,2,1,0:T(8,128)(2,1)S(1)}, bf16[2,2,2,32,1536]{4,3,2,1,0:T(8,128)(2,1)S(1)}, u32[]{:S(2)}, u32[]{:S(2)}) collective-permute-start(bf16[2,2,2,32,1536]{4,3,2,1,0:T(8,128)(2,1)S(1)} %dynamic-slice_bitcast_fusion.6), channel_id=1, source_target_pairs={{0,1},{1,0},{2,3},{3,2},{4,5},{5,4},{6,7},{7,6},{8,9},{9,8},{10,11... | collective-permute-start | bytes 2359304 | tf_op jit(solution)/shard_map/ppermute | solution.py:26
  1125.7 25.6 %collective-permute-start.73 = (bf16[1,32,1024]{2,1,0:T(8,128)(2,1)S(1)}, bf16[1,32,1024]{2,1,0:T(8,128)(2,1)S(1)}, u32[]{:S(2)}, u32[]{:S(2)}) collective-permute-start(bf16[1,32,1024]{2,1,0:T(8,128)(2,1)S(1)} %get-tuple-element.109), channel_id=1, source_target_pairs={{0,2},{1,3},{2,4},{3,5},{4,6},{5,7},{6,0},{7,1},{8,10},{9,11},{10,... | collective-permute-start | bytes 196616 | tf_op jit(solution)/shard_map/ppermute | solution.py:26
  1129.1 22.4 %collective-permute-start.74 = (bf16[1,32,1024]{2,1,0:T(8,128)(2,1)S(1)}, bf16[1,32,1024]{2,1,0:T(8,128)(2,1)S(1)}, u32[]{:S(2)}, u32[]{:S(2)}) collective-permute-start(bf16[1,32,1024]{2,1,0:T(8,128)(2,1)S(1)} %get-tuple-element.110), channel_id=1, source_target_pairs={{0,4},{1,5},{2,6},{3,7},{4,0},{5,1},{6,2},{7,3},{8,12},{9,13},{10,... | collective-permute-start | bytes 196616 | tf_op jit(solution)/shard_map/ppermute | solution.py:26
  1132.4 21.8 %collective-permute-start.75 = (bf16[1,32,1024]{2,1,0:T(8,128)(2,1)S(1)}, bf16[1,32,1024]{2,1,0:T(8,128)(2,1)S(1)}, u32[]{:S(2)}, u32[]{:S(2)}) collective-permute-start(bf16[1,32,1024]{2,1,0:T(8,128)(2,1)S(1)} %get-tuple-element.111), channel_id=1, source_target_pairs={{0,6},{1,7},{2,0},{3,1},{4,2},{5,3},{6,4},{7,5},{8,14},{9,15},{10,... | collective-permute-start | bytes 196616 | tf_op jit(solution)/shard_map/ppermute | solution.py:26
  (119 other events, 1467.9 us)

commit v2 on v1

v2 whole, which is shorter than its diff:
```python
import functools

import jax
import jax.numpy as jnp
from jax import lax
from jax.experimental import pallas as pl
from jax.experimental.pallas import tpu as pltpu
from jax.sharding import Mesh
from jax.sharding import PartitionSpec as P

EPS = 1e-05
AXES = ("x", "core", "z", "y")
BF = jnp.bfloat16
F32 = jnp.float32


class Axis:
    def __init__(self, name):
        self.name, self.size = name, lax.axis_size(name)
        self.here = lax.axis_index(name)
        near = sorted(range(1, self.size), key=lambda by: (min(by, self.size - by), by))
        self.steps = tuple(near)

    def shift(self, value, by=1):
        return lax.ppermute(value, self.name, [(i, (i + by) % self.size) for i in range(self.size)])

    def at(self, by):
        return lax.rem(self.here + by, self.size)


def passed_along(shard, by):
    peers = lax.axis_size(("z", "y"))
    pairs = [(i, i + by) for i in range(peers) if 0 <= i + by < peers]
    return lax.ppermute(shard, ("z", "y"), pairs)


def fence(*values):
    return lax.optimization_barrier(values)


def contract_rows(left, right):
    return lax.dot_general(
        left, right, (((0,), (0,)), ((), ())), preferred_element_type=F32
    )


def contract_cols(left, right):
    return lax.dot_general(
        left, right, (((1,), (1,)), ((), ())), preferred_element_type=F32
    )


def times(left, right):
    return jnp.dot(left, right, preferred_element_type=F32)


def pick(value, at, dim):
    return lax.dynamic_index_in_dim(value, at, dim, keepdims=False)


def ordered(mine, other, here, dim):
    low = jnp.where(here == 0, mine, other)
    high = jnp.where(here == 0, other, mine)
    return jnp.stack([low, high], dim)


def sent(value, axis, dim):
    own = pick(value, axis.here, dim)
    return own, [axis.shift(pick(value, axis.at(by), dim), by) for by in axis.steps]


def summed(own, others):
    total = own.astype(F32)
    for other in others:
        total = total + other.astype(F32)
    return total


def place_body(moves, here_ref, *refs):
    sems = refs[-1]
    copies = []
    for i, (source, target) in enumerate(moves(here_ref, refs[:-1])):
        copy = pltpu.make_async_copy(source, target, sems.at[i])
        copy.start()
        copies.append(copy)
    for copy in copies:
        copy.wait()


def place(moves, count, here, sources, shapes):
    return pl.pallas_call(
        functools.partial(place_body, moves),
        out_shape=[jax.ShapeDtypeStruct(shape, BF) for shape in shapes],
        in_specs=[pl.BlockSpec(memory_space=pltpu.SMEM)]
        + [pl.BlockSpec(memory_space=pl.ANY)] * len(sources),
        out_specs=[pl.BlockSpec(memory_space=pltpu.VMEM)] * len(shapes),
        scratch_shapes=[pltpu.SemaphoreType.DMA((count,))],
        compiler_params=pltpu.CompilerParams(vmem_limit_bytes=48 * 1024 * 1024),
        cost_estimate=pl.CostEstimate(flops=0, bytes_accessed=2**20, transcendentals=0),
    )(here, *sources)


def back(at, by, size):
    return lax.rem(at + size - by, size)


def place_mix(pieces, here, ax, ay, az, columns, width):
    nx, ny, nz = ax.size, ay.size, az.size
    arrays = []
    for piece in pieces:
        if not any(piece[3] is array for array in arrays):
            arrays.append(piece[3])
    rows, half = arrays[0].shape[-2], width // 2
    where = [next(i for i, a in enumerate(arrays) if a is piece[3]) for piece in pieces]

    def moves(at, refs):
        wide, small, narrow = refs[-3:]
        for (dx, dy, backs, _, lead), i in zip(pieces, where, strict=True):
            x, y = back(at[0], dx, nx), back(at[1], dy, ny)
            for n, dz in enumerate(backs):
                z = back(at[2], dz, nz)
                block = refs[i].at[lead + (n,)]
                yield block.at[:, :, pl.ds(0, columns)], wide.at[x, :, z, y]
                yield block.at[:, :, pl.ds(columns, 128)], small.at[x, :, z, y]
                for k in range(2):
                    yield (
                        block.at[k, :, pl.ds(columns + 128, half)],
                        narrow.at[x, z, y, :, pl.ds(k * half, half)],
                    )

    lead = (nx, 2, nz, ny, rows)
    shapes = [lead + (columns,), lead + (128,), (nx, nz, ny, rows, width)]
    wide, small, narrow = place(moves, 4 * nx * ny * nz, here, arrays, shapes)
    return wide.reshape(-1, columns), small.reshape(-1, 128), narrow.reshape(-1, width)


def cost():
    return pl.CostEstimate(flops=0, bytes_accessed=2**16, transcendentals=0)


def params():
    return pltpu.CompilerParams(vmem_limit_bytes=40 * 1024 * 1024)


def whole(array):
    return pl.BlockSpec(
        array.shape, lambda i: (0,) * array.ndim, pipeline_mode=pl.Buffered(1)
    )


def tiles(rows, columns):
    return pl.BlockSpec((rows, columns), lambda i: (i, 0))


def chunks(columns):
    step = 384 if columns % 384 == 0 else 128 if columns % 128 == 0 else columns
    return [(a, step) for a in range(0, columns, step)]


def logistic(v):
    return 0.5 * jnp.tanh(0.5 * v) + 0.5


def forward_body(x_ref, w_ref, ev_ref, s_ref):
    hidden = s_ref.shape[1]
    x = x_ref[...]
    for a, n in chunks(hidden):
        gate = times(x, w_ref[:, a : a + n])
        rise = times(x, w_ref[:, hidden + a : hidden + a + n])
        ev_ref[:, a : a + n] = gate.astype(BF)
        ev_ref[:, hidden + a : hidden + a + n] = rise.astype(BF)
        s_ref[:, a : a + n] = (gate * logistic(gate) * rise).astype(BF)


def ffn_forward(x, w, tile):
    count, both = x.shape[0], w.shape[1]
    return pl.pallas_call(
        forward_body,
        grid=(count // tile,),
        in_specs=[tiles(tile, x.shape[1]), whole(w)],
        out_specs=[tiles(tile, both), tiles(tile, both // 2)],
        out_shape=[
            jax.ShapeDtypeStruct((count, both), BF),
            jax.ShapeDtypeStruct((count, both // 2), BF),
        ],
        compiler_params=params(),
        cost_estimate=cost(),
    )(x, w)


def back_body(half, dy_ref, ev_ref, down_ref, w_ref, dev_ref, keep_ref, send_ref):
    hidden = down_ref.shape[0]
    dy = dy_ref[...]
    for a, n in chunks(hidden):
        back = contract_cols(dy, down_ref[a : a + n, :])
        gate = ev_ref[:, a : a + n].astype(F32)
        rise = ev_ref[:, hidden + a : hidden + a + n].astype(F32)
        sigma = logistic(gate)
        back = back * sigma
        dev_ref[:, a : a + n] = (back * rise * (1.0 + gate * (1.0 - sigma))).astype(BF)
        dev_ref[:, hidden + a : hidden + a + n] = (back * gate).astype(BF)
    split_rows(half, contract_cols(dev_ref[...], w_ref[...]), keep_ref, send_ref)


def split_rows(half, value, keep_ref, send_ref):
    @pl.when(pl.program_id(0) < half)
    def _():
        keep_ref[...] = value

    @pl.when(pl.program_id(0) >= half)
    def _():
        send_ref[...] = value


def split_specs(tile, columns, half):
    return [
        pl.BlockSpec((tile, columns), lambda i: (jnp.minimum(i, half - 1), 0)),
        pl.BlockSpec((tile, columns), lambda i: (jnp.maximum(i - half, 0), 0)),
    ]


def ffn_back(dy, ev, down, w, tile):
    count, width = dy.shape
    both, half = w.shape[1], count // (2 * tile)
    return pl.pallas_call(
        functools.partial(back_body, half),
        grid=(count // tile,),
        in_specs=[tiles(tile, width), tiles(tile, both), whole(down), whole(w)],
        out_specs=[tiles(tile, both)] + split_specs(tile, width, half),
        out_shape=[jax.ShapeDtypeStruct((count, both), BF)]
        + [jax.ShapeDtypeStruct((count // 2, width), F32)] * 2,
        compiler_params=params(),
        cost_estimate=cost(),
    )(dy, ev, down, w)


def fed_body(half, s_ref, down_ref, keep_ref, send_ref):
    split_rows(half, times(s_ref[...], down_ref[...]), keep_ref, send_ref)


def ffn_out(s, down, tile):
    count, width = s.shape[0], down.shape[1]
    half = count // (2 * tile)
    return pl.pallas_call(
        functools.partial(fed_body, half),
        grid=(2 * half,),
        in_specs=[tiles(tile, s.shape[1]), whole(down)],
        out_specs=split_specs(tile, width, half),
        out_shape=[jax.ShapeDtypeStruct((count // 2, width), F32)] * 2,
        compiler_params=params(),
        cost_estimate=cost(),
    )(s, down)


def grad_body(count, *refs):
    total = contract_rows(refs[0][...], refs[count][...])
    for i in range(1, count):
        total = total + contract_rows(refs[i][...], refs[count + i][...])
    for ref in refs[2 * count : -1]:
        total = total + ref[...]
    refs[-1][...] = total.astype(refs[-1].dtype).reshape(refs[-1].shape)


def weight_grad(lefts, rights, tile, out_spec, shape, kind=BF, extra=()):
    count, rows = lefts[0].shape
    left = pl.BlockSpec((count, tile), lambda i: (0, i))
    return pl.pallas_call(
        functools.partial(grad_body, len(lefts)),
        grid=(rows // tile,),
        in_specs=[left] * len(lefts) + [whole(right) for right in rights] + [out_spec] * len(extra),
        out_specs=out_spec,
        out_shape=jax.ShapeDtypeStruct(shape, kind),
        compiler_params=params(),
        cost_estimate=cost(),
    )(*lefts, *rights, *extra)


def gate_up_grad(lefts, rights, nx, nz, rows):
    columns, width = rights[0].shape[1], lefts[0].shape[1]
    tile, lead = nz * 2 * rows, (nx, nz, 2, 2 * rows)
    if tile % 128 == 0:
        spec = pl.BlockSpec((1, nz, 1, 2 * rows, columns), lambda i: (i // 2, 0, i % 2, 0, 0))
        out = weight_grad(lefts, rights, tile, spec, lead + (columns,))
    else:
        out = weight_grad(lefts, rights, 256, tiles(256, columns), (width, columns))
        out = out.reshape(nx, 2, nz, 2 * rows, columns).transpose(0, 2, 1, 3, 4)
    return out.reshape(width, columns)


def per_device(
    block_input,
    in_weight,
    out_weight,
    gate_weight,
    up_weight,
    down_weight,
    norm_gain,
    ffn_gain,
    conv_weight,
    seq_starts,
    cotangent,
):
    ax, ac, az, ay = (Axis(name) for name in AXES)
    nx, nz = ax.size, az.size
    core, y_here = ac.here, ay.here
    here = jnp.stack([ax.here, ay.here, az.here]).astype(jnp.int32)
    tokens, width = block_input.shape
    rows = in_weight.shape[0]
    hidden = gate_weight.shape[1] // 4
    feats = width // 2
    wide_cols = 3 * feats
    lower = nz // 2
    z_back = (0,) + az.steps
    first_back, second_back = z_back[:lower], z_back[lower:]

    small = jnp.concatenate(
        [norm_gain[:, None], ffn_gain[:, None], conv_weight, jnp.zeros((rows, 123), F32)], 1
    ).astype(BF)
    in_sets = in_weight.astype(BF).reshape(rows, 3 * nx, 2, feats // nx)

    def in_part(which):
        return jnp.concatenate([pick(in_sets, which, 2).reshape(rows, wide_cols), small], 1)

    in_mine, in_got = in_part(core), ac.shift(in_part(1 - core))
    starts_core = ac.shift(seq_starts)

    def split_hidden(weight):
        cut = weight.astype(BF).reshape(rows, nx, 2, nz, 2, hidden // (nx * nz))
        return jnp.transpose(cut, (2, 4, 0, 1, 3, 5)).reshape(2, 2, rows, hidden)

    in_mine, in_got, gate_weight, up_weight = fence(in_mine, in_got, gate_weight, up_weight)
    out_low = out_weight.astype(BF).reshape(rows, 2, feats).transpose(1, 0, 2)
    mix = jnp.concatenate([ordered(in_mine, in_got, core, 0), out_low], 2)
    mix_z = {by: az.shift(mix, by) for by in first_back[1:]}
    gate_up = jnp.concatenate([split_hidden(gate_weight), split_hidden(up_weight)], 3)
    pair_mine = pick(gate_up, core, 0)
    pair_got = ac.shift(pick(gate_up, 1 - core, 0))

    pair_mine, pair_got, mix, mix_z, cotangent, down_low = fence(
        pair_mine, pair_got, mix, mix_z, cotangent, down_weight.astype(BF)
    )
    first = jnp.stack([mix] + [mix_z[by] for by in first_back[1:]])
    first_x = [ax.shift(first, by) for by in ax.steps]
    second = [az.shift(mix, by) for by in second_back]
    pair = ordered(pair_mine, pair_got, core, 0)
    quad_mine, quad_got = pick(pair, y_here, 1), ay.shift(pick(pair, 1 - y_here, 1))
    dy_low, dy_high = cotangent[: tokens // 2], cotangent[tokens // 2 :]
    quad = ordered(quad_mine, quad_got, y_here, 1)
    second, first, first_x, quad, down_low = fence(second, first, first_x, quad, down_low)
    gathered = lax.all_gather(quad.reshape(4 * rows, 2 * hidden), ("x", "z"), axis=0, tiled=True)
    second = jnp.stack(second)
    second_y = ay.shift(second)

    second_y, second, first, first_x, block_input, cotangent, down_low = fence(
        second_y, second, first, first_x, block_input, cotangent, down_low
    )
    ffn_down = lax.all_gather(down_low, ("x", "z"), axis=0, tiled=True)
    second_pair = jnp.stack([second, second_y])
    second_x = [ax.shift(second_pair, by) for by in ax.steps]
    first_y = ay.shift(jnp.stack([first] + first_x))
    x_core = ac.shift(block_input)
    dy_core = ac.shift(cotangent)
    inputs = jnp.concatenate([block_input, x_core], 0).astype(F32)
    scale_mix = lax.rsqrt(jnp.mean(inputs * inputs, axis=1, keepdims=True) + EPS)

    first_y, second_x, second_pair, first, first_x, scale_mix, dy_core, dy_low = fence(
        first_y, second_x, second_pair, first, first_x, scale_mix, dy_core, dy_low
    )
    dy_low_y = ay.shift(dy_low)
    pieces = [(0, 0, first_back, first, ())]
    pieces += [(0, dy, second_back, second_pair, (dy,)) for dy in range(2)]
    pieces += [(dx, 0, first_back, a, ()) for dx, a in zip(ax.steps, first_x, strict=True)]
    pieces += [(dx, 1, first_back, first_y, (n,)) for n, dx in enumerate((0,) + ax.steps)]
    for dx, a in zip(ax.steps, second_x, strict=True):
        pieces += [(dx, dy, second_back, a, (dy,)) for dy in range(2)]
    mix_in, tiny, mix_out = place_mix(pieces, here, ax, ay, az, wide_cols, width)
    tiny = tiny[:, :8].astype(F32)
    gain_mix, gain_ffn = tiny[:, 0], tiny[:, 1]
    taps = pick(tiny[:, 2:5].reshape(nx, 2, feats // nx, 3), core, 1).reshape(feats, 3)

    own_inputs = block_input.astype(F32)
    starts = jnp.concatenate([seq_starts, starts_core], 0)
    normed_mix = (inputs * scale_mix * gain_mix[None, :]).astype(BF)
    projected = times(normed_mix, mix_in)
    projected, dy_low_y = fence(projected, dy_low_y)
    dy_low_far = ac.shift(dy_low_y)

    b_branch = projected[:, :feats]
    c_branch = projected[:, feats : 2 * feats]
    x_branch = projected[:, 2 * feats :]
    product = (b_branch * x_branch).reshape(2, tokens, feats)
    earlier = passed_along(product[:, tokens - 2 :], 1)
    position = lax.axis_index(("z", "y")) * tokens + jnp.arange(tokens + 2, dtype=jnp.int32)

    def offsets(at):
        reached = starts[:, None, :] <= at[None, :, None]
        return at[None, :] - jnp.max(jnp.where(reached, starts[:, None, :], 0), axis=2)

    own_offset = offsets(position[:tokens])
    next_offset = offsets(position)
    padded = jnp.concatenate([earlier, product], 1)
    mixed = jnp.zeros((2, tokens, feats), F32)
    for lag in range(3):
        valid = (own_offset >= lag).astype(F32)[:, :, None]
        mixed = mixed + valid * taps[:, 2 - lag] * padded[:, 2 - lag : 2 - lag + tokens]
    mixed = mixed.reshape(2 * tokens, feats)
    gated = (c_branch * mixed).astype(BF)
    mixer_keep = times(gated[:tokens], mix_out)
    mixer_got = ac.shift(times(gated[tokens:], mix_out))

    mixer_got, mixer_keep = fence(mixer_got, mixer_keep)
    h = own_inputs + (mixer_keep + mixer_got)
    scale_ffn = lax.rsqrt(jnp.mean(h * h, axis=1, keepdims=True) + EPS)
    normed_own = (h * scale_ffn * gain_ffn[None, :]).astype(BF)
    normed_core = ac.shift(normed_own)
    gathered = gathered.reshape(nx, nz, 2, 2 * rows, 2 * hidden).transpose(0, 2, 1, 3, 4)
    gate_up = gathered.reshape(width, 2 * hidden)

    normed_core, normed_own, h, scale_ffn, gate_up = fence(
        normed_core, normed_own, h, scale_ffn, gate_up
    )
    normed_y = ay.shift(normed_own)
    near = jnp.concatenate([normed_own, normed_core], 0)
    dy_near = jnp.concatenate([cotangent, dy_core], 0)
    near_ev, near_s = ffn_forward(near, gate_up, tokens // 2)
    tile = 384 if hidden % 384 == 0 else hidden
    spec = pl.BlockSpec((tile, width), lambda i: (i, 0))
    near_down = weight_grad([near_s], [dy_near], tile, spec, (hidden, width), F32)

    normed_y, near_ev, near_s, dy_high, near_down = fence(
        normed_y, near_ev, near_s, dy_high, near_down
    )
    dy_high_y = ay.shift(dy_high)
    far = jnp.concatenate([normed_y, ac.shift(normed_y)], 0)
    far_ev, far_s = ffn_forward(far, gate_up, tokens // 2)

    far_s, far_ev, ffn_down, dy_high_y = fence(far_s, far_ev, ffn_down, dy_high_y)
    dy_far = jnp.concatenate([dy_low_y, dy_high_y, dy_low_far, ac.shift(dy_high_y)], 0)
    grad_down = weight_grad([far_s], [dy_far], tile, spec, (hidden, width), BF, [near_down])
    far_ev, far_s, grad_down = fence(far_ev, far_s, grad_down)
    part_down = lax.psum_scatter(grad_down, ("x", "z"), scatter_dimension=0, tiled=True)

    far_dev, far_keep, far_send = ffn_back(dy_far, far_ev, ffn_down, gate_up, tokens // 2)
    far_keep, far_send, far_s, near_ev, dy_near = fence(
        far_keep, far_send, far_s, near_ev, dy_near
    )
    far_got = ac.shift(far_send)
    far_got, far_keep, near_ev, far_s = fence(far_got, far_keep, near_ev, far_s)

    normed_y_got = ay.shift((far_keep + far_got).astype(BF))
    near_dev, near_keep, near_send = ffn_back(dy_near, near_ev, ffn_down, gate_up, tokens // 2)
    grad_gate_up = gate_up_grad([near, far], [near_dev, far_dev], nx, nz, rows)
    normed_y_got, near_keep, near_send, grad_gate_up = fence(
        normed_y_got, near_keep, near_send, grad_gate_up
    )

    near_got = ac.shift(near_send)
    quad = lax.psum_scatter(grad_gate_up, ("x", "z"), scatter_dimension=0, tiled=True)
    near_got, near_keep, far_s = fence(near_got, near_keep, far_s)
    far_fed, far_fed_send = ffn_out(far_s, ffn_down, tokens // 2)
    grad_normed = near_keep + near_got + normed_y_got.astype(F32)
    grad_gain_ffn = jnp.sum(grad_normed * h * scale_ffn, axis=0)
    weighted = grad_normed * gain_ffn[None, :]
    grad_hidden = (
        cotangent.astype(F32)
        + scale_ffn * weighted
        - h * scale_ffn**3 * jnp.mean(weighted * h, axis=1, keepdims=True)
    )
    hidden_own = grad_hidden.astype(BF)
    hidden_got = ac.shift(hidden_own)

    hidden_got, hidden_own, grad_hidden, far_fed, far_fed_send = fence(
        hidden_got, hidden_own, grad_hidden, far_fed, far_fed_send
    )
    far_fed_got = ac.shift(far_fed_send)
    hidden_low = jnp.concatenate([hidden_own, hidden_got], 0)
    grad_gated = contract_cols(hidden_low, mix_out)
    grad_c = grad_gated * mixed
    grad_mixed = (grad_gated * c_branch).reshape(2, tokens, feats)
    later = passed_along(grad_mixed[:, :2], -1)
    back_out = contract_rows(gated, hidden_low).astype(BF)

    trailing = jnp.concatenate([grad_mixed, later], 1)
    grad_product = jnp.zeros((2, tokens, feats), F32)
    tap_grads = []
    for lag in range(3):
        ahead = (next_offset[:, lag : lag + tokens] >= lag).astype(F32)[:, :, None]
        grad_product = grad_product + ahead * taps[:, 2 - lag] * trailing[:, lag : lag + tokens]
    for column in range(3):
        valid = (own_offset >= 2 - column).astype(F32)[:, :, None]
        tap_grads.append(
            jnp.sum(valid * grad_mixed * padded[:, column : column + tokens], axis=(0, 1))
        )
    grad_product = grad_product.reshape(2 * tokens, feats)
    grad_projected = jnp.concatenate(
        [grad_product * x_branch, grad_c, grad_product * b_branch], 1
    ).astype(BF)

    back_in = contract_rows(normed_mix, grad_projected).astype(BF)
    back_mix = jnp.concatenate(
        [
            back_in.reshape(nx, 2, nz, 2, rows, wide_cols),
            back_out.reshape(nx, nz, 2, rows, 2, feats).transpose(0, 4, 1, 2, 3, 5),
        ],
        5,
    )
    back_mix, grad_projected, near_s, far_fed_got = fence(
        back_mix, grad_projected, near_s, far_fed_got
    )
    first_own, first_got = sent(back_mix[:, :, :lower], ay, 3)
    second_own, second_got = sent(back_mix[:, :, lower:], ax, 0)
    mix_got = ac.shift(contract_cols(grad_projected[tokens:], mix_in))
    mix_keep = contract_cols(grad_projected[:tokens], mix_in)
    near_fed, near_fed_send = ffn_out(near_s, ffn_down, tokens // 2)
    near_fed_got = ac.shift(near_fed_send)
    grad_normed_mix = mix_keep + mix_got
    own_scale = scale_mix[:tokens]
    grad_gain_mix = jnp.sum(grad_normed_mix * own_inputs * own_scale, axis=0)
    weighted_mix = grad_normed_mix * gain_mix[None, :]
    grad_inputs = (
        grad_hidden
        + own_scale * weighted_mix
        - own_inputs * own_scale**3 * jnp.mean(weighted_mix * own_inputs, axis=1, keepdims=True)
    ).astype(BF)
    tap_rows = jnp.stack(tap_grads).reshape(3, nx, 1, feats // nx)
    on_core = (jnp.arange(2) == core).astype(F32)[None, None, :, None]
    tap_rows = (tap_rows * on_core).reshape(3, width)
    terms = jnp.concatenate([grad_gain_mix[None], grad_gain_ffn[None], tap_rows], 0)
    terms = terms + ac.shift(terms)

    first_got, first_own, second_got, second_own, grad_inputs, near_fed_got, terms = fence(
        first_got, first_own, second_got, second_own, grad_inputs, near_fed_got, terms
    )
    first_own, first_got = sent(summed(first_own, first_got).astype(BF), ax, 0)
    second_own, second_got = sent(summed(second_own, second_got).astype(BF), ay, 2)
    terms = summed(terms, [az.shift(terms, by) for by in az.steps])

    first_got, first_own, second_got, second_own, terms = fence(
        first_got, first_own, second_got, second_own, terms
    )
    own_z = jnp.concatenate(
        [summed(first_own, first_got).astype(BF), summed(second_own, second_got).astype(BF)], 1
    )
    mix_own, mix_parts = sent(own_z, az, 1)
    terms = summed(terms, [ax.shift(terms, by) for by in ax.steps])
    terms = terms + ay.shift(terms)
    fed_y = ay.shift((far_fed + far_fed_got).astype(BF))
    mix_parts, mix_own, terms, fed_y, quad = fence(mix_parts, mix_own, terms, fed_y, quad)

    quad = quad.reshape(2, 2, rows, 2 * hidden)
    quad_mine, quad_got = sent(quad, ay, 1)
    block_output = (h + (near_fed + near_fed_got + fed_y.astype(F32))).astype(BF)
    mix_sum = summed(mix_own, mix_parts)
    part_out = mix_sum[..., wide_cols:].transpose(1, 0, 2).reshape(rows, width)
    in_mine, in_got = sent(mix_sum[..., :wide_cols], ac, 0)
    cut = (rows, 3 * nx, feats // nx)
    part_in = ordered(in_mine.reshape(cut), in_got[0].reshape(cut), core, 2)
    pair = ordered(quad_mine, quad_got[0], y_here, 1)
    pair_mine, pair_got = sent(pair, ac, 0)
    quads = ordered(pair_mine, pair_got[0], core, 0).astype(F32)

    def join_hidden(sets):
        cut = sets.reshape(2, 2, rows, nx, nz, hidden // (nx * nz))
        return jnp.transpose(cut, (2, 3, 0, 4, 1, 5)).reshape(rows, 4 * hidden)

    part_gate, part_rise = join_hidden(quads[..., :hidden]), join_hidden(quads[..., hidden:])
    own_terms = lax.dynamic_slice_in_dim(terms, lax.axis_index(AXES) * rows, rows, 1)
    return (
        block_output,
        grad_inputs,
        part_in.reshape(rows, 3 * width),
        part_out,
        part_gate,
        part_rise,
        part_down.astype(F32),
        own_terms[0],
        own_terms[1],
        own_terms[2:].T,
    )


def solution(mesh):
    nd, nf = mesh.shape["dp"], mesh.shape["fsdp"]
    rows, line = P(AXES, None), P(AXES)
    return jax.shard_map(
        per_device,
        mesh=Mesh(mesh.devices.reshape(nd // 2, 2, nf // 2, 2), AXES),
        in_specs=(rows,) * 6 + (line, line, rows, P(("x", "core"), None), rows),
        out_specs=(rows,) * 7 + (line, line, rows),
        check_vma=False,
    )
```

time: 1200 us -> 454 us (0.38)
  Pallas kernels: 574 us -> 71.1 us
  starting transfers between devices: 141 us -> 45.8 us
  matrix products: 106 us -> 24.8 us
  waiting for transfers between devices: 248 us -> 180 us
  other arithmetic: 83.5 us -> 45.2 us
  local copies, waits for them, and re-layouts: 33.9 us -> 63.8 us
  between operations: 2.91 us -> 15.7 us
    pallas_call x5 -> x10, Pallas kernels: 574 us -> 71.1 us  [the longest x2 24.8 us: ffn_back(): pl.pallas_call(functools.partial(back_body, half), grid=(count // tile,),...]
    ppermute x89 -> x47, starting transfers between devices: 141 us -> 45.5 us  [the longest x45 40.3 us: shift(): lax.ppermute(value, self.name, [(i, (i + by) % self.size) for i in range(...]
    ppermute x89 -> x47, waiting for transfers between devices: 248 us -> 164 us  [the longest x45 163 us: shift(): lax.ppermute(value, self.name, [(i, (i + by) % self.size) for i in range(...]
    dot_general x5 -> x3, matrix products: 42.7 us -> 8.41 us  [times(): return jnp.dot(left, right, preferred_element_type=F32)]
    another operation x35 -> x13, other arithmetic: 39.2 us -> 9.62 us  [the longest x26 31.3 us: spread(): jnp.stack([buffer] + [axis.shift(buffer, by) for by in range(1, axis.size)])]
    unnamed x173 -> x163, local copies, waits for them, and re-layouts: 12.2 us -> 37.5 us
    dot_general x5 -> x3, matrix products: 34.2 us -> 10.4 us  [contract_cols(): lax.dot_general(left, right, (((1,), (1,)), ((), ())), preferred_element_...]
    dot_general x5 -> x2, matrix products: 28.7 us -> 5.97 us  [contract_rows(): lax.dot_general(left, right, (((0,), (0,)), ((), ())), preferred_element_...]
  transfers between devices with their start and end apart: 89 -> 51, of which waited for: 32 -> 29; matrix products, arithmetic and copies ran while one was open for 14% -> 18% of each run, Pallas kernels for 48% -> 12%
where the time goes in v2:
time: 454 us; the launch traced here: 446 us
  waiting for transfers between devices  180 us (40%)
  Pallas kernels  71.1 us (16%)
  local copies, waits for them, and re-layouts  63.8 us (14%)
  starting transfers between devices  45.8 us (10%)
  other arithmetic  45.2 us (10%)
  matrix products  24.8 us (5%)
  between operations  15.7 us (3%)
    ppermute x45, waiting for transfers between devices, shift(): lax.ppermute(value, self.name, [(i, (i + by) % self.size) for i in range(...  163 us
    ppermute x45, starting transfers between devices, shift(): lax.ppermute(value, self.name, [(i, (i + by) % self.size) for i in range(...  40.3 us
    unnamed x163, local copies, waits for them, and re-layouts  37.5 us
    pallas_call x2, Pallas kernels, ffn_back(): pl.pallas_call(functools.partial(back_body, half), grid=(count // tile,),...  24.8 us
    pallas_call x3, Pallas kernels, weight_grad(): pl.pallas_call(functools.partial(grad_body, len(lefts)), grid=(rows // ti...  20.5 us
    pallas_call x2, Pallas kernels, ffn_forward(): pl.pallas_call(forward_body, grid=(count // tile,), in_specs=[tiles(tile,...  14.5 us
    all_gather x1, waiting for transfers between devices, per_device(): ffn_down = lax.all_gather(down_low, ('x', 'z'), axis=0, tiled=True)  10.9 us
    dot_general x3, matrix products, contract_cols(): lax.dot_general(left, right, (((1,), (1,)), ((), ())), preferred_element_...  10.4 us
  transfers between devices with their start and end apart: 51, of which 29 were waited for; matrix products, arithmetic and copies ran while one was open for 18% of the time, Pallas kernels for 12%

profile of v2, /device:TPU:0, one launch (start us, length us, event | category | flops | bytes accessed | tf_op | source)
XLA Modules:
  0.0 446.0 jit_solution(12512825617547478933)
XLA Ops:
  17.4 2.8 collective-permute-start.2
  20.9 8.4 %collective-permute-done.2 = bf16[2,32,2176]{2,1,0:T(8,128)(2,1)S(1)} collective-permute-done((bf16[2,32,2176]{2,1,0:T(8,128)(2,1)S(1)}, bf16[2,32,2176]{2,1,0:T(8,128)(2,1)S(1)}, u32[]{:S(2)}, u32[]{:S(2)}) %collective-permute-start.2) | collective-permute-done | bytes 278560 | tf_op jit(solution)/shard_map/ppermute | solution.py:25
  34.7 4.7 %collective-permute-done.6 = bf16[2,32,2304]{2,1,0:T(8,128)(2,1)S(1)} collective-permute-done((bf16[2,32,2304]{2,1,0:T(8,128)(2,1)S(1)}, bf16[2,32,2304]{2,1,0:T(8,128)(2,1)S(1)}, u32[]{:S(2)}, u32[]{:S(2)}) %collective-permute-start.6) | collective-permute-done | bytes 294944 | tf_op jit(solution)/shard_map/ppermute | solution.py:25
  40.4 3.2 collective-permute-done.4
  43.9 2.6 collective-permute-done.5.refs_2_
  48.2 12.0 %collective-permute-done.7 = bf16[2,2,32,2176]{3,2,1,0:T(8,128)(2,1)} collective-permute-done((bf16[2,2,32,2176]{3,2,1,0:T(8,128)(2,1)S(1)}, bf16[2,2,32,2176]{3,2,1,0:T(8,128)(2,1)}, u32[]{:S(2)}, u32[]{:S(2)}) %collective-permute-start.7) | collective-permute-done | bytes 557088 | tf_op jit(solution)/shard_map/ppermute | solution.py:25
  67.4 20.0 %collective-permute-done.9.refs_3_ = bf16[2,2,2,32,2176]{4,3,2,1,0:T(8,128)(2,1)S(1)} collective-permute-done((bf16[2,2,2,32,2176]{4,3,2,1,0:T(8,128)(2,1)S(1)}, bf16[2,2,2,32,2176]{4,3,2,1,0:T(8,128)(2,1)S(1)}, u32[]{:S(2)}, u32[]{:S(2)}) %collective-permute-start.9) | collective-permute-done | bytes 1114144 | tf_op jit(solution)/shard_map/ppermute | solution.py:25
  87.4 7.4 %collective-permute-done.10.refs_4_ = bf16[2,2,2,32,2176]{4,3,2,1,0:T(8,128)(2,1)S(1)} collective-permute-done((bf16[2,2,2,32,2176]{4,3,2,1,0:T(8,128)(2,1)S(1)}, bf16[2,2,2,32,2176]{4,3,2,1,0:T(8,128)(2,1)S(1)}, u32[]{:S(2)}, u32[]{:S(2)}) %collective-permute-start.10) | collective-permute-done | bytes 1114144 | tf_op jit(solution)/shard_map/ppermute | solution.py:25
  94.7 4.1 shard_map.186
  100.6 5.7 %fusion.52 = f32[1024,1536]{1,0:T(8,128)S(1)} fusion(bf16[1024,1536]{1,0:T(8,128)(2,1)} %bitcast.272, f32[1024]{0:T(1024)S(1)} %bitcast.263, f32[1024]{0:T(1024)S(1)} %add_rsqrt_fusion, bf16[512,1024]{1,0:T(8,128)(2,1)} %copy-done.54, bf16[512,1024]{1,0:T(8,128)(2,1)S(1)} %copy-done.42), kind=kOutput, calls=%fused_computation.194 | convolution fusion | flops 3228565504 | bytes 11542528 | tf_op jit(solution)/shard_map/dot_general | solution.py:54
  106.3 6.3 %collective-permute-done.12 = bf16[256,1024]{1,0:T(8,128)(2,1)S(1)} collective-permute-done((bf16[256,1024]{1,0:T(8,128)(2,1)}, bf16[256,1024]{1,0:T(8,128)(2,1)S(1)}, u32[]{:S(2)}, u32[]{:S(2)}) %collective-permute-start.12) | collective-permute-done | bytes 524320 | tf_op jit(solution)/shard_map/ppermute | solution.py:25
  113.1 3.8 collective-permute-start.14
  123.0 3.7 collective-permute-done.15
  130.5 4.5 %all-gather.3.cloned.1.call-done = bf16[1024,2304]{1,0:T(8,128)(2,1)} async-done(((bf16[128,2304]{1,0:T(8,128)(2,1)}), bf16[1024,2304]{1,0:T(8,128)(2,1)}) %all-gather.3.cloned.1.call-update) | async-done | bytes 4718608 | tf_op jit(solution)/shard_map/all_gather | solution.py:350
  135.1 2.8 copy.104
  138.0 2.6 collective-permute-start.17
  140.9 7.3 %shard_map.187 = (bf16[1024,2304]{1,0:T(8,128)(2,1)S(1)}, bf16[1024,1152]{1,0:T(8,128)(2,1)S(1)}) custom-call(bf16[1024,1024]{1,0:T(8,128)(2,1)S(1)} %constant_dynamic-update-slice_fusion.2.x_ref.refs_0_, bf16[1024,2304]{1,0:T(8,128)(2,1)S(1)} %bitcast.201), custom_call_target="tpu_custom_call" | custom-call | bytes 65536 | tf_op jit(solution)/shard_map/pallas_call | solution.py:177
  150.3 3.3 shard_map.188.refs_2_
  155.8 8.5 %collective-permute-done.17 = bf16[512,1024]{1,0:T(8,128)(2,1)S(1)} collective-permute-done((bf16[512,1024]{1,0:T(8,128)(2,1)S(1)}, bf16[512,1024]{1,0:T(8,128)(2,1)S(1)}, u32[]{:S(2)}, u32[]{:S(2)}) %collective-permute-start.17) | collective-permute-done | bytes 1048608 | tf_op jit(solution)/shard_map/ppermute | solution.py:25
  167.0 7.3 %shard_map.189 = (bf16[1024,2304]{1,0:T(8,128)(2,1)S(1)}, bf16[1024,1152]{1,0:T(8,128)(2,1)S(1)}) custom-call(bf16[1024,1024]{1,0:T(8,128)(2,1)S(1)} %constant_dynamic-update-slice_fusion.6.x_ref.refs_1_, bf16[1024,2304]{1,0:T(8,128)(2,1)S(1)} %bitcast.202), custom_call_target="tpu_custom_call" | custom-call | bytes 65536 | tf_op jit(solution)/shard_map/pallas_call | solution.py:177
  179.2 10.9 %all-gather.5.cloned.1.call-done.down_ref = bf16[1152,1024]{1,0:T(8,128)(2,1)} async-done(((bf16[144,1024]{1,0:T(8,128)(2,1)}), bf16[1152,1024]{1,0:T(8,128)(2,1)}) %all-gather.5.cloned.1.call-update) | async-done | bytes 2359312 | tf_op jit(solution)/shard_map/all_gather | solution.py:357
  192.1 2.3 copy-done.4
  194.4 3.3 shard_map.190
  202.1 12.4 %shard_map.191 = (bf16[1024,2304]{1,0:T(8,128)(2,1)S(1)}, f32[512,1024]{1,0:T(8,128)S(1)}, f32[512,1024]{1,0:T(8,128)S(1)}) custom-call(bf16[1024,1024]{1,0:T(8,128)(2,1)S(1)} %copy-done.12, bf16[1024,2304]{1,0:T(8,128)(2,1)} %copy-done.21, bf16[1152,1024]{1,0:T(8,128)(2,1)S(1)} %copy-done.1, bf16[1024,2304]{1,0:T(8,128)(2,1)} %bitcast.203), custom_call_target="tpu_custom_call" | custom-call | bytes 65536 | tf_op jit(solution)/shard_map/pallas_call | solution.py:225
  214.7 4.0 collective-permute-done.22
  223.3 12.5 %shard_map.192 = (bf16[1024,2304]{1,0:T(8,128)(2,1)S(1)}, f32[512,1024]{1,0:T(8,128)S(1)}, f32[512,1024]{1,0:T(8,128)S(1)}) custom-call(bf16[1024,1024]{1,0:T(8,128)(2,1)S(1)} %copy-done.10, bf16[1024,2304]{1,0:T(8,128)(2,1)} %copy-done.20, bf16[1152,1024]{1,0:T(8,128)(2,1)S(1)} %copy-done.1, bf16[1024,2304]{1,0:T(8,128)(2,1)} %bitcast.204), custom_call_target="tpu_custom_call" | custom-call | bytes 65536 | tf_op jit(solution)/shard_map/pallas_call | solution.py:225
  238.5 13.9 %shard_map.193 = bf16[2,4,2,64,2304]{4,3,2,1,0:T(8,128)(2,1)S(1)} custom-call(bf16[1024,1024]{1,0:T(8,128)(2,1)S(1)} %copy-done.8, bf16[1024,1024]{1,0:T(8,128)(2,1)S(1)} %copy-done.6, bf16[1024,2304]{1,0:T(8,128)(2,1)S(1)} %get-tuple-element.192.refs_2_, bf16[1024,2304]{1,0:T(8,128)(2,1)} %copy-done.19), custom_call_target="tpu_custom_call" | custom-call | bytes 65536 | tf_op jit(solution)/shard_map/pallas_call | solution.py:267
  254.5 4.4 collective-permute-done.24
  258.9 3.6 multiply_reduce_fusion.3
  266.9 3.6 shard_map.194
  274.1 2.3 convolution_convert_fusion.1
  276.4 3.3 multiply_reduce_fusion.2
  287.9 4.2 fusion.6
  292.1 3.3 fusion.15
  297.0 3.7 convolution_convert_fusion
  300.7 2.8 pad_maximum_fusion
  303.5 3.1 fusion.19
  310.3 3.6 shard_map.195
  316.7 2.5 collective-permute-start.28
  319.2 3.9 fusion.13
  324.9 29.2 %collective-permute-done.29 = bf16[2,2,2,32,2048]{4,3,1,0,2:T(8,128)(2,1)S(1)} collective-permute-done((bf16[2,2,2,32,2048]{4,3,1,0,2:T(8,128)(2,1)S(1)}, bf16[2,2,2,32,2048]{4,3,1,0,2:T(8,128)(2,1)S(1)}, u32[]{:S(2)}, u32[]{:S(2)}) %collective-permute-start.29) | collective-permute-done | bytes 1048608 | tf_op jit(solution)/shard_map/ppermute | solution.py:25
  362.3 8.2 %collective-permute-done.33 = bf16[2,2,32,2048]{3,2,1,0:T(8,128)(2,1)S(1)} collective-permute-done((bf16[2,2,32,2048]{3,2,1,0:T(8,128)(2,1)S(1)}, bf16[2,2,32,2048]{3,2,1,0:T(8,128)(2,1)S(1)}, u32[]{:S(2)}, u32[]{:S(2)}) %collective-permute-start.33) | collective-permute-done | bytes 524320 | tf_op jit(solution)/shard_map/ppermute | solution.py:25
  370.6 3.0 collective-permute-done.34
  375.7 3.2 collective-permute-start.39
  386.4 8.1 %collective-permute-done.42 = f32[5,1024]{1,0:T(8,128)S(1)} collective-permute-done((f32[5,1024]{1,0:T(8,128)S(1)}, f32[5,1024]{1,0:T(8,128)S(1)}, u32[]{:S(2)}, u32[]{:S(2)}) %collective-permute-start.42) | collective-permute-done | bytes 20512 | tf_op jit(solution)/shard_map/ppermute | solution.py:25
  394.5 5.1 %collective-permute-done.39 = bf16[2,32,2048]{2,1,0:T(8,128)(2,1)} collective-permute-done((bf16[2,32,2048]{2,1,0:T(8,128)(2,1)}, bf16[2,32,2048]{2,1,0:T(8,128)(2,1)}, u32[]{:S(2)}, u32[]{:S(2)}) %collective-permute-start.39) | collective-permute-done | bytes 262176 | tf_op jit(solution)/shard_map/ppermute | solution.py:25
  399.5 16.9 %collective-permute-done.40 = bf16[2,32,2048]{2,1,0:T(8,128)(2,1)} collective-permute-done((bf16[2,32,2048]{2,1,0:T(8,128)(2,1)}, bf16[2,32,2048]{2,1,0:T(8,128)(2,1)}, u32[]{:S(2)}, u32[]{:S(2)}) %collective-permute-start.40) | collective-permute-done | bytes 262176 | tf_op jit(solution)/shard_map/ppermute | solution.py:25
  419.6 4.4 add_convert_fusion
  (373 shorter events, 127.7 us)
Async XLA Ops:
  7.2 127.9 %all-gather.3.cloned.1.call-start = ((), (), s32[]{:S(2)}) async-start(), calls=%async_computation.2 | async-start | bytes 5308416 | tf_op jit(solution)/shard_map/all_gather | solution.py:350
  16.9 12.5 %collective-permute-start.1 = (bf16[2,32,2304]{2,1,0:T(8,128)(2,1)S(1)}, bf16[2,32,2304]{2,1,0:T(8,128)(2,1)S(1)}, u32[]{:S(2)}, u32[]{:S(2)}) collective-permute-start(bf16[2,32,2304]{2,1,0:T(8,128)(2,1)S(1)} %get-tuple-element.278), channel_id=1, source_target_pairs={{0,8},{8,0},{1,9},{9,1},{2,10},{10,2},{3,11},{11,3},{4,12},{12,4},... | collective-permute-start | bytes 884744 | tf_op jit(solution)/shard_map/ppermute | solution.py:25
  17.4 12.0 %collective-permute-start.2 = (bf16[2,32,2176]{2,1,0:T(8,128)(2,1)S(1)}, bf16[2,32,2176]{2,1,0:T(8,128)(2,1)S(1)}, u32[]{:S(2)}, u32[]{:S(2)}) collective-permute-start(bf16[2,32,2176]{2,1,0:T(8,128)(2,1)S(1)} %pad_maximum_fusion.11), channel_id=1, source_target_pairs={{0,2},{2,4},{4,6},{6,0},{1,3},{3,5},{5,7},{7,1},{8,10},{10,12},{12... | collective-permute-start | bytes 835592 | tf_op jit(solution)/shard_map/ppermute | solution.py:25
  29.3 14.3 %collective-permute-start.4 = (bf16[2,32,2176]{2,1,0:T(8,128)(2,1)S(1)}, bf16[2,32,2176]{2,1,0:T(8,128)(2,1)S(1)}, u32[]{:S(2)}, u32[]{:S(2)}) collective-permute-start(bf16[2,32,2176]{2,1,0:T(8,128)(2,1)S(1)} %pad_maximum_fusion.11), channel_id=1, source_target_pairs={{0,4},{2,6},{4,0},{6,2},{1,5},{3,7},{5,1},{7,3},{8,12},{10,14},{12... | collective-permute-start | bytes 835592 | tf_op jit(solution)/shard_map/ppermute | solution.py:25
  30.1 13.8 %collective-permute-start.3 = (bf16[2,32,2176]{2,1,0:T(8,128)(2,1)S(1)}, bf16[2,32,2176]{2,1,0:T(8,128)(2,1)S(1)}, u32[]{:S(2)}, u32[]{:S(2)}) collective-permute-start(bf16[2,32,2176]{2,1,0:T(8,128)(2,1)S(1)} %pad_maximum_fusion.11), channel_id=1, source_target_pairs={{0,6},{2,0},{4,2},{6,4},{1,7},{3,1},{5,3},{7,5},{8,14},{10,8},{12,... | collective-permute-start | bytes 835592 | tf_op jit(solution)/shard_map/ppermute | solution.py:25
  31.5 8.0 %collective-permute-start.6 = (bf16[2,32,2304]{2,1,0:T(8,128)(2,1)S(1)}, bf16[2,32,2304]{2,1,0:T(8,128)(2,1)S(1)}, u32[]{:S(2)}, u32[]{:S(2)}) collective-permute-start(bf16[2,32,2304]{2,1,0:T(8,128)(2,1)S(1)} %fusion.35), channel_id=1, source_target_pairs={{0,1},{1,0},{2,3},{3,2},{4,5},{5,4},{6,7},{7,6},{8,9},{9,8},{10,11... | collective-permute-start | bytes 884744 | tf_op jit(solution)/shard_map/ppermute | solution.py:25
  33.2 13.3 %collective-permute-start.5 = (bf16[2,2,32,2176]{3,2,1,0:T(8,128)(2,1)S(1)}, bf16[2,2,32,2176]{3,2,1,0:T(8,128)(2,1)S(1)}, u32[]{:S(2)}, u32[]{:S(2)}) collective-permute-start(bf16[2,2,32,2176]{3,2,1,0:T(8,128)(2,1)S(1)} %pad_maximum_fusion.8.refs_0_), channel_id=1, source_target_pairs={{0,16},{16,0},{1,17},{17,1},{2,18},{18,2},{3,19},{19,3},{4,20},{20... | collective-permute-start | bytes 1671176 | tf_op jit(solution)/shard_map/ppermute | solution.py:25
  46.5 143.6 %all-gather.5.cloned.1.call-start = ((), (), s32[]{:S(2)}) async-start(), calls=%async_computation.3 | async-start | bytes 2654208 | tf_op jit(solution)/shard_map/all_gather | solution.py:357
  47.7 12.5 %collective-permute-start.7 = (bf16[2,2,32,2176]{3,2,1,0:T(8,128)(2,1)S(1)}, bf16[2,2,32,2176]{3,2,1,0:T(8,128)(2,1)}, u32[]{:S(2)}, u32[]{:S(2)}) collective-permute-start(bf16[2,2,32,2176]{3,2,1,0:T(8,128)(2,1)S(1)} %pad_maximum_fusion.9), channel_id=1, source_target_pairs={{0,1},{1,0},{2,3},{3,2},{4,5},{5,4},{6,7},{7,6},{8,9},{9,8},{10,11... | collective-permute-start | bytes 1671176 | tf_op jit(solution)/shard_map/ppermute | solution.py:25
  48.2 16.5 %collective-permute-start.13 = (s32[1,4]{1,0:T(1,128)S(1)}, s32[1,4]{1,0:T(1,128)S(1)}, u32[]{:S(2)}, u32[]{:S(2)}) collective-permute-start(s32[1,4]{1,0:T(1,128)S(1)} %copy-done.68), channel_id=1, source_target_pairs={{0,8},{8,0},{1,9},{9,1},{2,10},{10,2},{3,11},{11,3},{4,12},{12,4},... | collective-permute-start | bytes 56 | tf_op jit(solution)/shard_map/ppermute | solution.py:25
  60.2 5.7 %collective-permute-start.8 = (bf16[512,1024]{1,0:T(8,128)(2,1)S(1)}, bf16[512,1024]{1,0:T(8,128)(2,1)S(1)}, u32[]{:S(2)}, u32[]{:S(2)}) collective-permute-start(bf16[512,1024]{1,0:T(8,128)(2,1)S(1)} %copy-done.42), channel_id=1, source_target_pairs={{0,8},{8,0},{1,9},{9,1},{2,10},{10,2},{3,11},{11,3},{4,12},{12,4},... | collective-permute-start | bytes 3145736 | tf_op jit(solution)/shard_map/ppermute | solution.py:25
  60.3 27.0 %collective-permute-start.9 = (bf16[2,2,2,32,2176]{4,3,2,1,0:T(8,128)(2,1)S(1)}, bf16[2,2,2,32,2176]{4,3,2,1,0:T(8,128)(2,1)S(1)}, u32[]{:S(2)}, u32[]{:S(2)}) collective-permute-start(bf16[2,2,2,32,2176]{4,3,2,1,0:T(8,128)(2,1)S(1)} %pad_maximum_fusion.5), channel_id=1, source_target_pairs={{0,1},{1,0},{2,3},{3,2},{4,5},{5,4},{6,7},{7,6},{8,9},{9,8},{10,11... | collective-permute-start | bytes 3342344 | tf_op jit(solution)/shard_map/ppermute | solution.py:25
  63.1 31.7 %collective-permute-start.10 = (bf16[2,2,2,32,2176]{4,3,2,1,0:T(8,128)(2,1)S(1)}, bf16[2,2,2,32,2176]{4,3,2,1,0:T(8,128)(2,1)S(1)}, u32[]{:S(2)}, u32[]{:S(2)}) collective-permute-start(bf16[2,2,2,32,2176]{4,3,2,1,0:T(8,128)(2,1)S(1)} %pad_maximum_fusion.6.refs_1_), channel_id=1, source_target_pairs={{0,16},{16,0},{1,17},{17,1},{2,18},{18,2},{3,19},{19,3},{4,20},{20... | collective-permute-start | bytes 3342344 | tf_op jit(solution)/shard_map/ppermute | solution.py:25
  64.7 2.7 collective-permute-start.11
  99.0 13.6 %collective-permute-start.12 = (bf16[256,1024]{1,0:T(8,128)(2,1)}, bf16[256,1024]{1,0:T(8,128)(2,1)S(1)}, u32[]{:S(2)}, u32[]{:S(2)}) collective-permute-start(bf16[256,1024]{1,0:T(8,128)(2,1)} %get-tuple-element.152), channel_id=1, source_target_pairs={{0,1},{1,0},{2,3},{3,2},{4,5},{5,4},{6,7},{7,6},{8,9},{9,8},{10,11... | collective-permute-start | bytes 1572872 | tf_op jit(solution)/shard_map/ppermute | solution.py:25
  113.1 4.7 %collective-permute-start.14 = (f32[2,2,512]{2,1,0:T(2,128)S(1)}, f32[2,2,512]{2,1,0:T(2,128)S(1)}, u32[]{:S(2)}, u32[]{:S(2)}) collective-permute-start(f32[2,2,512]{2,1,0:T(2,128)S(1)} %slice.154), channel_id=1, source_target_pairs={{0,1},{1,2},{2,3},{3,4},{4,5},{5,6},{6,7},{8,9},{9,10},{10,11},{11... | collective-permute-start | bytes 24584 | tf_op jit(solution)/shard_map/ppermute | solution.py:34
  122.2 4.5 %collective-permute-start.15 = (f32[512,1024]{1,0:T(8,128)}, f32[512,1024]{1,0:T(8,128)}, u32[]{:S(2)}, u32[]{:S(2)}) collective-permute-start(f32[512,1024]{1,0:T(8,128)} %fusion.28), channel_id=1, source_target_pairs={{0,8},{8,0},{1,9},{9,1},{2,10},{10,2},{3,11},{11,3},{4,12},{12,4},... | collective-permute-start | bytes 6291464 | tf_op jit(solution)/shard_map/ppermute | solution.py:25
  122.2 262.3 %reduce-scatter.5.cloned.1.call-start = ((), (), s32[]{:S(2)}) async-start(), calls=%async_computation.5 | async-start | bytes 2654208 | tf_op jit(solution)/shard_map/reduce_scatter | solution.py:441
  130.3 7.6 %collective-permute-start.16 = (bf16[512,1024]{1,0:T(8,128)(2,1)S(1)}, bf16[512,1024]{1,0:T(8,128)(2,1)S(1)}, u32[]{:S(2)}, u32[]{:S(2)}) collective-permute-start(bf16[512,1024]{1,0:T(8,128)(2,1)S(1)} %multiply_convert_fusion), channel_id=1, source_target_pairs={{0,8},{8,0},{1,9},{9,1},{2,10},{10,2},{3,11},{11,3},{4,12},{12,4},... | collective-permute-start | bytes 3145736 | tf_op jit(solution)/shard_map/ppermute | solution.py:25
  138.0 26.3 %collective-permute-start.17 = (bf16[512,1024]{1,0:T(8,128)(2,1)S(1)}, bf16[512,1024]{1,0:T(8,128)(2,1)S(1)}, u32[]{:S(2)}, u32[]{:S(2)}) collective-permute-start(bf16[512,1024]{1,0:T(8,128)(2,1)S(1)} %multiply_convert_fusion), channel_id=1, source_target_pairs={{0,1},{1,0},{2,3},{3,2},{4,5},{5,4},{6,7},{7,6},{8,9},{9,8},{10,11... | collective-permute-start | bytes 3145736 | tf_op jit(solution)/shard_map/ppermute | solution.py:25
  164.3 2.7 collective-permute-start.18
  164.3 25.8 %collective-permute-start.19 = (bf16[256,1024]{1,0:T(8,128)(2,1)S(1)}, bf16[256,1024]{1,0:T(8,128)(2,1)S(1)}, u32[]{:S(2)}, u32[]{:S(2)}) collective-permute-start(bf16[256,1024]{1,0:T(8,128)(2,1)S(1)} %copy-done.64), channel_id=1, source_target_pairs={{0,1},{1,0},{2,3},{3,2},{4,5},{5,4},{6,7},{7,6},{8,9},{9,8},{10,11... | collective-permute-start | bytes 1572872 | tf_op jit(solution)/shard_map/ppermute | solution.py:25
  166.0 24.2 %collective-permute-start.20 = (bf16[256,1024]{1,0:T(8,128)(2,1)S(1)}, bf16[256,1024]{1,0:T(8,128)(2,1)S(1)}, u32[]{:S(2)}, u32[]{:S(2)}) collective-permute-start(bf16[256,1024]{1,0:T(8,128)(2,1)S(1)} %copy-done.63), channel_id=1, source_target_pairs={{0,8},{8,0},{1,9},{9,1},{2,10},{10,2},{3,11},{11,3},{4,12},{12,4},... | collective-permute-start | bytes 1572872 | tf_op jit(solution)/shard_map/ppermute | solution.py:25
  190.1 1.9 collective-permute-start.21
  214.5 4.2 collective-permute-start.22
  220.0 34.5 %collective-permute-start.23 = (bf16[512,1024]{1,0:T(8,128)(2,1)}, bf16[512,1024]{1,0:T(8,128)(2,1)}, u32[]{:S(2)}, u32[]{:S(2)}) collective-permute-start(bf16[512,1024]{1,0:T(8,128)(2,1)} %add_convert_fusion.4), channel_id=1, source_target_pairs={{0,1},{1,0},{2,3},{3,2},{4,5},{5,4},{6,7},{7,6},{8,9},{9,8},{10,11... | collective-permute-start | bytes 3145736 | tf_op jit(solution)/shard_map/ppermute | solution.py:25
  221.5 195.0 %reduce-scatter.3.cloned.1.call-start = ((), (), s32[]{:S(2)}) async-start(), calls=%async_computation.4 | async-start | bytes 5308416 | tf_op jit(solution)/shard_map/reduce_scatter | solution.py:458
  254.5 4.4 collective-permute-start.24
  264.8 5.7 %collective-permute-start.25 = (bf16[512,1024]{1,0:T(8,128)(2,1)}, bf16[512,1024]{1,0:T(8,128)(2,1)}, u32[]{:S(2)}, u32[]{:S(2)}) collective-permute-start(bf16[512,1024]{1,0:T(8,128)(2,1)} %get-tuple-element.203), channel_id=1, source_target_pairs={{0,8},{8,0},{1,9},{9,1},{2,10},{10,2},{3,11},{11,3},{4,12},{12,4},... | collective-permute-start | bytes 3145736 | tf_op jit(solution)/shard_map/ppermute | solution.py:25
  281.1 6.8 %collective-permute-start.26 = (f32[2,2,512]{2,1,0:T(2,128)S(1)}, f32[2,2,512]{2,1,0:T(2,128)S(1)}, u32[]{:S(2)}, u32[]{:S(2)}) collective-permute-start(f32[2,2,512]{2,1,0:T(2,128)S(1)} %slice.163), channel_id=1, source_target_pairs={{1,0},{2,1},{3,2},{4,3},{5,4},{6,5},{7,6},{9,8},{10,9},{11,10},{12... | collective-permute-start | bytes 24584 | tf_op jit(solution)/shard_map/ppermute | solution.py:34
  287.5 15.9 %collective-permute-start.27 = (f32[512,1024]{1,0:T(8,128)S(1)}, f32[512,1024]{1,0:T(8,128)S(1)}, u32[]{:S(2)}, u32[]{:S(2)}) collective-permute-start(f32[512,1024]{1,0:T(8,128)S(1)} %copy-done.28), channel_id=1, source_target_pairs={{0,8},{8,0},{1,9},{9,1},{2,10},{10,2},{3,11},{11,3},{4,12},{12,4},... | collective-permute-start | bytes 6291464 | tf_op jit(solution)/shard_map/ppermute | solution.py:25
  306.6 12.6 %collective-permute-start.30 = (f32[512,1024]{1,0:T(8,128)}, f32[512,1024]{1,0:T(8,128)}, u32[]{:S(2)}, u32[]{:S(2)}) collective-permute-start(f32[512,1024]{1,0:T(8,128)} %fusion.19), channel_id=1, source_target_pairs={{0,8},{8,0},{1,9},{9,1},{2,10},{10,2},{3,11},{11,3},{4,12},{12,4},... | collective-permute-start | bytes 6291464 | tf_op jit(solution)/shard_map/ppermute | solution.py:25
  313.9 40.2 %collective-permute-start.31 = (f32[512,1024]{1,0:T(8,128)S(1)}, f32[512,1024]{1,0:T(8,128)S(1)}, u32[]{:S(2)}, u32[]{:S(2)}) collective-permute-start(f32[512,1024]{1,0:T(8,128)S(1)} %get-tuple-element.212), channel_id=1, source_target_pairs={{0,8},{8,0},{1,9},{9,1},{2,10},{10,2},{3,11},{11,3},{4,12},{12,4},... | collective-permute-start | bytes 6291464 | tf_op jit(solution)/shard_map/ppermute | solution.py:25
  315.9 38.2 %collective-permute-start.29 = (bf16[2,2,2,32,2048]{4,3,1,0,2:T(8,128)(2,1)S(1)}, bf16[2,2,2,32,2048]{4,3,1,0,2:T(8,128)(2,1)S(1)}, u32[]{:S(2)}, u32[]{:S(2)}) collective-permute-start(bf16[2,2,2,32,2048]{4,3,1,0,2:T(8,128)(2,1)S(1)} %bitcast.230), channel_id=1, source_target_pairs={{0,16},{16,0},{1,17},{17,1},{2,18},{18,2},{3,19},{19,3},{4,20},{20... | collective-permute-start | bytes 3145736 | tf_op jit(solution)/shard_map/ppermute | solution.py:25
  316.7 37.4 %collective-permute-start.28 = (bf16[2,2,2,32,2048]{4,3,2,1,0:T(8,128)(2,1)S(1)}, bf16[2,2,2,32,2048]{4,3,2,1,0:T(8,128)(2,1)S(1)}, u32[]{:S(2)}, u32[]{:S(2)}) collective-permute-start(bf16[2,2,2,32,2048]{4,3,2,1,0:T(8,128)(2,1)S(1)} %get-tuple-element.257), channel_id=1, source_target_pairs={{0,1},{1,0},{2,3},{3,2},{4,5},{5,4},{6,7},{7,6},{8,9},{9,8},{10,11... | collective-permute-start | bytes 3145736 | tf_op jit(solution)/shard_map/ppermute | solution.py:25
  354.1 6.5 %collective-permute-start.37 = (f32[5,1024]{1,0:T(8,128)S(1)}, f32[5,1024]{1,0:T(8,128)S(1)}, u32[]{:S(2)}, u32[]{:S(2)}) collective-permute-start(f32[5,1024]{1,0:T(8,128)S(1)} %fusion.50), channel_id=1, source_target_pairs={{0,4},{2,6},{4,0},{6,2},{1,5},{3,7},{5,1},{7,3},{8,12},{10,14},{12... | collective-permute-start | bytes 61448 | tf_op jit(solution)/shard_map/ppermute | solution.py:25
  354.7 7.4 %collective-permute-start.36 = (f32[5,1024]{1,0:T(8,128)S(1)}, f32[5,1024]{1,0:T(8,128)S(1)}, u32[]{:S(2)}, u32[]{:S(2)}) collective-permute-start(f32[5,1024]{1,0:T(8,128)S(1)} %fusion.50), channel_id=1, source_target_pairs={{0,6},{2,0},{4,2},{6,4},{1,7},{3,1},{5,3},{7,5},{8,14},{10,8},{12,... | collective-permute-start | bytes 61448 | tf_op jit(solution)/shard_map/ppermute | solution.py:25
  356.4 5.9 %collective-permute-start.35 = (f32[5,1024]{1,0:T(8,128)S(1)}, f32[5,1024]{1,0:T(8,128)S(1)}, u32[]{:S(2)}, u32[]{:S(2)}) collective-permute-start(f32[5,1024]{1,0:T(8,128)S(1)} %fusion.50), channel_id=1, source_target_pairs={{0,2},{2,4},{4,6},{6,0},{1,3},{3,5},{5,7},{7,1},{8,10},{10,12},{12... | collective-permute-start | bytes 61448 | tf_op jit(solution)/shard_map/ppermute | solution.py:25
  357.5 13.1 %collective-permute-start.33 = (bf16[2,2,32,2048]{3,2,1,0:T(8,128)(2,1)S(1)}, bf16[2,2,32,2048]{3,2,1,0:T(8,128)(2,1)S(1)}, u32[]{:S(2)}, u32[]{:S(2)}) collective-permute-start(bf16[2,2,32,2048]{3,2,1,0:T(8,128)(2,1)S(1)} %get-tuple-element.267), channel_id=1, source_target_pairs={{0,16},{16,0},{1,17},{17,1},{2,18},{18,2},{3,19},{19,3},{4,20},{20... | collective-permute-start | bytes 1572872 | tf_op jit(solution)/shard_map/ppermute | solution.py:25
  358.6 14.9 %collective-permute-start.34 = (bf16[2,2,32,2048]{3,2,1,0:T(8,128)(2,1)S(1)}, bf16[2,2,32,2048]{3,2,1,0:T(8,128)(2,1)S(1)}, u32[]{:S(2)}, u32[]{:S(2)}) collective-permute-start(bf16[2,2,32,2048]{3,2,1,0:T(8,128)(2,1)S(1)} %get-tuple-element.265), channel_id=1, source_target_pairs={{0,1},{1,0},{2,3},{3,2},{4,5},{5,4},{6,7},{7,6},{8,9},{9,8},{10,11... | collective-permute-start | bytes 1572872 | tf_op jit(solution)/shard_map/ppermute | solution.py:25
  360.6 33.8 %collective-permute-start.43 = (bf16[512,1024]{1,0:T(8,128)(2,1)S(1)}, bf16[512,1024]{1,0:T(8,128)(2,1)}, u32[]{:S(2)}, u32[]{:S(2)}) collective-permute-start(bf16[512,1024]{1,0:T(8,128)(2,1)S(1)} %add_convert_fusion.1), channel_id=1, source_target_pairs={{0,1},{1,0},{2,3},{3,2},{4,5},{5,4},{6,7},{7,6},{8,9},{9,8},{10,11... | collective-permute-start | bytes 3145736 | tf_op jit(solution)/shard_map/ppermute | solution.py:25
  375.1 19.4 %collective-permute-start.38 = (bf16[2,32,2048]{2,1,0:T(8,128)(2,1)}, bf16[2,32,2048]{2,1,0:T(8,128)(2,1)}, u32[]{:S(2)}, u32[]{:S(2)}) collective-permute-start(bf16[2,32,2048]{2,1,0:T(8,128)(2,1)} %get-tuple-element.261), channel_id=1, source_target_pairs={{0,2},{2,4},{4,6},{6,0},{1,3},{3,5},{5,7},{7,1},{8,10},{10,12},{12... | collective-permute-start | bytes 786440 | tf_op jit(solution)/shard_map/ppermute | solution.py:25
  375.7 23.8 %collective-permute-start.39 = (bf16[2,32,2048]{2,1,0:T(8,128)(2,1)}, bf16[2,32,2048]{2,1,0:T(8,128)(2,1)}, u32[]{:S(2)}, u32[]{:S(2)}) collective-permute-start(bf16[2,32,2048]{2,1,0:T(8,128)(2,1)} %get-tuple-element.262), channel_id=1, source_target_pairs={{0,6},{2,0},{4,2},{6,4},{1,7},{3,1},{5,3},{7,5},{8,14},{10,8},{12,... | collective-permute-start | bytes 786440 | tf_op jit(solution)/shard_map/ppermute | solution.py:25
  378.9 37.6 %collective-permute-start.40 = (bf16[2,32,2048]{2,1,0:T(8,128)(2,1)}, bf16[2,32,2048]{2,1,0:T(8,128)(2,1)}, u32[]{:S(2)}, u32[]{:S(2)}) collective-permute-start(bf16[2,32,2048]{2,1,0:T(8,128)(2,1)} %get-tuple-element.263), channel_id=1, source_target_pairs={{0,4},{2,6},{4,0},{6,2},{1,5},{3,7},{5,1},{7,3},{8,12},{10,14},{12... | collective-permute-start | bytes 786440 | tf_op jit(solution)/shard_map/ppermute | solution.py:25
  379.0 3.9 collective-permute-start.41
  383.0 11.5 %collective-permute-start.42 = (f32[5,1024]{1,0:T(8,128)S(1)}, f32[5,1024]{1,0:T(8,128)S(1)}, u32[]{:S(2)}, u32[]{:S(2)}) collective-permute-start(f32[5,1024]{1,0:T(8,128)S(1)} %add.276), channel_id=1, source_target_pairs={{0,1},{1,0},{2,3},{3,2},{4,5},{5,4},{6,7},{7,6},{8,9},{9,8},{10,11... | collective-permute-start | bytes 61448 | tf_op jit(solution)/shard_map/ppermute | solution.py:25
  417.9 9.2 %collective-permute-start.45 = (bf16[2,32,2304]{2,1,0:T(8,128)(2,1)S(1)}, bf16[2,32,2304]{2,1,0:T(8,128)(2,1)}, u32[]{:S(2)}, u32[]{:S(2)}) collective-permute-start(bf16[2,32,2304]{2,1,0:T(8,128)(2,1)S(1)} %dynamic-slice_bitcast_fusion.6), channel_id=1, source_target_pairs={{0,1},{1,0},{2,3},{3,2},{4,5},{5,4},{6,7},{7,6},{8,9},{9,8},{10,11... | collective-permute-start | bytes 884744 | tf_op jit(solution)/shard_map/ppermute | solution.py:25
  428.2 1.9 collective-permute-start.46
  (76 other events, 446.5 us)
Sparse Core Ops, SparseCore 0:
  46.6 88.4 all-gather.2
  137.8 52.3 all-gather.4
  221.6 66.5 reduce-scatter.4
  291.7 123.2 reduce-scatter.2

commit v3 on v2

v3 whole, which is shorter than its diff:
```python
import functools
import itertools
import math

import jax
import jax.numpy as jnp
from jax import lax
from jax.experimental import pallas as pl
from jax.experimental.pallas import tpu as pltpu
from jax.sharding import Mesh
from jax.sharding import PartitionSpec as P

EPS = 1e-05
AXES = ("far", "x", "core", "z", "y")
SPREAD = ("far", "z", "y")
BF = jnp.bfloat16
F32 = jnp.float32


class Axis:
    def __init__(self, name):
        self.name, self.size = name, lax.axis_size(name)
        self.here = lax.axis_index(name)
        near = sorted(range(1, self.size), key=lambda by: (min(by, self.size - by), by))
        self.steps = tuple(near)

    def shift(self, value, by=1):
        return lax.ppermute(value, self.name, [(i, (i + by) % self.size) for i in range(self.size)])

    def at(self, by):
        return lax.rem(self.here + by, self.size)


def passed_along(shard, by):
    peers = lax.axis_size(("z", "y"))
    pairs = [(i, i + by) for i in range(peers) if 0 <= i + by < peers]
    return lax.ppermute(shard, ("z", "y"), pairs)


def fence(*values):
    return lax.optimization_barrier(values)


def contract_rows(left, right):
    return lax.dot_general(
        left, right, (((0,), (0,)), ((), ())), preferred_element_type=F32
    )


def contract_cols(left, right):
    return lax.dot_general(
        left, right, (((1,), (1,)), ((), ())), preferred_element_type=F32
    )


def times(left, right):
    return jnp.dot(left, right, preferred_element_type=F32)


def pick(value, at, dim):
    return lax.dynamic_index_in_dim(value, at, dim, keepdims=False)


def ordered(mine, other, here, dim):
    low = jnp.where(here == 0, mine, other)
    high = jnp.where(here == 0, other, mine)
    return jnp.stack([low, high], dim)


def cut(value, axis, dim):
    return pick(value, axis.here, dim), [pick(value, axis.at(by), dim) for by in axis.steps]


def shifted(parts, axis):
    return [axis.shift(part, by) for part, by in zip(parts, axis.steps, strict=True)]


def summed(own, others):
    total = own.astype(F32)
    for other in others:
        total = total + other.astype(F32)
    return total


def place_body(moves, here_ref, *refs):
    sems = refs[-1]
    copies = []
    for i, (source, target) in enumerate(moves(here_ref, refs[:-1])):
        copy = pltpu.make_async_copy(source, target, sems.at[i])
        copy.start()
        copies.append(copy)
    for copy in copies:
        copy.wait()


def out_array(shape, kind):
    return pltpu.HBM(shape, kind) if math.prod(shape) >= 2**18 else jax.ShapeDtypeStruct(shape, kind)


def pinned(*arrays):
    return [
        pltpu.with_memory_space_constraint(a, pltpu.HBM) if a.size >= 2**18 else a for a in arrays
    ]


def place(moves, count, here, sources, shapes):
    return pl.pallas_call(
        functools.partial(place_body, moves),
        out_shape=[out_array(shape, BF) for shape in shapes],
        in_specs=[pl.BlockSpec(memory_space=pltpu.SMEM)]
        + [pl.BlockSpec(memory_space=pl.ANY)] * len(sources),
        out_specs=[pl.BlockSpec(memory_space=pltpu.VMEM)] * len(shapes),
        scratch_shapes=[pltpu.SemaphoreType.DMA((count,))],
        compiler_params=params(20),
        cost_estimate=pl.CostEstimate(flops=0, bytes_accessed=2**20, transcendentals=0),
    )(here, *pinned(*sources))


def back(at, by, size):
    return lax.rem(at + size - by, size)


def place_mix(pieces, here, ax, ay, az, columns, width):
    nx, ny, nz = ax.size, ay.size, az.size
    rows, half = pieces[0][3].shape[-2], width // 2

    def moves(at, refs):
        wide, small, narrow = refs[-3:]
        for (dx, dy, backs, _), source in zip(pieces, refs[:-3], strict=True):
            x, y = back(at[0], dx, nx), back(at[1], dy, ny)
            for n, dz in enumerate(backs):
                z = back(at[2], dz, nz)
                block = source.at[n]
                yield block.at[:, :, pl.ds(0, columns)], wide.at[x, :, z, y]
                yield block.at[:, :, pl.ds(columns, 128)], small.at[x, :, z, y]
                for k in range(2):
                    yield (
                        block.at[k, :, pl.ds(columns + 128, half)],
                        narrow.at[x, z, y, :, pl.ds(k * half, half)],
                    )

    lead = (nx, 2, nz, ny, rows)
    shapes = [lead + (columns,), lead + (128,), (nx, nz, ny, rows, width)]
    arrays = [piece[3] for piece in pieces]
    wide, small, narrow = place(moves, 4 * nx * ny * nz, here, arrays, shapes)
    return wide.reshape(-1, columns), small.reshape(-1, 128), narrow.reshape(-1, width)


def cost():
    return pl.CostEstimate(flops=0, bytes_accessed=2**16, transcendentals=0)


def params(mib):
    return pltpu.CompilerParams(vmem_limit_bytes=mib * 1024 * 1024)


def whole(array):
    return pl.BlockSpec(
        array.shape, lambda i: (0,) * array.ndim, pipeline_mode=pl.Buffered(1)
    )


def tiles(rows, columns):
    return pl.BlockSpec((rows, columns), lambda i: (i, 0))


def chunks(columns):
    step = 384 if columns % 384 == 0 else 128 if columns % 128 == 0 else columns
    return [(a, step) for a in range(0, columns, step)]


def logistic(v):
    return 0.5 * jnp.tanh(0.5 * v) + 0.5


def piece_specs(pieces, tile):
    specs = []
    for p, piece in enumerate(pieces):
        first, last = p * piece.shape[0] // tile, (p + 1) * piece.shape[0] // tile - 1

        def at(i, first=first, last=last):
            return jnp.clip(i - first, 0, last - first), 0

        specs.append(pl.BlockSpec((tile, piece.shape[1]), at))
    return specs


def piece_tile(refs):
    steps = pl.num_programs(0) // len(refs)
    value = refs[0][...]
    for p, ref in enumerate(refs[1:], 1):
        value = jnp.where(pl.program_id(0) >= p * steps, ref[...], value)
    return value


def forward_body(count, *refs):
    w_ref, ev_ref, s_ref = refs[count:]
    hidden = s_ref.shape[1]
    x = piece_tile(refs[:count])
    for a, n in chunks(hidden):
        gate = times(x, w_ref[:, a : a + n])
        rise = times(x, w_ref[:, hidden + a : hidden + a + n])
        ev_ref[:, a : a + n] = gate.astype(BF)
        ev_ref[:, hidden + a : hidden + a + n] = rise.astype(BF)
        s_ref[:, a : a + n] = (gate * logistic(gate) * rise).astype(BF)


def ffn_forward(pieces, w, tile):
    count, both = sum(piece.shape[0] for piece in pieces), w.shape[1]
    return pl.pallas_call(
        functools.partial(forward_body, len(pieces)),
        grid=(count // tile,),
        in_specs=piece_specs(pieces, tile) + [whole(w)],
        out_specs=[tiles(tile, both), tiles(tile, both // 2)],
        out_shape=[out_array((count, both), BF), out_array((count, both // 2), BF)],
        compiler_params=params(24),
        cost_estimate=cost(),
    )(*pinned(*pieces, w))


def back_body(count, half, *refs):
    ev_ref, down_ref, w_ref, dev_ref, keep_ref, *sends = refs[count:]
    hidden = down_ref.shape[0]
    dy = piece_tile(refs[:count])
    for a, n in chunks(hidden):
        back = contract_cols(dy, down_ref[a : a + n, :])
        gate = ev_ref[:, a : a + n].astype(F32)
        rise = ev_ref[:, hidden + a : hidden + a + n].astype(F32)
        sigma = logistic(gate)
        back = back * sigma
        dev_ref[:, a : a + n] = (back * rise * (1.0 + gate * (1.0 - sigma))).astype(BF)
        dev_ref[:, hidden + a : hidden + a + n] = (back * gate).astype(BF)
    split_pieces(half, contract_cols(dev_ref[...], w_ref[...]), keep_ref, sends)


def split_rows(half, value, keep_ref, send_ref):
    @pl.when(pl.program_id(0) < half)
    def _():
        keep_ref[...] = value

    @pl.when(pl.program_id(0) >= half)
    def _():
        send_ref[...] = value


def split_specs(tile, columns, half):
    return [
        pl.BlockSpec((tile, columns), lambda i: (jnp.minimum(i, half - 1), 0)),
        pl.BlockSpec((tile, columns), lambda i: (jnp.maximum(i - half, 0), 0)),
    ]


def split_pieces(half, value, keep_ref, sends):
    cuts = len(sends) // half
    size = value.shape[0] // cuts

    @pl.when(pl.program_id(0) < half)
    def _():
        keep_ref[...] = value

    for n, ref in enumerate(sends):

        @pl.when(pl.program_id(0) == half + n // cuts)
        def _(n=n, ref=ref):
            at = n % cuts * size
            ref[...] = value[at : at + size].astype(ref.dtype)


def piece_outputs(count, width, tile, cuts):
    half, size = count // (2 * tile), tile // cuts
    specs = split_specs(tile, width, half)[:1]
    specs += [pl.BlockSpec((size, width), lambda i: (0, 0))] * (half * cuts)
    shapes = [out_array((count // 2, width), F32)]
    return specs, shapes + [out_array((size, width), BF)] * (half * cuts)


def ffn_back(pieces, ev, down, w, tile):
    count, both = ev.shape
    width, half = down.shape[1], count // (2 * tile)
    specs, shapes = piece_outputs(count, width, tile, 2)
    out = pl.pallas_call(
        functools.partial(back_body, len(pieces), half),
        grid=(2 * half,),
        in_specs=piece_specs(pieces, tile) + [tiles(tile, both), whole(down), whole(w)],
        out_specs=[tiles(tile, both)] + specs,
        out_shape=[out_array((count, both), BF)] + shapes,
        compiler_params=params(32),
        cost_estimate=cost(),
    )(*pinned(*pieces, ev, down, w))
    return out[0], out[1], out[2:]


def rows_body(function, half, left_ref, weight_ref, keep_ref, *sends):
    split_pieces(half, function(left_ref[...], weight_ref[...]), keep_ref, sends)


def row_halves(function, left, weight, width, tile):
    count = left.shape[0]
    half = count // (2 * tile)
    specs, shapes = piece_outputs(count, width, tile, 2)
    out = pl.pallas_call(
        functools.partial(rows_body, function, half),
        grid=(2 * half,),
        in_specs=[tiles(tile, left.shape[1]), whole(weight)],
        out_specs=specs,
        out_shape=shapes,
        compiler_params=params(20),
        cost_estimate=cost(),
    )(*pinned(left, weight))
    return out[0], out[1:]


def input_grad_body(half, dp_ref, win_ref, x_ref, keep_ref, *refs):
    sends, gain_ref = refs[:-1], refs[-1]
    value = contract_cols(dp_ref[...], win_ref[...])
    split_pieces(half, value, keep_ref, sends)
    x = x_ref[...].astype(F32)
    scale = lax.rsqrt(jnp.mean(x * x, axis=1, keepdims=True) + EPS)

    @pl.when(pl.program_id(0) == 0)
    def _():
        gain_ref[...] = jnp.zeros_like(gain_ref)

    gain_ref[...] += jnp.sum(value * (x * scale), axis=0, keepdims=True)


def input_grad(dp, win, x, tile):
    count, width = x.shape
    half = count // (2 * tile)
    specs, shapes = piece_outputs(count, width, tile, 2)
    out = pl.pallas_call(
        functools.partial(input_grad_body, half),
        grid=(2 * half,),
        in_specs=[tiles(tile, dp.shape[1]), whole(win), tiles(tile, width)],
        out_specs=specs + [pl.BlockSpec((1, width), lambda i: (0, 0))],
        out_shape=shapes + [jax.ShapeDtypeStruct((1, width), F32)],
        compiler_params=params(24),
        cost_estimate=cost(),
    )(*pinned(dp, win, x))
    return out[0], out[1:-1], out[-1][0]


def grad_body(lefts, rights, *refs):
    rest = refs[len(lefts) + len(rights) :]
    total = None
    for i, (first, end) in enumerate(lefts):
        for j, (start, stop) in enumerate(rights):
            low, high = max(first, start), min(end, stop)
            if low < high:
                left = refs[i][low - first : high - first, :]
                right = refs[len(lefts) + j][low - start : high - start, :]
                term = contract_rows(left, right)
                total = term if total is None else total + term
    for ref in rest[:-1]:
        total = total + ref[...]
    rest[-1][...] = total.astype(rest[-1].dtype).reshape(rest[-1].shape)


def token_spans(pieces):
    ends = list(itertools.accumulate(piece.shape[0] for piece in pieces))
    return list(zip([0] + ends[:-1], ends, strict=True))


def weight_grad(lefts, rights, tile, out_spec, shape, kind=BF, extra=()):
    rows = lefts[0].shape[1]
    return pl.pallas_call(
        functools.partial(grad_body, token_spans(lefts), token_spans(rights)),
        grid=(rows // tile,),
        in_specs=[pl.BlockSpec((left.shape[0], tile), lambda i: (0, i)) for left in lefts]
        + [whole(right) for right in rights]
        + [out_spec] * len(extra),
        out_specs=out_spec,
        out_shape=out_array(shape, kind),
        compiler_params=params(34),
        cost_estimate=cost(),
    )(*pinned(*lefts, *rights, *extra))


def gate_up_grad(lefts, rights, far, nz, rows):
    columns, width = rights[0].shape[1], lefts[0].shape[1]
    tile = 2 * nz * rows
    if tile % 128 == 0 and rows % 16 == 0:
        block = (1, 2 * nz, 1, rows, columns)
        spec = pl.BlockSpec(block, lambda i: (i // 4, 0, i % 4, 0, 0))
        out = weight_grad(lefts, rights, tile, spec, (far, 2 * nz, 4, rows, columns))
    else:
        out = weight_grad(lefts, rights, 256, tiles(256, columns), (width, columns))
        out = out.reshape(far, 4, 2 * nz, rows, columns).transpose(0, 2, 1, 3, 4)
    return out.reshape(width, columns)


def mix_grad_body(lower, here_ref, a_ref, dp_ref, g_ref, dh_ref, dh2_ref, *refs):
    group, wide, columns = dh_ref.shape[0], dp_ref.shape[1], refs[0].shape[-1]
    out = contract_rows(g_ref[:group, :], dh_ref[...])
    out = out + contract_rows(g_ref[group:, :], dh2_ref[...])
    parts = (
        (contract_rows(a_ref[...], dp_ref[...]), slice(0, wide)),
        (out, slice(wide, columns)),
    )
    own_y = here_ref[1] == 0
    for value, where in parts:
        value = value.astype(BF).reshape(-1, 2, refs[0].shape[2], value.shape[1])
        low, high = value[:, 0], value[:, 1]
        own, other = jnp.where(own_y, low, high), jnp.where(own_y, high, low)
        blocks = (own[:lower], other[:lower], own[lower:], other[lower:])
        for dx in range(2):

            @pl.when(lax.rem(pl.program_id(1) + here_ref[0], 2) == dx)
            def _(blocks=blocks, targets=refs[4 * dx : 4 * dx + 4], where=where):
                for block, target in zip(blocks, targets, strict=True):
                    target[0, :, :, where] = block


def mix_grad(normed, grad_projected, gated, hidden_low, here, nz, rows, lower):
    count, wide = grad_projected.shape
    half = hidden_low[0].shape[1] // 2
    columns, tile = wide + half, 2 * nz * rows
    shapes = [(2, n, rows, columns) for n in (lower, lower, nz - lower, nz - lower)] * 2
    out = pl.pallas_call(
        functools.partial(mix_grad_body, lower),
        grid=(2, 2),
        in_specs=[
            pl.BlockSpec(memory_space=pltpu.SMEM),
            pl.BlockSpec((count, tile), lambda k, x: (0, 2 * x + k)),
            pl.BlockSpec((count, wide), lambda k, x: (0, 0), pipeline_mode=pl.Buffered(1)),
            pl.BlockSpec((count, tile), lambda k, x: (0, x)),
            pl.BlockSpec((count // 2, half), lambda k, x: (0, k)),
            pl.BlockSpec((count // 2, half), lambda k, x: (0, k)),
        ],
        out_specs=[pl.BlockSpec((1,) + shape[1:], lambda k, x: (k, 0, 0, 0)) for shape in shapes],
        out_shape=[out_array(shape, BF) for shape in shapes],
        compiler_params=params(24),
        cost_estimate=cost(),
    )(here, *pinned(normed, grad_projected, gated, *hidden_low))
    return [out[:4], out[4:]]


def mixer_body(
    per_group, x_ref, gain_ref, win_ref, halo_ref, masks_ref, taps_ref, wout_ref, *refs
):
    normed_ref, projected_ref, mixed_ref, gated_ref, keep_ref, send_ref, rows, carry = refs
    count, feats = mixed_ref.shape
    x = x_ref[...].astype(F32)
    scale = lax.rsqrt(jnp.mean(x * x, axis=1, keepdims=True) + EPS)
    normed = (x * scale * gain_ref[...]).astype(BF)
    normed_ref[...] = normed
    projected = times(normed, win_ref[...])
    projected_ref[...] = projected
    product = projected[:, :feats] * projected[:, 2 * feats :]
    opens = lax.rem(pl.program_id(0), per_group) == 0
    rows[6:8, :] = jnp.where(opens, halo_ref[0], carry[...])
    rows[8 : 8 + count, :] = product
    mixed = taps_ref[2:3, :] * product
    mixed = mixed + masks_ref[:, 0:1] * (taps_ref[1:2, :] * rows[7 : 7 + count, :])
    mixed = mixed + masks_ref[:, 1:2] * (taps_ref[0:1, :] * rows[6 : 6 + count, :])
    carry[...] = product[count - 2 :]
    mixed_ref[...] = mixed
    gated = (projected[:, feats : 2 * feats] * mixed).astype(BF)
    gated_ref[...] = gated
    half = pl.num_programs(0) // 2
    split_rows(half, times(gated, wout_ref[...]), keep_ref, send_ref)


def mixer_forward(x, gain, win, halo, masks, taps, wout, tile):
    count, width = x.shape
    wide, feats = win.shape[1], wout.shape[0]
    per_group = count // (2 * tile)
    row = pl.BlockSpec((1, width), lambda i: (0, 0))
    return pl.pallas_call(
        functools.partial(mixer_body, per_group),
        grid=(2 * per_group,),
        in_specs=[
            tiles(tile, width),
            row,
            whole(win),
            pl.BlockSpec((1, 2, feats), lambda i: (i // per_group, 0, 0)),
            tiles(tile, masks.shape[1]),
            whole(taps),
            whole(wout),
        ],
        out_specs=[tiles(tile, width), tiles(tile, wide), tiles(tile, feats), tiles(tile, feats)]
        + split_specs(tile, width, per_group),
        out_shape=[
            out_array((count, width), BF),
            out_array((count, wide), F32),
            out_array((count, feats), F32),
            out_array((count, feats), BF),
        ]
        + [out_array((count // 2, width), F32)] * 2,
        scratch_shapes=[pltpu.VMEM((tile + 8, feats), F32), pltpu.VMEM((2, feats), F32)],
        compiler_params=params(28),
        cost_estimate=cost(),
    )(*pinned(x, gain[None], win, halo, masks, taps, wout))


def mixer_back_body(
    per_group, dh_ref, dh2_ref, wout_ref, projected_ref, mixed_ref, halo_ref, masks_ref, *refs
):
    taps_ref, *refs = refs
    out_ref, grad_ref, rows, carry = refs
    count, feats = mixed_ref.shape
    projected = projected_ref[...]
    dh = jnp.where(pl.program_id(0) < per_group, dh_ref[...], dh2_ref[...])
    back = contract_cols(dh, wout_ref[...])
    grad_c = back * mixed_ref[...]
    grad_mixed = back * projected[:, feats : 2 * feats]
    closes = lax.rem(pl.program_id(0), per_group) == 0
    rows[0:count, :] = grad_mixed
    rows[count : count + 2, :] = jnp.where(closes, halo_ref[0], carry[...])
    carry[...] = grad_mixed[:2]
    ahead = (
        grad_mixed,
        masks_ref[:, 2:3] * rows[1 : 1 + count, :],
        masks_ref[:, 3:4] * rows[2 : 2 + count, :],
    )
    grad_product = sum(taps_ref[2 - lag : 3 - lag, :] * ahead[lag] for lag in range(3))
    b_branch, x_branch = projected[:, :feats], projected[:, 2 * feats :]
    out_ref[:, :feats] = (grad_product * x_branch).astype(BF)
    out_ref[:, feats : 2 * feats] = grad_c.astype(BF)
    out_ref[:, 2 * feats :] = (grad_product * b_branch).astype(BF)

    @pl.when(pl.program_id(0) == 0)
    def _():
        grad_ref[...] = jnp.zeros_like(grad_ref)

    product = b_branch * x_branch
    for lag in range(3):
        grad_ref[2 - lag : 3 - lag, :] += jnp.sum(product * ahead[lag], axis=0, keepdims=True)


def mixer_back(dh, wout, projected, mixed, halo, masks, taps, tile):
    count, wide = projected.shape
    width, feats = dh[0].shape[1], wout.shape[0]
    per_group = count // (2 * tile)

    def at(i):
        return (i // per_group) * per_group + per_group - 1 - lax.rem(i, per_group)

    def turned(columns):
        return pl.BlockSpec((tile, columns), lambda i: (at(i), 0))

    return pl.pallas_call(
        functools.partial(mixer_back_body, per_group),
        grid=(2 * per_group,),
        in_specs=[
            pl.BlockSpec((tile, width), lambda i: (jnp.maximum(per_group - 1 - i, 0), 0)),
            pl.BlockSpec(
                (tile, width), lambda i: (jnp.minimum(2 * per_group - 1 - i, per_group - 1), 0)
            ),
            whole(wout),
            turned(wide),
            turned(feats),
            pl.BlockSpec((1, 2, feats), lambda i: (i // per_group, 0, 0)),
            turned(masks.shape[1]),
            whole(taps),
        ],
        out_specs=[turned(wide), pl.BlockSpec((8, feats), lambda i: (0, 0))],
        out_shape=[
            out_array((count, wide), BF),
            out_array((8, feats), F32),
        ],
        scratch_shapes=[pltpu.VMEM((tile + 8, feats), F32), pltpu.VMEM((2, feats), F32)],
        compiler_params=params(24),
        cost_estimate=cost(),
    )(*pinned(*dh, wout, projected, mixed, halo, masks, taps))


def norm_back_body(counts, *refs):
    grad, refs = 0.0, list(refs)
    for count in counts:
        grad = grad + piece_tile(refs[:count]).astype(F32)
        refs = refs[count:]
    x_ref, gain_ref, up_ref, *outs = refs
    x = x_ref[...].astype(F32)
    scale = lax.rsqrt(jnp.mean(x * x, axis=1, keepdims=True) + EPS)
    scaled = x * scale
    weighted = grad * gain_ref[...]
    mean = jnp.mean(weighted * scaled, axis=1, keepdims=True)
    out = up_ref[...].astype(F32) + scale * (weighted - scaled * mean)
    for ref in outs[:-1]:
        ref[...] = out.astype(ref.dtype)

    @pl.when(pl.program_id(0) == 0)
    def _():
        outs[-1][...] = jnp.zeros_like(outs[-1])

    outs[-1][...] += jnp.sum(grad * scaled, axis=0, keepdims=True)


def norm_back(grads, x, gain, upstream, kinds, tile):
    count, width = x.shape
    line = pl.BlockSpec((1, width), lambda i: (0, 0))
    specs = [spec for pieces in grads for spec in piece_specs(pieces, tile)]
    out = pl.pallas_call(
        functools.partial(norm_back_body, [len(pieces) for pieces in grads]),
        grid=(count // tile,),
        in_specs=specs + [tiles(tile, width), line, tiles(tile, width)],
        out_specs=[tiles(tile, width)] * len(kinds) + [line],
        out_shape=[out_array((count, width), kind) for kind in kinds]
        + [jax.ShapeDtypeStruct((1, width), F32)],
        compiler_params=params(16),
        cost_estimate=cost(),
    )(*pinned(*[piece for pieces in grads for piece in pieces], x, gain[None], upstream))
    return out[:-1], out[-1][0]


def per_device(
    block_input,
    in_weight,
    out_weight,
    gate_weight,
    up_weight,
    down_weight,
    norm_gain,
    ffn_gain,
    conv_weight,
    seq_starts,
    cotangent,
):
    ax, ac, az, ay = Axis(("far", "x")), Axis("core"), Axis("z"), Axis("y")
    ap = Axis("x")
    nx, nz, far = ax.size, az.size, lax.axis_size("far")
    core = ac.here
    here = jnp.stack([ax.here, ay.here, az.here]).astype(jnp.int32)
    tokens, width = block_input.shape
    rows = in_weight.shape[0]
    hidden = gate_weight.shape[1] // 4
    feats = width // 2
    wide_cols = 3 * feats
    lower = nz // 2
    few = max(1, nz // 4)
    z_back = (0,) + az.steps
    first_back, second_back = z_back[:lower], z_back[lower:]

    small = jnp.concatenate(
        [norm_gain[:, None], ffn_gain[:, None], conv_weight, jnp.zeros((rows, 123), F32)], 1
    ).astype(BF)
    in_sets = in_weight.astype(BF).reshape(rows, 3 * nx, 2, feats // nx)

    def in_part(which):
        return jnp.concatenate([pick(in_sets, which, 2).reshape(rows, wide_cols), small], 1)

    in_mine, in_got = in_part(core), ac.shift(in_part(1 - core))
    starts_core = ac.shift(seq_starts)

    def split_hidden(weight):
        cut = weight.astype(BF).reshape(rows, far, 2, 2, hidden // far)
        return jnp.transpose(cut, (2, 3, 0, 1, 4)).reshape(2, 2, rows, hidden)

    in_mine, in_got, gate_weight, up_weight = fence(in_mine, in_got, gate_weight, up_weight)
    out_low = out_weight.astype(BF).reshape(rows, 2, feats).transpose(1, 0, 2)
    mix = jnp.concatenate([ordered(in_mine, in_got, core, 0), out_low], 2)
    mix_z = {by: az.shift(mix, by) for by in first_back[1:]}
    gate_up = jnp.concatenate([split_hidden(gate_weight), split_hidden(up_weight)], 3)
    pair_mine = pick(gate_up, core, 1)
    pair_got = ac.shift(pick(gate_up, 1 - core, 1))

    pair_mine, pair_got, mix, mix_z, cotangent, down_low = fence(
        pair_mine, pair_got, mix, mix_z, cotangent, down_weight.astype(BF)
    )
    first = jnp.stack([mix] + [mix_z[by] for by in first_back[1:]])
    first_y = ay.shift(first)
    second = [az.shift(mix, by) for by in second_back]
    pair = ordered(pair_mine, pair_got, core, 1)
    quad_mine, quad_got = pick(pair, ap.here, 0), ap.shift(pick(pair, 1 - ap.here, 0))
    quad = ordered(quad_mine, quad_got, ap.here, 0)
    first_x = [ax.shift(first, by) for by in ax.steps]
    second, first, first_y, first_x, quad, down_low = fence(
        second, first, first_y, first_x, quad, down_low
    )

    gathered = lax.all_gather(quad.reshape(4 * rows, 2 * hidden), SPREAD, axis=0, tiled=True)
    second = jnp.stack(second)
    second_x = [ax.shift(second, by) for by in ax.steps]
    second_y = ay.shift(second)
    second_x, second_y, second, first_y, block_input, cotangent, down_low = fence(
        second_x, second_y, second, first_y, block_input, cotangent, down_low
    )

    ffn_down = lax.all_gather(down_low, SPREAD, axis=0, tiled=True)
    first_yx = [ax.shift(first_y, by) for by in ax.steps]
    second_xy = [ay.shift(part) for part in second_x]
    x_core = ac.shift(block_input)
    dy_core = ac.shift(cotangent)
    x_all = jnp.concatenate([block_input, x_core], 0)
    starts = jnp.concatenate([seq_starts, starts_core], 0)
    position = lax.axis_index(("z", "y")) * tokens + jnp.arange(tokens + 2, dtype=jnp.int32)
    reached = starts[:, None, :] <= position[None, :, None]
    offset = position[None, :] - jnp.max(jnp.where(reached, starts[:, None, :], 0), axis=2)
    masks = [offset[:, :tokens] >= 1, offset[:, :tokens] >= 2]
    masks += [offset[:, 1 : 1 + tokens] >= 1, offset[:, 2:] >= 2]
    masks = jnp.stack(masks, 2).astype(F32).reshape(2 * tokens, 4)
    first_yx, second_xy, first, second, x_all, dy_core, masks, cotangent = fence(
        first_yx, second_xy, first, second, x_all, dy_core, masks, cotangent
    )

    dy_low, dy_high = cotangent[: tokens // 2], cotangent[tokens // 2 :]
    dy_low_x = ap.shift(dy_low)
    pieces = [(0, 0, first_back, first), (0, 1, first_back, first_y)]
    pieces += [(0, 0, second_back, second), (0, 1, second_back, second_y)]
    for n, dx in enumerate(ax.steps):
        pieces += [(dx, 0, first_back, first_x[n]), (dx, 1, first_back, first_yx[n])]
        pieces += [(dx, 0, second_back, second_x[n]), (dx, 1, second_back, second_xy[n])]
    mix_in, tiny, mix_out = place_mix(pieces, here, ax, ay, az, wide_cols, width)
    tiny = tiny[:, :8].astype(F32)
    gain_mix, gain_ffn = tiny[:, 0], tiny[:, 1]
    taps = pick(tiny[:, 2:5].reshape(nx, 2, feats // nx, 3), core, 1).reshape(feats, 3)

    taps = jnp.concatenate([taps.T, jnp.zeros((5, feats), F32)], 0)

    last = x_all.reshape(2, tokens, width)[:, tokens - 2 :].reshape(4, width).astype(F32)
    scale = lax.rsqrt(jnp.mean(last * last, axis=1, keepdims=True) + EPS)
    last = times((last * scale * gain_mix[None, :]).astype(BF), mix_in)
    halo = passed_along((last[:, :feats] * last[:, 2 * feats :]).reshape(2, 2, feats), 1)
    normed_mix, projected, mixed, gated, mixer_keep, mixer_send = mixer_forward(
        x_all, gain_mix, mix_in, halo, masks, taps, mix_out, tokens // 2
    )
    mixer_send, mixer_keep, dy_low_x = fence(mixer_send, mixer_keep, dy_low_x)

    mixer_got = ac.shift(mixer_send)
    dy_low_far = ac.shift(dy_low_x)
    own_inputs = block_input.astype(F32)
    h = own_inputs + (mixer_keep + mixer_got)
    scale_ffn = lax.rsqrt(jnp.mean(h * h, axis=1, keepdims=True) + EPS)
    normed_own = (h * scale_ffn * gain_ffn[None, :]).astype(BF)
    normed_core = ac.shift(normed_own)

    normed_core, normed_own, h, scale_ffn = fence(normed_core, normed_own, h, scale_ffn)
    normed_x = ap.shift(normed_own)
    gathered = gathered.reshape(far, 2 * nz, 4, rows, 2 * hidden)
    gate_up = gathered.transpose(0, 2, 1, 3, 4).reshape(width, 2 * hidden)
    near = [normed_own, normed_core]
    dy_near = [cotangent, dy_core]
    near_ev, near_s = ffn_forward(near, gate_up, tokens // 2)
    tile = 384 if hidden % 384 == 0 else hidden
    spec = pl.BlockSpec((tile, width), lambda i: (i, 0))
    near_down = weight_grad([near_s], dy_near, tile, spec, (hidden, width), F32)
    normed_x, near_ev, near_s, dy_high, near_down = fence(
        normed_x, near_ev, near_s, dy_high, near_down
    )

    dy_high_x = ap.shift(dy_high)
    far_tokens = [normed_x, ac.shift(normed_x)]
    far_ev, far_s = ffn_forward(far_tokens, gate_up, tokens // 2)
    far_s, far_ev, dy_high_x = fence(far_s, far_ev, dy_high_x)

    dy_far = [dy_low_x, dy_high_x, dy_low_far, ac.shift(dy_high_x)]
    grad_down = weight_grad([far_s], dy_far, tile, spec, (hidden, width), BF, [near_down])
    far_ev, far_s, grad_down, ffn_down = fence(far_ev, far_s, grad_down, ffn_down)

    down_own, down_send = cut(grad_down.reshape(far, nz, 2, -1, width), ay, 2)
    down_got = shifted(down_send, ay)
    far_dev, far_keep, far_send = ffn_back(dy_far, far_ev, ffn_down, gate_up, tokens // 2)
    far_got = [ac.shift(part) for part in far_send]
    far_fed, far_fed_send = row_halves(times, far_s, ffn_down, width, tokens // 2)
    down_own, down_got, far_dev, far_keep, far_got, far_fed, far_fed_send, near_ev, dy_near = fence(
        down_own, down_got, far_dev, far_keep, far_got, far_fed, far_fed_send, near_ev, dy_near
    )

    down_own, down_send = cut(summed(down_own, down_got).astype(BF), az, 1)
    down_got = shifted(down_send, az)
    normed_x_got = ap.shift((far_keep + jnp.concatenate(far_got, 0)).astype(BF))
    near_dev, near_keep, near_send = ffn_back(dy_near, near_ev, ffn_down, gate_up, tokens // 2)
    grad_gate_up = gate_up_grad(near + far_tokens, [near_dev, far_dev], far, nz, rows)
    normed_x_got, near_keep, near_send, grad_gate_up, down_own, down_got = fence(
        normed_x_got, near_keep, near_send, grad_gate_up, down_own, down_got
    )

    quad = lax.psum_scatter(grad_gate_up, SPREAD, scatter_dimension=0, tiled=True)
    near_got = [ac.shift(part) for part in near_send]
    far_fed_got = [ac.shift(part) for part in far_fed_send]
    near_got, near_keep, far_fed_got, far_fed = fence(near_got, near_keep, far_fed_got, far_fed)
    (grad_hidden, hidden_own), grad_gain_ffn = norm_back(
        [[near_keep], near_got, [normed_x_got]], h, gain_ffn, cotangent, (F32, BF), tokens // 4
    )
    hidden_got = ac.shift(hidden_own)

    hidden_got, hidden_own, grad_hidden, far_fed, far_fed_got = fence(
        hidden_got, hidden_own, grad_hidden, far_fed, far_fed_got
    )
    fed_x = ap.shift((far_fed + jnp.concatenate(far_fed_got, 0)).astype(BF))
    hidden_low = [hidden_own, hidden_got]
    opening = jnp.concatenate([part[:2] for part in hidden_low], 0)
    branch = projected.reshape(2, tokens, wide_cols)[:, :2, feats : 2 * feats].reshape(4, feats)
    opening = contract_cols(opening, mix_out) * branch
    later = passed_along(opening.reshape(2, 2, feats), -1)
    grad_projected, tap_grads = mixer_back(
        hidden_low, mix_out, projected, mixed, later, masks, taps, tokens // 2
    )
    if nx == 2 and rows % 16 == 0 and 2 * nz * rows % 128 == 0:
        blocks = mix_grad(normed_mix, grad_projected, gated, hidden_low, here, nz, rows, few)
    else:
        back_in = contract_rows(normed_mix, grad_projected).astype(BF)
        back_out = contract_rows(gated, jnp.concatenate(hidden_low, 0)).astype(BF)
        back_out = back_out.reshape(nx, nz, 2, rows, 2, feats).transpose(0, 4, 1, 2, 3, 5)
        back_mix = jnp.concatenate(
            [back_in.reshape(nx, 2, nz, 2, rows, wide_cols), back_out], 5
        )
        blocks = []
        for dx in (0,) + ax.steps:
            ys = [pick(pick(back_mix, ax.at(dx), 0), ay.at(dy), 2) for dy in range(2)]
            blocks.append([y[:, part] for part in (slice(few), slice(few, None)) for y in ys])
    blocks, grad_projected, near_s, fed_x = fence(blocks, grad_projected, near_s, fed_x)

    first_hop = [ay.shift(block[1]) for block in blocks[1:]]
    first_got = [ay.shift(blocks[0][1])]
    second_hop = [ax.shift(block[3], by) for block, by in zip(blocks[1:], ax.steps, strict=True)]
    mix_keep, mix_send, grad_gain_mix = input_grad(grad_projected, mix_in, x_all, tokens // 2)
    near_fed, near_fed_send = row_halves(times, near_s, ffn_down, width, tokens // 2)
    tap_rows = tap_grads[:3].reshape(3, nx, 1, feats // nx)
    on_core = (jnp.arange(2) == core).astype(F32)[None, None, :, None]
    tap_rows = (tap_rows * on_core).reshape(3, width)
    own_gain = jnp.concatenate([grad_gain_mix[None], grad_gain_ffn[None]], 0)
    terms = jnp.concatenate([own_gain, tap_rows], 0)
    first_hop, first_got, second_hop, blocks, mix_keep, mix_send, near_fed_send, terms = fence(
        first_hop, first_got, second_hop, blocks, mix_keep, mix_send, near_fed_send, terms
    )

    second_got = [ay.shift(summed(blocks[0][3], second_hop).astype(BF))]
    for n, by in enumerate(ax.steps):
        block = blocks[n + 1]
        first_got.append(ax.shift(summed(block[0], [first_hop[n]]).astype(BF), by))
        second_got.append(ax.shift(block[2], by))
    mix_got = [ac.shift(part) for part in mix_send]
    near_fed_got = [ac.shift(part) for part in near_fed_send]
    (grad_inputs,), _ = norm_back(
        [[mix_keep], mix_got], block_input, gain_mix, grad_hidden, (BF,), tokens // 4
    )
    for axis in (ac, ax):
        terms = summed(terms, [axis.shift(terms, by) for by in axis.steps])
    terms = terms.reshape(5, 2 * nx, nz, 2 * rows).transpose(2, 0, 1, 3).reshape(nz, -1)
    high = lax.reduce_precision(terms, 8, 7)
    terms = jnp.concatenate([high, terms - high], 1).astype(BF)
    extra = -(-terms.shape[1] // (2 * rows * 128)) * 128
    terms = jnp.pad(terms, ((0, 0), (0, 2 * rows * extra - terms.shape[1])))
    terms = terms.reshape(nz, 2, rows, extra).transpose(1, 0, 2, 3)
    first_got, second_got, blocks, grad_inputs, terms, near_fed_got = fence(
        first_got, second_got, blocks, grad_inputs, terms, near_fed_got
    )

    own_z = jnp.concatenate(
        [summed(blocks[0][0], first_got).astype(BF), summed(blocks[0][2], second_got).astype(BF)], 1
    )
    own_z = jnp.concatenate([own_z, terms], 3)
    mix_own, mix_send = cut(own_z, az, 1)
    mix_parts = shifted(mix_send, az)
    quad = quad.reshape(2, 2, rows, 2 * hidden)
    quad_mine, quad_send = cut(quad, ap, 0)
    quad_got = jnp.concatenate([ap.shift(part) for part in jnp.split(quad_send[0], 2, 2)], 2)
    mix_parts, mix_own, quad_mine, quad_got = fence(mix_parts, mix_own, quad_mine, quad_got)
    mix_sum = summed(mix_own, mix_parts)
    terms = mix_sum[..., wide_cols + feats :].reshape(-1)
    count = 5 * 4 * nx * rows
    terms = (terms[:count] + terms[count : 2 * count]).reshape(5, 4 * nx * rows)

    pair = ordered(quad_mine, quad_got, ap.here, 0)
    pair_mine, pair_send = cut(pair, ac, 1)
    pair_got = shifted(pair_send, ac)[0]

    terms = terms + ay.shift(terms)
    at = ((ax.here * 2 + core) * 2 + ay.here) * rows

    part_down = summed(down_own, down_got)
    if far > 1:
        part_down = lax.psum_scatter(part_down, "far", scatter_dimension=0, tiled=True)
    part_down = part_down[0]
    block_output = (h + (near_fed + jnp.concatenate(near_fed_got, 0) + fed_x.astype(F32))).astype(BF)
    part_out = mix_sum[..., wide_cols : wide_cols + feats].transpose(1, 0, 2).reshape(rows, width)
    in_mine, in_send = cut(mix_sum[..., :wide_cols], ac, 0)
    in_got = shifted(in_send, ac)[0]
    blocks = (rows, 3 * nx, feats // nx)
    part_in = ordered(in_mine.reshape(blocks), in_got.reshape(blocks), core, 2)
    quads = ordered(pair_mine, pair_got, core, 1).astype(F32)

    def join_hidden(sets):
        sets = sets.reshape(2, 2, rows, far, hidden // far)
        return jnp.transpose(sets, (2, 3, 0, 1, 4)).reshape(rows, 4 * hidden)

    part_gate, part_rise = join_hidden(quads[..., :hidden]), join_hidden(quads[..., hidden:])
    own_terms = lax.dynamic_slice_in_dim(terms, at, rows, 1)
    return (
        block_output,
        grad_inputs,
        part_in.reshape(rows, 3 * width),
        part_out,
        part_gate,
        part_rise,
        part_down,
        own_terms[0],
        own_terms[1],
        own_terms[2:].T,
    )


def solution(mesh):
    nd, nf = mesh.shape["dp"], mesh.shape["fsdp"]
    rows, line = P(AXES, None), P(AXES)
    return jax.shard_map(
        per_device,
        mesh=Mesh(mesh.devices.reshape(nd // 4, 2, 2, nf // 2, 2), AXES),
        in_specs=(rows,) * 6 + (line, line, rows, P(AXES[:3], None), rows),
        out_specs=(rows,) * 7 + (line, line, rows),
        check_vma=False,
    )
```

time: 454 us -> 408 us (0.90)
  Pallas kernels: 71.1 us -> 152 us
  waiting for transfers between devices: 180 us -> 120 us
  local copies, waits for them, and re-layouts: 63.8 us -> 27.6 us
  matrix products: 24.8 us -> 2.77 us
  other arithmetic: 45.2 us -> 29.1 us
  starting transfers between devices: 45.8 us -> 54.2 us
    pallas_call x10 -> x16, Pallas kernels: 71.1 us -> 152 us  [the longest x2 30.2 us: ffn_back(): pl.pallas_call(functools.partial(back_body, len(pieces), half), grid=(2 *...]
    ppermute x45 -> x66, waiting for transfers between devices: 163 us -> 97.9 us  [shift(): lax.ppermute(value, self.name, [(i, (i + by) % self.size) for i in range(...]
    unnamed x163 -> x91, local copies, waits for them, and re-layouts: 37.5 us -> 5.76 us
    reduce_scatter x2 -> x1, waiting for transfers between devices: 0.01 us -> 14.7 us  [per_device(): lax.psum_scatter(grad_gate_up, SPREAD, scatter_dimension=0, tiled=True)]
    all_gather x2, waiting for transfers between devices: 15.5 us -> 2.28 us  [the longest x1 2.28 us: per_device(): ffn_down = lax.all_gather(down_low, SPREAD, axis=0, tiled=True)]
    dot_general x3 -> x1, matrix products: 10.4 us -> 0.37 us  [contract_cols(): lax.dot_general(left, right, (((1,), (1,)), ((), ())), preferred_element_...]
    reshape x15 -> x13, local copies, waits for them, and re-layouts: 13.5 us -> 4.09 us  [the longest x2 2.57 us: join_hidden(): return jnp.transpose(sets, (2, 3, 0, 1, 4)).reshape(rows, 4 * hidden)]
    ppermute x45 -> x66, starting transfers between devices: 40.3 us -> 47.7 us  [shift(): lax.ppermute(value, self.name, [(i, (i + by) % self.size) for i in range(...]
  transfers between devices with their start and end apart: 51 -> 71, of which waited for: 29 -> 36; matrix products, arithmetic and copies ran while one was open for 18% -> 10% of each run, Pallas kernels for 12% -> 38%
where the time goes in v3:
time: 408 us; the launch traced here: 401 us
  Pallas kernels  152 us (37%)
  waiting for transfers between devices  120 us (29%)
  starting transfers between devices  54.2 us (13%)
  other arithmetic  29.1 us (7%)
  local copies, waits for them, and re-layouts  27.6 us (7%)
  between operations  15 us (4%)
    ppermute x66, waiting for transfers between devices, shift(): lax.ppermute(value, self.name, [(i, (i + by) % self.size) for i in range(...  97.9 us
    ppermute x66, starting transfers between devices, shift(): lax.ppermute(value, self.name, [(i, (i + by) % self.size) for i in range(...  47.7 us
    pallas_call x2, Pallas kernels, ffn_back(): pl.pallas_call(functools.partial(back_body, len(pieces), half), grid=(2 *...  30.2 us
    pallas_call x3, Pallas kernels, weight_grad(): pl.pallas_call(functools.partial(grad_body, token_spans(lefts), token_spa...  29.9 us
    pallas_call x2, Pallas kernels, ffn_forward(): pl.pallas_call(functools.partial(forward_body, len(pieces)), grid=(count...  22.6 us
    reduce_scatter x1, waiting for transfers between devices, per_device(): lax.psum_scatter(grad_gate_up, SPREAD, scatter_dimension=0, tiled=True)  14.7 us
    pallas_call x2, Pallas kernels, row_halves(): pl.pallas_call(functools.partial(rows_body, function, half), grid=(2 * ha...  14.3 us
    pallas_call x1, Pallas kernels, mixer_forward(): pl.pallas_call(functools.partial(mixer_body, per_group), grid=(2 * per_gr...  11.8 us
  transfers between devices with their start and end apart: 71, of which 36 were waited for; matrix products, arithmetic and copies ran while one was open for 10% of the time, Pallas kernels for 38%

profile of v3, /device:TPU:0, one launch (start us, length us, event | category | flops | bytes accessed | tf_op | source)
XLA Modules:
  0.0 400.6 jit_solution(16917206089774863492)
XLA Ops:
  16.1 2.8 collective-permute-start.2
  19.7 8.4 %collective-permute-done.2 = bf16[2,32,2176]{2,1,0:T(8,128)(2,1)S(1)} collective-permute-done((bf16[2,32,2176]{2,1,0:T(8,128)(2,1)S(1)}, bf16[2,32,2176]{2,1,0:T(8,128)(2,1)S(1)}, u32[]{:S(2)}, u32[]{:S(2)}) %collective-permute-start.2) | collective-permute-done | bytes 278560 | tf_op jit(solution)/shard_map/ppermute | solution.py:28
  33.7 6.2 %collective-permute-done.7 = bf16[2,32,2304]{2,1,0:T(8,128)(2,1)S(1)} collective-permute-done((bf16[2,32,2304]{2,1,0:T(8,128)(2,1)S(1)}, bf16[2,32,2304]{2,1,0:T(8,128)(2,1)S(1)}, u32[]{:S(2)}, u32[]{:S(2)}) %collective-permute-start.7) | collective-permute-done | bytes 294944 | tf_op jit(solution)/shard_map/ppermute | solution.py:28
  40.9 6.4 %collective-permute-done.4 = bf16[2,32,2176]{2,1,0:T(8,128)(2,1)S(1)} collective-permute-done((bf16[2,32,2176]{2,1,0:T(8,128)(2,1)S(1)}, bf16[2,32,2176]{2,1,0:T(8,128)(2,1)S(1)}, u32[]{:S(2)}, u32[]{:S(2)}) %collective-permute-start.4) | collective-permute-done | bytes 278560 | tf_op jit(solution)/shard_map/ppermute | solution.py:28
  47.3 2.8 collective-permute-done.6.refs_4_
  55.1 9.9 %collective-permute-done.8.refs_6_ = bf16[2,2,32,2176]{3,2,1,0:T(8,128)(2,1)S(1)} collective-permute-done((bf16[2,2,32,2176]{3,2,1,0:T(8,128)(2,1)S(1)}, bf16[2,2,32,2176]{3,2,1,0:T(8,128)(2,1)S(1)}, u32[]{:S(2)}, u32[]{:S(2)}) %collective-permute-start.8) | collective-permute-done | bytes 557088 | tf_op jit(solution)/shard_map/ppermute | solution.py:28
  65.0 7.5 %collective-permute-done.9.refs_3_ = bf16[2,2,32,2176]{3,2,1,0:T(8,128)(2,1)S(1)} collective-permute-done((bf16[2,2,32,2176]{3,2,1,0:T(8,128)(2,1)S(1)}, bf16[2,2,32,2176]{3,2,1,0:T(8,128)(2,1)S(1)}, u32[]{:S(2)}, u32[]{:S(2)}) %collective-permute-start.9) | collective-permute-done | bytes 557088 | tf_op jit(solution)/shard_map/ppermute | solution.py:28
  75.1 1.9 collective-permute-start.11
  79.3 10.6 %collective-permute-done.10.refs_5_ = bf16[2,2,32,2176]{3,2,1,0:T(8,128)(2,1)} collective-permute-done((bf16[2,2,32,2176]{3,2,1,0:T(8,128)(2,1)S(1)}, bf16[2,2,32,2176]{3,2,1,0:T(8,128)(2,1)}, u32[]{:S(2)}, u32[]{:S(2)}) %collective-permute-start.10) | collective-permute-done | bytes 557088 | tf_op jit(solution)/shard_map/ppermute | solution.py:28
  89.9 2.5 collective-permute-done.11.refs_7_
  92.4 5.5 %shard_map.186 = (bf16[2,2,4,2,32,1536]{5,4,3,2,1,0:T(8,128)(2,1)}, bf16[2,2,4,2,32,128]{5,4,3,2,1,0:T(8,128)(2,1)S(1)}, bf16[2,4,2,32,1024]{4,3,2,1,0:T(8,128)(2,1)}) custom-call(s32[3]{0:T(128)S(1)} %pad_add_fusion.2.here_ref, bf16[2,2,32,2176]{3,2,1,0:T(8,128)(2,1)} %copy-done.10, bf16[2,2,32,2176]{3,2,1,0:T(8,128)(2,1)} %copy-done.24, ...), custom_call_target="tpu_custom_call" | custom-call | bytes 1048576 | tf_op jit(solution)/shard_map/pallas_call | solution.py:107
  98.3 2.1 fusion.26
  101.7 2.4 fusion.29
  104.1 4.4 %collective-permute-start.15 = (f32[2,2,512]{2,1,0:T(2,128)S(1)}, f32[2,2,512]{2,1,0:T(2,128)S(1)}, u32[]{:S(2)}, u32[]{:S(2)}) collective-permute-start(f32[2,2,512]{2,1,0:T(2,128)S(1)} %reshape.241), channel_id=1, source_target_pairs={{0,1},{1,2},{2,3},{3,4},{4,5},{5,6},{6,7},{8,9},{9,10},{10,11},{11... | collective-permute-start | bytes 24584 | tf_op jit(solution)/shard_map/ppermute | solution.py:37
  109.9 11.8 %shard_map.187 = (bf16[1024,1024]{1,0:T(8,128)(2,1)}, f32[1024,1536]{1,0:T(8,128)}, f32[1024,512]{1,0:T(8,128)}, bf16[1024,512]{1,0:T(8,128)(2,1)}, f32[512,1024]{1,0:T(8,128)}, /*index=5*/f32[512,1024]{1,0:T(8,128)}) custom-call(bf16[1024,1024]{1,0:T(8,128)(2,1)} %copy-done.2, f32[1,1024]{1,0:T(1,128)S(1)} %get-tuple-element.443.gain_ref.refs_6_, ...), custom_call_target="tpu_custom_call" | custom-call | bytes 65536 | tf_op jit(solution)/shard_map/pallas_call | solution.py:469
  122.3 3.9 collective-permute-done.17
  126.2 2.7 multiply_reduce_fusion
  130.7 2.5 collective-permute-done.18.refs_1_
  134.0 4.8 %copy.101 = bf16[1,4,8,32,2304]{4,3,2,1,0:T(8,128)(2,1)} copy(bf16[1,4,8,32,2304]{4,3,1,2,0:T(8,128)(2,1)} %bitcast.198) | data formatting | bytes 9437184 | tf_op jit(solution)/shard_map/transpose | solution.py:731
  138.8 11.3 %shard_map.188 = (bf16[1024,2304]{1,0:T(8,128)(2,1)}, bf16[1024,1152]{1,0:T(8,128)(2,1)}) custom-call(bf16[512,1024]{1,0:T(8,128)(2,1)} %copy-done.4, bf16[512,1024]{1,0:T(8,128)(2,1)} %copy-done.8, bf16[1024,2304]{1,0:T(8,128)(2,1)} %bitcast.183), custom_call_target="tpu_custom_call" | custom-call | bytes 65536 | tf_op jit(solution)/shard_map/pallas_call | solution.py:210
  150.2 6.8 %shard_map.189.refs_5_ = f32[1152,1024]{1,0:T(8,128)} custom-call(bf16[1024,1152]{1,0:T(8,128)(2,1)} %get-tuple-element.337.refs_0_.left_ref, bf16[512,1024]{1,0:T(8,128)(2,1)} %refs_8_, bf16[512,1024]{1,0:T(8,128)(2,1)} %collective-permute-done.13.refs_2_.refs_1_), custom_call_target="tpu_custom_call" | custom-call | bytes 65536 | tf_op jit(solution)/shard_map/pallas_call | solution.py:366
  162.3 11.2 %shard_map.190 = (bf16[1024,2304]{1,0:T(8,128)(2,1)}, bf16[1024,1152]{1,0:T(8,128)(2,1)}) custom-call(bf16[512,1024]{1,0:T(8,128)(2,1)} %collective-permute-done.19.refs_0_.refs_2_, bf16[512,1024]{1,0:T(8,128)(2,1)} %copy-done.9, bf16[1024,2304]{1,0:T(8,128)(2,1)} %bitcast.184), custom_call_target="tpu_custom_call" | custom-call | bytes 65536 | tf_op jit(solution)/shard_map/pallas_call | solution.py:210
  176.3 7.2 %shard_map.191 = bf16[1152,1024]{1,0:T(8,128)(2,1)} custom-call(bf16[1024,1152]{1,0:T(8,128)(2,1)} %get-tuple-element.270.refs_0_.left_ref, bf16[256,1024]{1,0:T(8,128)(2,1)} %copy-done.14, bf16[256,1024]{1,0:T(8,128)(2,1)} %copy-done.15, bf16[256,1024]{1,0:T(8,128)(2,1)} %copy-done.16, bf16[256,1024]{1,0:T(8,128)(2,1)} %copy-done.17, ...), custom_call_target="tpu_custom_call" | custom-call | bytes 65536 | tf_op jit(solution)/shard_map/pallas_call | solution.py:366
  183.5 2.3 all-gather.5.cloned.1.call-done.refs_5_.weight_ref.refs_3_
  188.3 15.3 %shard_map.192 = (bf16[1024,2304]{1,0:T(8,128)(2,1)}, f32[512,1024]{1,0:T(8,128)}, bf16[128,1024]{1,0:T(8,128)(2,1)S(1)}, bf16[128,1024]{1,0:T(8,128)(2,1)S(1)},...) custom-call(bf16[256,1024]{1,0:T(8,128)(2,1)} %copy-done.14, bf16[256,1024]{1,0:T(8,128)(2,1)} %copy-done.15, ...), custom_call_target="tpu_custom_call" | custom-call | bytes 65536 | tf_op jit(solution)/shard_map/pallas_call | solution.py:281
  204.6 7.2 %shard_map.193 = (f32[512,1024]{1,0:T(8,128)}, bf16[128,1024]{1,0:T(8,128)(2,1)S(1)}, bf16[128,1024]{1,0:T(8,128)(2,1)S(1)}, bf16[128,1024]{1,0:T(8,128)(2,1)S(1)}, bf16[128,1024]{1,0:T(8,128)(2,1)S(1)}) custom-call(bf16[1024,1152]{1,0:T(8,128)(2,1)} %get-tuple-element.270.refs_0_.left_ref, ...), custom_call_target="tpu_custom_call" | custom-call | bytes 65536 | tf_op jit(solution)/shard_map/pallas_call | solution.py:301
  211.8 2.4 collective-permute-done.24
  220.6 2.4 collective-permute-start.31
  223.5 14.9 %shard_map.194 = (bf16[1024,2304]{1,0:T(8,128)(2,1)}, f32[512,1024]{1,0:T(8,128)}, bf16[128,1024]{1,0:T(8,128)(2,1)S(1)}, bf16[128,1024]{1,0:T(8,128)(2,1)S(1)},...) custom-call(bf16[512,1024]{1,0:T(8,128)(2,1)} %refs_8_, ...), custom_call_target="tpu_custom_call" | custom-call | bytes 65536 | tf_op jit(solution)/shard_map/pallas_call | solution.py:281
  238.4 15.9 %shard_map.195 = bf16[1,8,4,32,2304]{4,3,2,1,0:T(8,128)(2,1)} custom-call(bf16[512,1024]{1,0:T(8,128)(2,1)} %copy-done.4, bf16[512,1024]{1,0:T(8,128)(2,1)} %copy-done.8, bf16[512,1024]{1,0:T(8,128)(2,1)} %collective-permute-done.19.refs_0_.refs_2_, bf16[512,1024]{1,0:T(8,128)(2,1)} %copy-done.9, bf16[1024,2304]{1,0:T(8,128)(2,1)} %get-tuple-element.290.refs_4_, ...), custom_call_target="tpu_custom_call" | custom-call | bytes 65536 | tf_op jit(solution)/shard_map/pallas_call | solution.py:366
  258.6 5.6 %shard_map.196 = (f32[512,1024]{1,0:T(8,128)}, bf16[512,1024]{1,0:T(8,128)(2,1)}, f32[1,1024]{1,0:T(1,128)S(1)}) custom-call(f32[512,1024]{1,0:T(8,128)} %get-tuple-element.304.refs_0_, bf16[128,1024]{1,0:T(8,128)(2,1)S(1)} %collective-permute-done.33.refs_1_, bf16[128,1024]{1,0:T(8,128)(2,1)S(1)} %collective-permute-done.34.refs_2_, ...), custom_call_target="tpu_custom_call" | custom-call | bytes 65536 | tf_op jit(solution)/shard_map/pallas_call | solution.py:594
  264.3 2.7 collective-permute-done.41.dh2_ref
  272.7 4.0 %collective-permute-done.42.halo_ref = f32[2,2,512]{2,1,0:T(2,128)S(1)} collective-permute-done((f32[2,2,512]{2,1,0:T(2,128)S(1)}, f32[2,2,512]{2,1,0:T(2,128)S(1)}, u32[]{:S(2)}, u32[]{:S(2)}) %collective-permute-start.42) | collective-permute-done | bytes 8224 | tf_op jit(solution)/shard_map/ppermute | solution.py:37
  276.7 7.8 %shard_map.197 = (bf16[1024,1536]{1,0:T(8,128)(2,1)}, f32[8,512]{1,0:T(8,128)S(1)}) custom-call(bf16[512,1024]{1,0:T(8,128)(2,1)} %get-tuple-element.317.dh_ref, bf16[512,1024]{1,0:T(8,128)(2,1)} %copy-done.7, bf16[512,1024]{1,0:T(8,128)(2,1)} %bitcast.195, f32[1024,1536]{1,0:T(8,128)} %get-tuple-element.319.projected_ref, ...), custom_call_target="tpu_custom_call" | custom-call | bytes 65536 | tf_op jit(solution)/shard_map/pallas_call | solution.py:542
  284.5 10.0 %shard_map.198 = (bf16[2,1,32,2048]{3,2,1,0:T(8,128)(2,1)S(1)}, bf16[2,1,32,2048]{3,2,1,0:T(8,128)(2,1)S(1)}, bf16[2,3,32,2048]{3,2,1,0:T(8,128)(2,1)}, bf16[2,3...) custom-call(s32[3]{0:T(128)S(1)} %pad_add_fusion.2.here_ref, ...), custom_call_target="tpu_custom_call" | custom-call | bytes 65536 | tf_op jit(solution)/shard_map/pallas_call | solution.py:419
  295.9 2.8 collective-permute-start.44
  298.8 7.1 %shard_map.199 = (f32[512,1024]{1,0:T(8,128)}, bf16[128,1024]{1,0:T(8,128)(2,1)S(1)}, bf16[128,1024]{1,0:T(8,128)(2,1)S(1)}, bf16[128,1024]{1,0:T(8,128)(2,1)S(1)}, bf16[128,1024]{1,0:T(8,128)(2,1)S(1)}) custom-call(bf16[1024,1152]{1,0:T(8,128)(2,1)} %get-tuple-element.337.refs_0_.left_ref, ...), custom_call_target="tpu_custom_call" | custom-call | bytes 65536 | tf_op jit(solution)/shard_map/pallas_call | solution.py:301
  305.9 9.3 %shard_map.200 = (f32[512,1024]{1,0:T(8,128)}, bf16[128,1024]{1,0:T(8,128)(2,1)S(1)}, bf16[128,1024]{1,0:T(8,128)(2,1)S(1)}, bf16[128,1024]{1,0:T(8,128)(2,1)S(1...) custom-call(bf16[1024,1536]{1,0:T(8,128)(2,1)} %get-tuple-element.347.dp_ref, bf16[1024,1536]{1,0:T(8,128)(2,1)} %bitcast.189, ...), custom_call_target="tpu_custom_call" | custom-call | bytes 65536 | tf_op jit(solution)/shard_map/pallas_call | solution.py:331
  319.5 2.3 add_convert_fusion.5
  323.0 3.2 collective-permute-done.55
  329.1 2.1 add_bitcast_fusion
  332.1 5.0 %shard_map.201 = (bf16[512,1024]{1,0:T(8,128)(2,1)}, f32[1,1024]{1,0:T(1,128)}) custom-call(f32[512,1024]{1,0:T(8,128)} %get-tuple-element.368.refs_0_, bf16[128,1024]{1,0:T(8,128)(2,1)S(1)} %collective-permute-done.50.refs_1_, bf16[128,1024]{1,0:T(8,128)(2,1)S(1)} %collective-permute-done.51.refs_2_, bf16[128,1024]{1,0:T(8,128)(2,1)S(1)} %collective-permute-done.52.refs_3_, ...), custom_call_target="tpu_custom_call" | custom-call | bytes 65536 | tf_op jit(solution)/shard_map/pallas_call | solution.py:594
  337.2 9.4 %collective-permute-done.48 = bf16[2,3,32,2048]{3,2,1,0:T(8,128)(2,1)} collective-permute-done((bf16[2,3,32,2048]{3,2,1,0:T(8,128)(2,1)}, bf16[2,3,32,2048]{3,2,1,0:T(8,128)(2,1)}, u32[]{:S(2)}, u32[]{:S(2)}) %collective-permute-start.48) | collective-permute-done | bytes 786464 | tf_op jit(solution)/shard_map/ppermute | solution.py:28
  349.5 4.1 %collective-permute-start.61 = (bf16[2,32,2176]{2,1,0:T(8,128)(2,1)S(1)}, bf16[2,32,2176]{2,1,0:T(8,128)(2,1)}, u32[]{:S(2)}, u32[]{:S(2)}) collective-permute-start(bf16[2,32,2176]{2,1,0:T(8,128)(2,1)S(1)} %get-tuple-element.418), channel_id=1, source_target_pairs={{0,6},{2,0},{4,2},{6,4},{1,7},{3,1},{5,3},{7,5},{8,14},{10,8},{12,... | collective-permute-start | bytes 835592 | tf_op jit(solution)/shard_map/ppermute | solution.py:28
  353.5 14.7 %reduce-scatter.2.cloned.1.call-done = bf16[128,2304]{1,0:T(8,128)(2,1)} async-done(((bf16[1024,2304]{1,0:T(8,128)(2,1)}), bf16[128,2304]{1,0:T(8,128)(2,1)}) %reduce-scatter.2.cloned.1.call-update) | async-done | bytes 589840 | tf_op jit(solution)/shard_map/reduce_scatter | solution.py:769
  371.4 3.8 add_convert_fusion.1
  376.1 2.2 collective-permute-done.63
  378.3 3.6 collective-permute-done.62
  (322 shorter events, 90.1 us)
Async XLA Ops:
  7.2 126.8 %all-gather.3.cloned.1.call-start = ((), (), s32[]{:S(2)}) async-start(), calls=%async_computation.1 | async-start | bytes 5308416 | tf_op jit(solution)/shard_map/all_gather | solution.py:672
  15.6 12.5 %collective-permute-start.1 = (bf16[2,32,2304]{2,1,0:T(8,128)(2,1)S(1)}, bf16[2,32,2304]{2,1,0:T(8,128)(2,1)S(1)}, u32[]{:S(2)}, u32[]{:S(2)}) collective-permute-start(bf16[2,32,2304]{2,1,0:T(8,128)(2,1)S(1)} %bitcast.209), channel_id=1, source_target_pairs={{0,8},{8,0},{1,9},{9,1},{2,10},{10,2},{3,11},{11,3},{4,12},{12,4},... | collective-permute-start | bytes 884744 | tf_op jit(solution)/shard_map/ppermute | solution.py:28
  16.1 12.0 %collective-permute-start.2 = (bf16[2,32,2176]{2,1,0:T(8,128)(2,1)S(1)}, bf16[2,32,2176]{2,1,0:T(8,128)(2,1)S(1)}, u32[]{:S(2)}, u32[]{:S(2)}) collective-permute-start(bf16[2,32,2176]{2,1,0:T(8,128)(2,1)S(1)} %pad_maximum_fusion.7), channel_id=1, source_target_pairs={{0,2},{2,4},{4,6},{6,0},{1,3},{3,5},{5,7},{7,1},{8,10},{10,12},{12... | collective-permute-start | bytes 835592 | tf_op jit(solution)/shard_map/ppermute | solution.py:28
  28.1 12.8 %collective-permute-start.3 = (bf16[2,32,2176]{2,1,0:T(8,128)(2,1)S(1)}, bf16[2,32,2176]{2,1,0:T(8,128)(2,1)S(1)}, u32[]{:S(2)}, u32[]{:S(2)}) collective-permute-start(bf16[2,32,2176]{2,1,0:T(8,128)(2,1)S(1)} %pad_maximum_fusion.7), channel_id=1, source_target_pairs={{0,6},{2,0},{4,2},{6,4},{1,7},{3,1},{5,3},{7,5},{8,14},{10,8},{12,... | collective-permute-start | bytes 835592 | tf_op jit(solution)/shard_map/ppermute | solution.py:28
  29.8 17.4 %collective-permute-start.4 = (bf16[2,32,2176]{2,1,0:T(8,128)(2,1)S(1)}, bf16[2,32,2176]{2,1,0:T(8,128)(2,1)S(1)}, u32[]{:S(2)}, u32[]{:S(2)}) collective-permute-start(bf16[2,32,2176]{2,1,0:T(8,128)(2,1)S(1)} %pad_maximum_fusion.7), channel_id=1, source_target_pairs={{0,4},{2,6},{4,0},{6,2},{1,5},{3,7},{5,1},{7,3},{8,12},{10,14},{12... | collective-permute-start | bytes 835592 | tf_op jit(solution)/shard_map/ppermute | solution.py:28
  29.9 10.0 %collective-permute-start.7 = (bf16[2,32,2304]{2,1,0:T(8,128)(2,1)S(1)}, bf16[2,32,2304]{2,1,0:T(8,128)(2,1)S(1)}, u32[]{:S(2)}, u32[]{:S(2)}) collective-permute-start(bf16[2,32,2304]{2,1,0:T(8,128)(2,1)S(1)} %fusion.5), channel_id=1, source_target_pairs={{0,16},{16,0},{1,17},{17,1},{2,18},{18,2},{3,19},{19,3},{4,20},{20... | collective-permute-start | bytes 884744 | tf_op jit(solution)/shard_map/ppermute | solution.py:28
  31.6 15.7 %collective-permute-start.5 = (bf16[2,2,32,2176]{3,2,1,0:T(8,128)(2,1)S(1)}, bf16[2,2,32,2176]{3,2,1,0:T(8,128)(2,1)S(1)}, u32[]{:S(2)}, u32[]{:S(2)}) collective-permute-start(bf16[2,2,32,2176]{3,2,1,0:T(8,128)(2,1)S(1)} %pad_maximum_fusion.3.refs_0_), channel_id=1, source_target_pairs={{0,1},{1,0},{2,3},{3,2},{4,5},{5,4},{6,7},{7,6},{8,9},{9,8},{10,11... | collective-permute-start | bytes 1671176 | tf_op jit(solution)/shard_map/ppermute | solution.py:28
  33.2 16.9 %collective-permute-start.6 = (bf16[2,2,32,2176]{3,2,1,0:T(8,128)(2,1)S(1)}, bf16[2,2,32,2176]{3,2,1,0:T(8,128)(2,1)S(1)}, u32[]{:S(2)}, u32[]{:S(2)}) collective-permute-start(bf16[2,2,32,2176]{3,2,1,0:T(8,128)(2,1)S(1)} %pad_maximum_fusion.3.refs_0_), channel_id=1, source_target_pairs={{0,16},{16,0},{1,17},{17,1},{2,18},{18,2},{3,19},{19,3},{4,20},{20... | collective-permute-start | bytes 1671176 | tf_op jit(solution)/shard_map/ppermute | solution.py:28
  50.9 134.9 %all-gather.5.cloned.1.call-start = ((), (), s32[]{:S(2)}) async-start(), calls=%async_computation.2 | async-start | bytes 2654208 | tf_op jit(solution)/shard_map/all_gather | solution.py:680
  52.0 12.9 %collective-permute-start.8 = (bf16[2,2,32,2176]{3,2,1,0:T(8,128)(2,1)S(1)}, bf16[2,2,32,2176]{3,2,1,0:T(8,128)(2,1)S(1)}, u32[]{:S(2)}, u32[]{:S(2)}) collective-permute-start(bf16[2,2,32,2176]{3,2,1,0:T(8,128)(2,1)S(1)} %pad_maximum_fusion.4.refs_2_), channel_id=1, source_target_pairs={{0,16},{16,0},{1,17},{17,1},{2,18},{18,2},{3,19},{19,3},{4,20},{20... | collective-permute-start | bytes 1671176 | tf_op jit(solution)/shard_map/ppermute | solution.py:28
  53.6 18.9 %collective-permute-start.9 = (bf16[2,2,32,2176]{3,2,1,0:T(8,128)(2,1)S(1)}, bf16[2,2,32,2176]{3,2,1,0:T(8,128)(2,1)S(1)}, u32[]{:S(2)}, u32[]{:S(2)}) collective-permute-start(bf16[2,2,32,2176]{3,2,1,0:T(8,128)(2,1)S(1)} %pad_maximum_fusion.4.refs_2_), channel_id=1, source_target_pairs={{0,1},{1,0},{2,3},{3,2},{4,5},{5,4},{6,7},{7,6},{8,9},{9,8},{10,11... | collective-permute-start | bytes 1671176 | tf_op jit(solution)/shard_map/ppermute | solution.py:28
  73.0 19.4 %collective-permute-start.13 = (bf16[512,1024]{1,0:T(8,128)(2,1)}, bf16[512,1024]{1,0:T(8,128)(2,1)}, u32[]{:S(2)}, u32[]{:S(2)}) collective-permute-start(bf16[512,1024]{1,0:T(8,128)(2,1)} %refs_8_), channel_id=1, source_target_pairs={{0,8},{8,0},{1,9},{9,1},{2,10},{10,2},{3,11},{11,3},{4,12},{12,4},... | collective-permute-start | bytes 3145736 | tf_op jit(solution)/shard_map/ppermute | solution.py:28
  74.9 15.0 %collective-permute-start.10 = (bf16[2,2,32,2176]{3,2,1,0:T(8,128)(2,1)S(1)}, bf16[2,2,32,2176]{3,2,1,0:T(8,128)(2,1)}, u32[]{:S(2)}, u32[]{:S(2)}) collective-permute-start(bf16[2,2,32,2176]{3,2,1,0:T(8,128)(2,1)S(1)} %collective-permute-done.5.refs_1_), channel_id=1, source_target_pairs={{0,16},{16,0},{1,17},{17,1},{2,18},{18,2},{3,19},{19,3},{4,20},{20... | collective-permute-start | bytes 1671176 | tf_op jit(solution)/shard_map/ppermute | solution.py:28
  75.1 17.4 %collective-permute-start.11 = (bf16[2,2,32,2176]{3,2,1,0:T(8,128)(2,1)}, bf16[2,2,32,2176]{3,2,1,0:T(8,128)(2,1)}, u32[]{:S(2)}, u32[]{:S(2)}) collective-permute-start(bf16[2,2,32,2176]{3,2,1,0:T(8,128)(2,1)} %copy-done.26), channel_id=1, source_target_pairs={{0,1},{1,0},{2,3},{3,2},{4,5},{5,4},{6,7},{7,6},{8,9},{9,8},{10,11... | collective-permute-start | bytes 1671176 | tf_op jit(solution)/shard_map/ppermute | solution.py:28
  100.4 21.3 %collective-permute-start.16 = (bf16[256,1024]{1,0:T(8,128)(2,1)S(1)}, bf16[256,1024]{1,0:T(8,128)(2,1)S(1)}, u32[]{:S(2)}, u32[]{:S(2)}) collective-permute-start(bf16[256,1024]{1,0:T(8,128)(2,1)S(1)} %get-tuple-element.421), channel_id=1, source_target_pairs={{0,16},{16,0},{1,17},{17,1},{2,18},{18,2},{3,19},{19,3},{4,20},{20... | collective-permute-start | bytes 1572872 | tf_op jit(solution)/shard_map/ppermute | solution.py:28
  104.1 5.8 %collective-permute-start.15 = (f32[2,2,512]{2,1,0:T(2,128)S(1)}, f32[2,2,512]{2,1,0:T(2,128)S(1)}, u32[]{:S(2)}, u32[]{:S(2)}) collective-permute-start(f32[2,2,512]{2,1,0:T(2,128)S(1)} %reshape.241), channel_id=1, source_target_pairs={{0,1},{1,2},{2,3},{3,4},{4,5},{5,6},{6,7},{8,9},{9,10},{10,11},{11... | collective-permute-start | bytes 24584 | tf_op jit(solution)/shard_map/ppermute | solution.py:37
  121.7 246.4 %reduce-scatter.2.cloned.1.call-start = ((), (), s32[]{:S(2)}) async-start(), calls=%async_computation.3 | async-start | bytes 5308416 | tf_op jit(solution)/shard_map/reduce_scatter | solution.py:769
  133.2 25.3 %collective-permute-start.19 = (bf16[512,1024]{1,0:T(8,128)(2,1)S(1)}, bf16[512,1024]{1,0:T(8,128)(2,1)}, u32[]{:S(2)}, u32[]{:S(2)}) collective-permute-start(bf16[512,1024]{1,0:T(8,128)(2,1)S(1)} %multiply_convert_fusion.refs_0_), channel_id=1, source_target_pairs={{0,16},{16,0},{1,17},{17,1},{2,18},{18,2},{3,19},{19,3},{4,20},{20... | collective-permute-start | bytes 3145736 | tf_op jit(solution)/shard_map/ppermute | solution.py:28
  158.5 15.1 %collective-permute-start.21 = (bf16[256,1024]{1,0:T(8,128)(2,1)S(1)}, bf16[256,1024]{1,0:T(8,128)(2,1)S(1)}, u32[]{:S(2)}, u32[]{:S(2)}) collective-permute-start(bf16[256,1024]{1,0:T(8,128)(2,1)S(1)} %copy-done.28), channel_id=1, source_target_pairs={{0,16},{16,0},{1,17},{17,1},{2,18},{18,2},{3,19},{19,3},{4,20},{20... | collective-permute-start | bytes 1572872 | tf_op jit(solution)/shard_map/ppermute | solution.py:28
  159.3 14.5 %collective-permute-start.22 = (bf16[256,1024]{1,0:T(8,128)(2,1)S(1)}, bf16[256,1024]{1,0:T(8,128)(2,1)S(1)}, u32[]{:S(2)}, u32[]{:S(2)}) collective-permute-start(bf16[256,1024]{1,0:T(8,128)(2,1)S(1)} %collective-permute-done.16.refs_1_.refs_0_), channel_id=1, source_target_pairs={{0,8},{8,0},{1,9},{9,1},{2,10},{10,2},{3,11},{11,3},{4,12},{12,4},... | collective-permute-start | bytes 1572872 | tf_op jit(solution)/shard_map/ppermute | solution.py:28
  187.7 26.6 %collective-permute-start.24 = (bf16[1,4,144,1024]{3,2,1,0:T(8,128)(2,1)S(1)}, bf16[1,4,144,1024]{3,2,1,0:T(8,128)(2,1)S(1)}, u32[]{:S(2)}, u32[]{:S(2)}) collective-permute-start(bf16[1,4,144,1024]{3,2,1,0:T(8,128)(2,1)S(1)} %get-tuple-element.408), channel_id=1, source_target_pairs={{0,1},{1,0},{2,3},{3,2},{4,5},{5,4},{6,7},{7,6},{8,9},{9,8},{10,11... | collective-permute-start | bytes 3538952 | tf_op jit(solution)/shard_map/ppermute | solution.py:28
  203.6 8.2 %collective-permute-start.25 = (bf16[128,1024]{1,0:T(8,128)(2,1)S(1)}, bf16[128,1024]{1,0:T(8,128)(2,1)S(1)}, u32[]{:S(2)}, u32[]{:S(2)}) collective-permute-start(bf16[128,1024]{1,0:T(8,128)(2,1)S(1)} %get-tuple-element.266), channel_id=1, source_target_pairs={{0,8},{8,0},{1,9},{9,1},{2,10},{10,2},{3,11},{11,3},{4,12},{12,4},... | collective-permute-start | bytes 786440 | tf_op jit(solution)/shard_map/ppermute | solution.py:28
  203.6 8.2 %collective-permute-start.26 = (bf16[128,1024]{1,0:T(8,128)(2,1)S(1)}, bf16[128,1024]{1,0:T(8,128)(2,1)S(1)}, u32[]{:S(2)}, u32[]{:S(2)}) collective-permute-start(bf16[128,1024]{1,0:T(8,128)(2,1)S(1)} %get-tuple-element.267), channel_id=1, source_target_pairs={{0,8},{8,0},{1,9},{9,1},{2,10},{10,2},{3,11},{11,3},{4,12},{12,4},... | collective-permute-start | bytes 786440 | tf_op jit(solution)/shard_map/ppermute | solution.py:28
  204.1 7.7 %collective-permute-start.27 = (bf16[128,1024]{1,0:T(8,128)(2,1)S(1)}, bf16[128,1024]{1,0:T(8,128)(2,1)S(1)}, u32[]{:S(2)}, u32[]{:S(2)}) collective-permute-start(bf16[128,1024]{1,0:T(8,128)(2,1)S(1)} %get-tuple-element.268), channel_id=1, source_target_pairs={{0,8},{8,0},{1,9},{9,1},{2,10},{10,2},{3,11},{11,3},{4,12},{12,4},... | collective-permute-start | bytes 786440 | tf_op jit(solution)/shard_map/ppermute | solution.py:28
  204.2 7.6 %collective-permute-start.28 = (bf16[128,1024]{1,0:T(8,128)(2,1)S(1)}, bf16[128,1024]{1,0:T(8,128)(2,1)S(1)}, u32[]{:S(2)}, u32[]{:S(2)}) collective-permute-start(bf16[128,1024]{1,0:T(8,128)(2,1)S(1)} %get-tuple-element.269), channel_id=1, source_target_pairs={{0,8},{8,0},{1,9},{9,1},{2,10},{10,2},{3,11},{11,3},{4,12},{12,4},... | collective-permute-start | bytes 786440 | tf_op jit(solution)/shard_map/ppermute | solution.py:28
  215.6 38.7 %collective-permute-start.29 = (bf16[512,1024]{1,0:T(8,128)(2,1)}, bf16[512,1024]{1,0:T(8,128)(2,1)}, u32[]{:S(2)}, u32[]{:S(2)}) collective-permute-start(bf16[512,1024]{1,0:T(8,128)(2,1)} %add_convert_fusion.3), channel_id=1, source_target_pairs={{0,16},{16,0},{1,17},{17,1},{2,18},{18,2},{3,19},{19,3},{4,20},{20... | collective-permute-start | bytes 3145736 | tf_op jit(solution)/shard_map/ppermute | solution.py:28
  218.9 35.4 %collective-permute-start.30 = (bf16[1,144,1024]{2,1,0:T(8,128)(2,1)S(1)}, bf16[1,144,1024]{2,1,0:T(8,128)(2,1)S(1)}, u32[]{:S(2)}, u32[]{:S(2)}) collective-permute-start(bf16[1,144,1024]{2,1,0:T(8,128)(2,1)S(1)} %get-tuple-element.414), channel_id=1, source_target_pairs={{0,2},{2,4},{4,6},{6,0},{1,3},{3,5},{5,7},{7,1},{8,10},{10,12},{12... | collective-permute-start | bytes 884744 | tf_op jit(solution)/shard_map/ppermute | solution.py:28
  220.6 33.7 %collective-permute-start.31 = (bf16[1,144,1024]{2,1,0:T(8,128)(2,1)S(1)}, bf16[1,144,1024]{2,1,0:T(8,128)(2,1)}, u32[]{:S(2)}, u32[]{:S(2)}) collective-permute-start(bf16[1,144,1024]{2,1,0:T(8,128)(2,1)S(1)} %get-tuple-element.413), channel_id=1, source_target_pairs={{0,6},{2,0},{4,2},{6,4},{1,7},{3,1},{5,3},{7,5},{8,14},{10,8},{12,... | collective-permute-start | bytes 884744 | tf_op jit(solution)/shard_map/ppermute | solution.py:28
  222.9 31.4 %collective-permute-start.32 = (bf16[1,144,1024]{2,1,0:T(8,128)(2,1)S(1)}, bf16[1,144,1024]{2,1,0:T(8,128)(2,1)}, u32[]{:S(2)}, u32[]{:S(2)}) collective-permute-start(bf16[1,144,1024]{2,1,0:T(8,128)(2,1)S(1)} %get-tuple-element.412), channel_id=1, source_target_pairs={{0,4},{2,6},{4,0},{6,2},{1,5},{3,7},{5,1},{7,3},{8,12},{10,14},{12... | collective-permute-start | bytes 884744 | tf_op jit(solution)/shard_map/ppermute | solution.py:28
  268.4 26.1 %collective-permute-start.43 = (bf16[512,1024]{1,0:T(8,128)(2,1)}, bf16[512,1024]{1,0:T(8,128)(2,1)}, u32[]{:S(2)}, u32[]{:S(2)}) collective-permute-start(bf16[512,1024]{1,0:T(8,128)(2,1)} %add_convert_fusion.2), channel_id=1, source_target_pairs={{0,16},{16,0},{1,17},{17,1},{2,18},{18,2},{3,19},{19,3},{4,20},{20... | collective-permute-start | bytes 3145736 | tf_op jit(solution)/shard_map/ppermute | solution.py:28
  271.1 5.5 %collective-permute-start.42 = (f32[2,2,512]{2,1,0:T(2,128)S(1)}, f32[2,2,512]{2,1,0:T(2,128)S(1)}, u32[]{:S(2)}, u32[]{:S(2)}) collective-permute-start(f32[2,2,512]{2,1,0:T(2,128)S(1)} %reshape.252), channel_id=1, source_target_pairs={{1,0},{2,1},{3,2},{4,3},{5,4},{6,5},{7,6},{9,8},{10,9},{11,10},{12... | collective-permute-start | bytes 24584 | tf_op jit(solution)/shard_map/ppermute | solution.py:37
  294.5 22.2 %collective-permute-start.46 = (bf16[2,3,32,2048]{3,2,1,0:T(8,128)(2,1)}, bf16[2,3,32,2048]{3,2,1,0:T(8,128)(2,1)}, u32[]{:S(2)}, u32[]{:S(2)}) collective-permute-start(bf16[2,3,32,2048]{3,2,1,0:T(8,128)(2,1)} %get-tuple-element.341), channel_id=1, source_target_pairs={{0,16},{16,0},{1,17},{17,1},{2,18},{18,2},{3,19},{19,3},{4,20},{20... | collective-permute-start | bytes 2359304 | tf_op jit(solution)/shard_map/ppermute | solution.py:28
  295.9 19.3 %collective-permute-start.44 = (bf16[2,1,32,2048]{3,2,1,0:T(8,128)(2,1)S(1)}, bf16[2,1,32,2048]{3,2,1,0:T(8,128)(2,1)S(1)}, u32[]{:S(2)}, u32[]{:S(2)}) collective-permute-start(bf16[2,1,32,2048]{3,2,1,0:T(8,128)(2,1)S(1)} %get-tuple-element.339), channel_id=1, source_target_pairs={{0,1},{1,0},{2,3},{3,2},{4,5},{5,4},{6,7},{7,6},{8,9},{9,8},{10,11... | collective-permute-start | bytes 786440 | tf_op jit(solution)/shard_map/ppermute | solution.py:28
  298.7 18.0 %collective-permute-start.45 = (bf16[2,1,32,2048]{3,2,1,0:T(8,128)(2,1)S(1)}, bf16[2,1,32,2048]{3,2,1,0:T(8,128)(2,1)S(1)}, u32[]{:S(2)}, u32[]{:S(2)}) collective-permute-start(bf16[2,1,32,2048]{3,2,1,0:T(8,128)(2,1)S(1)} %get-tuple-element.340), channel_id=1, source_target_pairs={{0,1},{1,0},{2,3},{3,2},{4,5},{5,4},{6,7},{7,6},{8,9},{9,8},{10,11... | collective-permute-start | bytes 786440 | tf_op jit(solution)/shard_map/ppermute | solution.py:28
  316.7 11.1 %collective-permute-start.47 = (bf16[2,1,32,2048]{3,2,1,0:T(8,128)(2,1)S(1)}, bf16[2,1,32,2048]{3,2,1,0:T(8,128)(2,1)S(1)}, u32[]{:S(2)}, u32[]{:S(2)}) collective-permute-start(bf16[2,1,32,2048]{3,2,1,0:T(8,128)(2,1)S(1)} %add_convert_fusion.7), channel_id=1, source_target_pairs={{0,16},{16,0},{1,17},{17,1},{2,18},{18,2},{3,19},{19,3},{4,20},{20... | collective-permute-start | bytes 786440 | tf_op jit(solution)/shard_map/ppermute | solution.py:28
  318.5 10.1 %collective-permute-start.50 = (bf16[128,1024]{1,0:T(8,128)(2,1)S(1)}, bf16[128,1024]{1,0:T(8,128)(2,1)S(1)}, u32[]{:S(2)}, u32[]{:S(2)}) collective-permute-start(bf16[128,1024]{1,0:T(8,128)(2,1)S(1)} %get-tuple-element.369), channel_id=1, source_target_pairs={{0,8},{8,0},{1,9},{9,1},{2,10},{10,2},{3,11},{11,3},{4,12},{12,4},... | collective-permute-start | bytes 786440 | tf_op jit(solution)/shard_map/ppermute | solution.py:28
  318.7 9.9 %collective-permute-start.51 = (bf16[128,1024]{1,0:T(8,128)(2,1)S(1)}, bf16[128,1024]{1,0:T(8,128)(2,1)S(1)}, u32[]{:S(2)}, u32[]{:S(2)}) collective-permute-start(bf16[128,1024]{1,0:T(8,128)(2,1)S(1)} %get-tuple-element.370), channel_id=1, source_target_pairs={{0,8},{8,0},{1,9},{9,1},{2,10},{10,2},{3,11},{11,3},{4,12},{12,4},... | collective-permute-start | bytes 786440 | tf_op jit(solution)/shard_map/ppermute | solution.py:28
  319.0 7.2 %collective-permute-start.55 = (f32[5,1024]{1,0:T(8,128)S(1)}, f32[5,1024]{1,0:T(8,128)S(1)}, u32[]{:S(2)}, u32[]{:S(2)}) collective-permute-start(f32[5,1024]{1,0:T(8,128)S(1)} %add.231), channel_id=1, source_target_pairs={{0,16},{16,0},{1,17},{17,1},{2,18},{18,2},{3,19},{19,3},{4,20},{20... | collective-permute-start | bytes 61448 | tf_op jit(solution)/shard_map/ppermute | solution.py:28
  321.8 24.8 %collective-permute-start.48 = (bf16[2,3,32,2048]{3,2,1,0:T(8,128)(2,1)}, bf16[2,3,32,2048]{3,2,1,0:T(8,128)(2,1)}, u32[]{:S(2)}, u32[]{:S(2)}) collective-permute-start(bf16[2,3,32,2048]{3,2,1,0:T(8,128)(2,1)} %add_convert_fusion.5), channel_id=1, source_target_pairs={{0,1},{1,0},{2,3},{3,2},{4,5},{5,4},{6,7},{7,6},{8,9},{9,8},{10,11... | collective-permute-start | bytes 2359304 | tf_op jit(solution)/shard_map/ppermute | solution.py:28
  326.2 20.4 %collective-permute-start.49 = (bf16[2,3,32,2048]{3,2,1,0:T(8,128)(2,1)}, bf16[2,3,32,2048]{3,2,1,0:T(8,128)(2,1)}, u32[]{:S(2)}, u32[]{:S(2)}) collective-permute-start(bf16[2,3,32,2048]{3,2,1,0:T(8,128)(2,1)} %get-tuple-element.365), channel_id=1, source_target_pairs={{0,16},{16,0},{1,17},{17,1},{2,18},{18,2},{3,19},{19,3},{4,20},{20... | collective-permute-start | bytes 2359304 | tf_op jit(solution)/shard_map/ppermute | solution.py:28
  331.4 5.8 %collective-permute-start.57 = (bf16[128,1024]{1,0:T(8,128)(2,1)S(1)}, bf16[128,1024]{1,0:T(8,128)(2,1)S(1)}, u32[]{:S(2)}, u32[]{:S(2)}) collective-permute-start(bf16[128,1024]{1,0:T(8,128)(2,1)S(1)} %get-tuple-element.377), channel_id=1, source_target_pairs={{0,8},{8,0},{1,9},{9,1},{2,10},{10,2},{3,11},{11,3},{4,12},{12,4},... | collective-permute-start | bytes 786440 | tf_op jit(solution)/shard_map/ppermute | solution.py:28
  331.5 5.7 %collective-permute-start.58 = (bf16[128,1024]{1,0:T(8,128)(2,1)S(1)}, bf16[128,1024]{1,0:T(8,128)(2,1)S(1)}, u32[]{:S(2)}, u32[]{:S(2)}) collective-permute-start(bf16[128,1024]{1,0:T(8,128)(2,1)S(1)} %get-tuple-element.378), channel_id=1, source_target_pairs={{0,8},{8,0},{1,9},{9,1},{2,10},{10,2},{3,11},{11,3},{4,12},{12,4},... | collective-permute-start | bytes 786440 | tf_op jit(solution)/shard_map/ppermute | solution.py:28
  332.0 5.2 %collective-permute-start.59 = (bf16[128,1024]{1,0:T(8,128)(2,1)S(1)}, bf16[128,1024]{1,0:T(8,128)(2,1)S(1)}, u32[]{:S(2)}, u32[]{:S(2)}) collective-permute-start(bf16[128,1024]{1,0:T(8,128)(2,1)S(1)} %get-tuple-element.379), channel_id=1, source_target_pairs={{0,8},{8,0},{1,9},{9,1},{2,10},{10,2},{3,11},{11,3},{4,12},{12,4},... | collective-permute-start | bytes 786440 | tf_op jit(solution)/shard_map/ppermute | solution.py:28
  349.5 28.8 %collective-permute-start.60 = (bf16[2,32,2176]{2,1,0:T(8,128)(2,1)}, bf16[2,32,2176]{2,1,0:T(8,128)(2,1)S(1)}, u32[]{:S(2)}, u32[]{:S(2)}) collective-permute-start(bf16[2,32,2176]{2,1,0:T(8,128)(2,1)} %get-tuple-element.419), channel_id=1, source_target_pairs={{0,2},{2,4},{4,6},{6,0},{1,3},{3,5},{5,7},{7,1},{8,10},{10,12},{12... | collective-permute-start | bytes 835592 | tf_op jit(solution)/shard_map/ppermute | solution.py:28
  349.5 28.8 %collective-permute-start.61 = (bf16[2,32,2176]{2,1,0:T(8,128)(2,1)S(1)}, bf16[2,32,2176]{2,1,0:T(8,128)(2,1)}, u32[]{:S(2)}, u32[]{:S(2)}) collective-permute-start(bf16[2,32,2176]{2,1,0:T(8,128)(2,1)S(1)} %get-tuple-element.418), channel_id=1, source_target_pairs={{0,6},{2,0},{4,2},{6,4},{1,7},{3,1},{5,3},{7,5},{8,14},{10,8},{12,... | collective-permute-start | bytes 835592 | tf_op jit(solution)/shard_map/ppermute | solution.py:28
  353.5 28.4 %collective-permute-start.62 = (bf16[2,32,2176]{2,1,0:T(8,128)(2,1)S(1)}, bf16[2,32,2176]{2,1,0:T(8,128)(2,1)}, u32[]{:S(2)}, u32[]{:S(2)}) collective-permute-start(bf16[2,32,2176]{2,1,0:T(8,128)(2,1)S(1)} %get-tuple-element.417), channel_id=1, source_target_pairs={{0,4},{2,6},{4,0},{6,2},{1,5},{3,7},{5,1},{7,3},{8,12},{10,14},{12... | collective-permute-start | bytes 835592 | tf_op jit(solution)/shard_map/ppermute | solution.py:28
  369.3 6.8 %collective-permute-start.64 = (bf16[2,32,1152]{2,1,0:T(8,128)(2,1)S(1)}, bf16[2,32,1152]{2,1,0:T(8,128)(2,1)S(1)}, u32[]{:S(2)}, u32[]{:S(2)}) collective-permute-start(bf16[2,32,1152]{2,1,0:T(8,128)(2,1)S(1)} %get-tuple-element.439), channel_id=1, source_target_pairs={{0,16},{16,0},{1,17},{17,1},{2,18},{18,2},{3,19},{19,3},{4,20},{20... | collective-permute-start | bytes 442376 | tf_op jit(solution)/shard_map/ppermute | solution.py:28
  370.9 7.4 %collective-permute-start.63 = (bf16[2,32,1152]{2,1,0:T(8,128)(2,1)S(1)}, bf16[2,32,1152]{2,1,0:T(8,128)(2,1)S(1)}, u32[]{:S(2)}, u32[]{:S(2)}) collective-permute-start(bf16[2,32,1152]{2,1,0:T(8,128)(2,1)S(1)} %get-tuple-element.438), channel_id=1, source_target_pairs={{0,16},{16,0},{1,17},{17,1},{2,18},{18,2},{3,19},{19,3},{4,20},{20... | collective-permute-start | bytes 442376 | tf_op jit(solution)/shard_map/ppermute | solution.py:28
  (62 other events, 515.8 us)
Sparse Core Ops, SparseCore 0:
  51.0 81.2 all-gather.2
  135.1 50.6 all-gather.4
  254.5 113.6 reduce-scatter.1
